TPU v7x, 512 devices: a whole 4x4x16 slice. The times are simulated.
512 devices in a mesh: row: 32 (over z, x_lo), col: 16 (over y, x_hi, core).
Axes of the slice: x: 4 (x_hi: 2, x_lo: 2; x = x_hi * 2 + x_lo), y: 4, z: 16, core: 2. Of those that a mesh axis runs over, the one named last changes fastest.
Arguments:
- samples: bfloat16 [32, 262144], P('row', 'col'), may hold values from -6 to 6
- blocks: bfloat16 [32, 16, 32, 128, 128], P('row', 'col'), may hold values from -0.29882812 to 0.29882812
- diagonal: float32 [262144], P('col'), may hold values from 0.5 to 2
- block_rows: int32 [32, 16, 32], P('row', 'col'), may hold values from 0 to 63, as said below
- block_cols: int32 [32, 16, 32], P('row', 'col'), may hold values from 0 to 127, as said below
Outputs:
- new_blocks: bfloat16 [32, 16, 32, 128, 128], P('row', 'col')
- new_diagonal: float32 [262144], P('col')
Inputs may be any that keep to these rules, and one draw needn't show every extreme that they name: Within a grid cell the 32 pairs (block_rows, block_cols) are distinct. `block_cols`: pairs with block_rows, as stated there.
All inputs are finite; a program needn't handle non-finite values.
Results may differ from a plain program's by a relative error of at most 0.018.
Values may be sent and summed in bfloat16 or wider, within the bound.
No kernel may reach another device: no remote copies, remote signals or barrier semaphores. Data moves between devices by JAX's collectives and lax.ppermute only.
A program may use at most 64 MiB of HBM per device.

v0:
```python
import jax
import jax.numpy as jnp
from jax import lax
from jax.sharding import PartitionSpec as P

TAU = 0.5
PENALTY = 0.1


def from_root(x, axis, root):
    mine = lax.axis_index(axis) == root
    return lax.psum(jnp.where(mine, x, jnp.zeros_like(x)), axis)


def on_device(samples, blocks, diagonal, block_rows, block_cols):
    width = samples.shape[1]
    bsize = blocks.shape[-1]
    cbcount = width // bsize
    ratio = lax.axis_size("row") // lax.axis_size("col")
    rbcount = cbcount // ratio
    rindex = lax.axis_index("row")
    offset = rindex % ratio * (rbcount * bsize)
    root = rindex // ratio
    panel = lax.all_gather(samples, "row", axis=0, tiled=True)
    count = panel.shape[0]
    sub = lax.dynamic_slice_in_dim(panel, offset, rbcount * bsize, 1)
    sub_panel = from_root(sub, "col", root)
    rows = block_rows[0, 0]
    cols = block_cols[0, 0]
    local = blocks[0, 0]
    xr = sub_panel.reshape(count, rbcount, bsize)[:, rows]
    prod = jnp.einsum("nki,kij->knj", xr, local, preferred_element_type=jnp.float32)
    summed = jax.ops.segment_sum(prod, cols, num_segments=cbcount)
    partial_sum = jnp.transpose(summed, (1, 0, 2)).reshape(count, width).astype(jnp.bfloat16)
    totals = lax.psum(partial_sum, "row").astype(jnp.float32)
    mixed = (totals + panel.astype(jnp.float32) * diagonal[None, :]).astype(jnp.bfloat16)
    quad = jnp.einsum("np,np->p", panel, mixed, preferred_element_type=jnp.float32)
    diag_grad = -1.0 / diagonal + quad / count
    new_diagonal = diagonal - TAU * diag_grad
    mixed_sub = lax.dynamic_slice_in_dim(mixed, offset, rbcount * bsize, 1)
    mixed_rowpanel = from_root(mixed_sub, "col", root)
    wc = mixed.reshape(count, cbcount, bsize)[:, cols]
    xc = panel.reshape(count, cbcount, bsize)[:, cols]
    wr = mixed_rowpanel.reshape(count, rbcount, bsize)[:, rows]
    direct = jnp.einsum("nki,nkj->kij", xr, wc, preferred_element_type=jnp.float32) / count
    partner = jnp.einsum("nki,nkj->kij", xc, wr, preferred_element_type=jnp.float32) / count
    grad = 0.5 * (direct + jnp.swapaxes(partner, -1, -2))
    moved = local.astype(jnp.float32) - TAU * grad
    shrunk = jnp.sign(moved) * jnp.maximum(jnp.abs(moved) - TAU * PENALTY, 0.0)
    new_blocks = shrunk.astype(jnp.bfloat16)[None, None]
    return (new_blocks, new_diagonal)


def solution(mesh):
    in_specs = (
        P("row", "col"),
        P("row", "col", None, None, None),
        P("col"),
        P("row", "col", None),
        P("row", "col", None),
    )
    out_specs = (P("row", "col", None, None, None), P("col"))
    return jax.shard_map(
        on_device, mesh=mesh, in_specs=in_specs, out_specs=out_specs, check_vma=False
    )
```

profile of v0, /device:TPU:1, one launch (start us, length us, event | category | flops | bytes accessed | tf_op | source)
XLA Modules:
  0.0 753.7 jit_solution(15687602103857089952)
XLA Ops:
  7.2 0.0 copy-start.5
  7.2 0.0 copy-start.1
  7.2 0.0 all-gather.3.cloned.1.call-start
  7.2 0.7 all-gather.3.cloned.1.call-update
  7.9 0.0 all-reduce.4.cloned.1.call-start
  8.0 120.3 %all-gather.3.cloned.1.call-done = bf16[32,1,16384]{2,1,0:T(2,128)(2,1)} async-done(((bf16[1,1,16384]{2,1,0:T(2,128)(2,1)}), bf16[32,1,16384]{2,1,0:T(2,128)(2,1)}) %all-gather.3.cloned.1.call-update) | async-done | bytes 1048592 | tf_op jit(solution)/shard_map/all_gather | solution.py:24
  128.3 4.3 fusion.2
  132.7 0.9 copy_bitcast_fusion.4
  133.5 0.0 all-reduce.4.cloned.1.call-update
  133.6 0.0 all-reduce.6.cloned.1.call-start
  133.6 0.0 copy-done.5
  133.7 173.3 %all-reduce.4.cloned.1.call-done = bf16[32,64,128]{2,0,1:T(8,128)(2,1)} async-done(((bf16[32,64,128]{2,0,1:T(8,128)(2,1)}), bf16[32,64,128]{2,0,1:T(8,128)(2,1)}) %all-reduce.4.cloned.1.call-update) | async-done | bytes 524304 | tf_op jit(solution)/shard_map/psum | solution.py:12
  307.0 1.6 gather_fusion
  308.6 0.0 copy-done.1
  308.6 0.0 copy-start.4
  308.6 0.4 fusion.3
  309.0 1.6 broadcast_in_dim.4
  310.6 0.0 copy-done.4
  310.6 4.3 scatter_fusion
  314.9 0.0 copy-start
  314.9 2.8 copy_bitcast_fusion
  317.7 0.0 all-reduce.6.cloned.1.call-update
  317.7 0.2 all-reduce.8.cloned.1.call-start
  318.0 0.0 copy-done
  318.0 6.4 reduce.2
  324.4 0.0 copy-start.2
  324.4 1.2 copy_bitcast_fusion.1
  325.6 2.5 gather_fusion.3
  328.1 235.6 %all-reduce.6.cloned.1.call-done = bf16[32,16384]{1,0:T(8,128)(2,1)} async-done(((bf16[32,16384]{1,0:T(8,128)(2,1)}), bf16[32,16384]{1,0:T(8,128)(2,1)}) %all-reduce.6.cloned.1.call-update) | async-done | bytes 1048592 | tf_op jit(solution)/shard_map/psum | solution.py:35
  563.7 0.0 copy-done.2
  563.8 2.9 fusion
  566.7 0.2 copy_bitcast_fusion.2
  566.9 0.9 copy_bitcast_fusion.3
  567.8 0.0 copy-start.3
  567.8 0.6 gather_fusion.1
  568.4 0.0 all-reduce.8.cloned.1.call-update
  568.4 0.5 fusion.7
  568.9 0.6 multiply_subtract_fusion
  569.5 172.4 %all-reduce.8.cloned.1.call-done = bf16[32,64,128]{2,0,1:T(8,128)(2,1)} async-done(((bf16[32,64,128]{2,0,1:T(8,128)(2,1)}), bf16[32,64,128]{2,0,1:T(8,128)(2,1)}) %all-reduce.8.cloned.1.call-update) | async-done | bytes 524304 | tf_op jit(solution)/shard_map/psum | solution.py:12
  741.9 1.6 gather_fusion.2
  743.6 0.0 copy-done.3
  743.6 3.5 fusion.1
  (4 shorter events, 0.0 us)
Async XLA Ops:
  7.2 126.5 %copy-start.5 = (s32[1,1,32]{2,1,0:T(1,128)S(1)}, s32[1,1,32]{2,1,0:T(1,128)}, u32[]{:S(2)}) copy-start(s32[1,1,32]{2,1,0:T(1,128)} %param.8) | copy-start | bytes 388
  7.2 301.4 %copy-start.1 = (bf16[1,1,32,128,128]{4,3,2,1,0:T(8,128)(2,1)S(1)}, bf16[1,1,32,128,128]{4,3,2,1,0:T(8,128)(2,1)}, u32[]{:S(2)}) copy-start(bf16[1,1,32,128,128]{4,3,2,1,0:T(8,128)(2,1)} %param.6) | copy-start | bytes 3145732
  7.2 121.1 %all-gather.3.cloned.1.call-start = ((), (), s32[]{:S(2)}) async-start(), calls=%async_computation.3 | async-start | bytes 2162688 | tf_op jit(solution)/shard_map/all_gather | solution.py:24
  7.9 299.1 %all-reduce.4.cloned.1.call-start = ((), (), s32[]{:S(2)}) async-start(), calls=%async_computation | async-start | bytes 1048576 | tf_op jit(solution)/shard_map/psum | solution.py:12
  133.6 430.2 %all-reduce.6.cloned.1.call-start = ((), (), s32[]{:S(2)}) async-start(), calls=%async_computation.1 | async-start | bytes 2097152 | tf_op jit(solution)/shard_map/psum | solution.py:35
  308.6 2.0 copy-start.4
  314.9 3.1 copy-start
  317.7 424.2 %all-reduce.8.cloned.1.call-start = ((), (), s32[]{:S(2)}) async-start(), calls=%async_computation.2 | async-start | bytes 1048576 | tf_op jit(solution)/shard_map/psum | solution.py:12
  324.4 239.3 %copy-start.2 = (f32[16384]{0:T(1024)S(1)}, f32[16384]{0:T(1024)}, u32[]{:S(2)}) copy-start(f32[16384]{0:T(1024)} %param.7) | copy-start | bytes 196612
  567.8 175.8 %copy-start.3 = (bf16[32,32,128]{2,1,0:T(8,128)(2,1)S(1)}, bf16[32,32,128]{2,1,0:T(8,128)(2,1)}, u32[]{:S(2)}) copy-start(bf16[32,32,128]{2,1,0:T(8,128)(2,1)} %gather_fusion.3) | copy-start | bytes 786436
Sparse Core Ops, SparseCore 0:
  10.1 118.1 all-gather.2
  133.7 173.2 all-reduce.3
  317.8 245.8 all-reduce.5
  568.5 173.3 all-reduce.7
where the time goes:
time: 754 us
  waiting for transfers between devices  702 us (93%)
  other arithmetic  22.3 us (3%)
  between operations  13.9 us (2%)
  local copies, waits for them, and re-layouts  10.2 us (1%)
    psum x2, waiting for transfers between devices, from_root(): return lax.psum(jnp.where(mine, x, jnp.zeros_like(x)), axis)  346 us
    psum x1, waiting for transfers between devices, on_device(): totals = lax.psum(partial_sum, 'row').astype(jnp.float32)  236 us
    all_gather x1, waiting for transfers between devices, on_device(): panel = lax.all_gather(samples, 'row', axis=0, tiled=True)  120 us
  transfers between devices with their start and end apart: 4, of which 4 were waited for; matrix products, arithmetic and copies ran while one was open for 1% of the time, Pallas kernels for 0%

commit v1 on v0

v1 whole, which is shorter than its diff:
```python
import jax
import jax.numpy as jnp
from jax import lax
from jax.sharding import PartitionSpec as P

TAU = 0.5
PENALTY = 0.1
BF = jnp.bfloat16


def exchange(x, axis):
    return lax.all_to_all(x, axis, 0, 0, tiled=True)


def spread(x, axis):
    return exchange(jnp.broadcast_to(x[None], (lax.axis_size(axis),) + x.shape), axis)


def pick(index, size):
    return (index.reshape(-1, 1) == jnp.arange(size, dtype=index.dtype)[None, :]).astype(BF)


def turned(x, nrow, ncol):
    ratio = nrow // ncol
    rindex = lax.axis_index("row")
    mine = rindex % ratio
    parts = x.reshape((ratio, -1) + x.shape[1:])
    got = []
    for shift in range(ratio):
        target = (mine + shift) % ratio
        part = lax.dynamic_index_in_dim(parts, target, 0, keepdims=False)
        perm = []
        for r in range(nrow):
            for c in range(ncol):
                to = c * ratio + (r + shift) % ratio
                perm.append((r * ncol + c, to * ncol + r // ratio))
        got.append(lax.ppermute(part, ("row", "col"), perm))
    out = []
    for e in range(ratio):
        value = got[0]
        for shift in range(1, ratio):
            value = jnp.where((mine - shift) % ratio == e, got[shift], value)
        out.append(value)
    return jnp.concatenate(out, axis=1)


def on_device(samples, blocks, diagonal, block_rows, block_cols):
    nrow, ncol = lax.axis_size("row"), lax.axis_size("col")
    ratio = nrow // ncol
    width = samples.shape[1]
    b = blocks.shape[-1]
    cb = width // b
    rb = cb // ratio
    rows, cols, local = block_rows[0, 0], block_cols[0, 0], blocks[0, 0]
    k = rows.shape[0]
    x = samples.reshape(cb, b)
    diag = diagonal.reshape(cb, b)

    pick_r = pick(spread(rows[None], "col"), rb)
    pick_c = pick(spread(cols[None], "row"), cb)

    def to_rows(v):
        t = turned(v, nrow, ncol)
        out = jnp.dot(pick_r, t, preferred_element_type=jnp.float32).astype(BF)
        got = exchange(out.reshape(ncol, k, ratio * b), "col")
        return got.reshape(ncol, k, ratio, b).transpose(0, 2, 1, 3).reshape(nrow, k, b)

    def to_cols(v):
        out = jnp.dot(pick_c, v, preferred_element_type=jnp.float32).astype(BF)
        return exchange(out.reshape(nrow, k, b), "row")

    xr = to_rows(x)
    xc = to_cols(x)
    prod = jnp.einsum("nki,kij->nkj", xr, local, preferred_element_type=jnp.float32)
    terms = exchange(prod.astype(BF), "row").reshape(nrow * k, b)
    total = lax.dot_general(pick_c, terms, (((0,), (0,)), ((), ())), preferred_element_type=jnp.float32)
    xf = x.astype(jnp.float32)
    mixed = (total + xf * diag).astype(BF)

    quads = exchange((xf * mixed.astype(jnp.float32)).reshape(nrow, cb // nrow, b), "row")
    quad = jnp.sum(quads, axis=0)
    mine = lax.dynamic_index_in_dim(diag.reshape(nrow, cb // nrow, b), lax.axis_index("row"), 0, keepdims=False)
    diag_grad = -1.0 / mine + quad / nrow
    new_diagonal = spread(mine - TAU * diag_grad, "row").reshape(width)

    wr = to_rows(mixed)
    wc = to_cols(mixed)
    left = jnp.concatenate([xr, wr], axis=0)
    right = jnp.concatenate([wc, xc], axis=0)
    both = jnp.einsum("nki,nkj->kij", left, right, preferred_element_type=jnp.float32)
    grad = both * (0.5 / nrow)
    moved = local.astype(jnp.float32) - TAU * grad
    shrunk = jnp.sign(moved) * jnp.maximum(jnp.abs(moved) - TAU * PENALTY, 0.0)
    return shrunk.astype(BF)[None, None], new_diagonal


def solution(mesh):
    in_specs = (
        P("row", "col"),
        P("row", "col", None, None, None),
        P("col"),
        P("row", "col", None),
        P("row", "col", None),
    )
    out_specs = (P("row", "col", None, None, None), P("col"))
    return jax.shard_map(
        on_device, mesh=mesh, in_specs=in_specs, out_specs=out_specs, check_vma=False
    )
```

time: 754 us -> 209 us (0.28)
  the two profiles are of different devices: /device:TPU:1 before, /device:TPU:2 now
where the time goes in v1:
time: 209 us; the launch traced here: 208 us
  waiting for transfers between devices  106 us (51%)
  starting transfers between devices  71.6 us (34%)
  blocking collectives  14.2 us (7%)
  matrix products  7.07 us (3%)
  local copies, waits for them, and re-layouts  5.25 us (3%)
  other arithmetic  2.57 us (1%)
    all_to_all x8, waiting for transfers between devices, exchange(): return lax.all_to_all(x, axis, 0, 0, tiled=True)  106 us
    all_to_all x8, starting transfers between devices, exchange(): return lax.all_to_all(x, axis, 0, 0, tiled=True)  60.1 us
    all_to_all x1, blocking collectives, exchange(): return lax.all_to_all(x, axis, 0, 0, tiled=True)  14.2 us
    ppermute x4, starting transfers between devices, turned(): got.append(lax.ppermute(part, ('row', 'col'), perm))  11.5 us
  transfers between devices with their start and end apart: 12, of which 8 were waited for; matrix products, arithmetic and copies ran while one was open for 4% of the time, Pallas kernels for 0%

profile of v1, /device:TPU:2, one launch (start us, length us, event | category | flops | bytes accessed | tf_op | source)
XLA Modules:
  0.0 208.0 jit_solution(11002599327373650037)
XLA Ops:
  0.6 0.0 copy-start.2
  0.7 1.0 reduce.1
  1.7 0.0 copy-start
  1.7 0.8 collective-permute-start.1
  2.5 7.8 %collective-permute-start = (bf16[64,128]{1,0:T(8,128)(2,1)S(1)}, bf16[64,128]{1,0:T(8,128)(2,1)S(1)}, u32[]{:S(2)}, u32[]{:S(2)}) collective-permute-start(bf16[64,128]{1,0:T(8,128)(2,1)S(1)} %get-tuple-element.13), channel_id=1, source_target_pairs={{0,16},{1,48},{2,80},{3,112},{4,144},{5,176},{6,208},{7,240},{8,27... | collective-permute-start | bytes 49160 | tf_op jit(solution)/shard_map/ppermute | solution.py:37
  10.4 1.3 broadcast_in_dim.28
  11.6 15.2 %all-to-all-start = ((s32[16,1,32]{2,1,0:T(1,128)}), s32[16,1,32]{2,1,0:T(1,128)S(1)}, u32[]{:S(2)}, u32[]{:S(2)}) async-start(s32[16,1,32]{2,1,0:T(1,128)} %broadcast_in_dim.28), calls=%async_computation | async-start | bytes 16384 | tf_op jit(solution)/shard_map/all_to_all | solution.py:12
  26.8 7.5 %all-to-all-done = s32[16,1,32]{2,1,0:T(1,128)S(1)} async-done(((s32[16,1,32]{2,1,0:T(1,128)}), s32[16,1,32]{2,1,0:T(1,128)S(1)}, u32[]{:S(2)}, u32[]{:S(2)}) %all-to-all-start) | async-done | bytes 2080 | tf_op jit(solution)/shard_map/all_to_all | solution.py:12
  34.3 0.6 broadcast.32
  34.9 0.7 reduce.8
  35.6 0.1 eq.49
  35.7 0.0 collective-permute-done.1
  35.7 0.0 collective-permute-done
  35.7 0.3 convolution_convert_fusion.1
  36.0 14.2 %all_to_all.45 = bf16[16,32,256]{2,1,0:T(8,128)(2,1)S(1)} all-to-all(bf16[16,32,256]{2,1,0:T(8,128)(2,1)S(1)} %bitcast.48), channel_id=1, replica_groups=mesh['row'=32,'col'=16] {'col'}, dimensions={0} | all-to-all | bytes 524288 | tf_op jit(solution)/shard_map/all_to_all | solution.py:12
  50.2 0.0 copy-done.2
  50.2 0.6 broadcast_in_dim.30
  50.8 12.2 %all-to-all-start.2 = ((s32[32,1,32]{2,1,0:T(1,128)}), s32[32,1,32]{2,1,0:T(1,128)S(1)}, u32[]{:S(2)}, u32[]{:S(2)}) async-start(s32[32,1,32]{2,1,0:T(1,128)} %broadcast_in_dim.30), calls=%async_computation.2 | async-start | bytes 32768 | tf_op jit(solution)/shard_map/all_to_all | solution.py:12
  63.1 0.0 copy-done
  63.1 0.4 fusion.1
  63.5 0.0 copy-start.1
  63.5 0.8 copy.16
  64.3 10.8 %all-to-all-done.2 = s32[32,1,32]{2,1,0:T(1,128)S(1)} async-done(((s32[32,1,32]{2,1,0:T(1,128)}), s32[32,1,32]{2,1,0:T(1,128)S(1)}, u32[]{:S(2)}, u32[]{:S(2)}) %all-to-all-start.2) | async-done | bytes 4128 | tf_op jit(solution)/shard_map/all_to_all | solution.py:12
  75.1 4.8 %all-to-all-start.3 = ((bf16[32,32,128]{2,1,0:T(8,128)(2,1)}), bf16[32,32,128]{2,1,0:T(8,128)(2,1)S(1)}, u32[]{:S(2)}, u32[]{:S(2)}) async-start(bf16[32,32,128]{2,1,0:T(8,128)(2,1)} %copy.16), calls=%async_computation.3 | async-start | bytes 524288 | tf_op jit(solution)/shard_map/all_to_all | solution.py:12
  79.9 0.7 reduce.9
  80.7 0.1 eq.55
  80.7 1.0 convolution_convert_fusion.2
  81.8 18.4 %all-to-all-done.3 = bf16[32,32,128]{2,1,0:T(8,128)(2,1)S(1)} async-done(((bf16[32,32,128]{2,1,0:T(8,128)(2,1)}), bf16[32,32,128]{2,1,0:T(8,128)(2,1)S(1)}, u32[]{:S(2)}, u32[]{:S(2)}) %all-to-all-start.3) | async-done | bytes 262176 | tf_op jit(solution)/shard_map/all_to_all | solution.py:12
  100.2 4.1 %all-to-all-start.6 = ((bf16[32,32,128]{2,1,0:T(8,128)(2,1)}), bf16[32,32,128]{2,1,0:T(8,128)(2,1)S(1)}, u32[]{:S(2)}, u32[]{:S(2)}) async-start(bf16[32,32,128]{2,1,0:T(8,128)(2,1)} %bitcast.16), calls=%async_computation.6 | async-start | bytes 524288 | tf_op jit(solution)/shard_map/all_to_all | solution.py:12
  104.3 0.0 copy-done.1
  104.3 1.1 convert_multiply_fusion
  105.4 0.7 collective-permute-start.3
  106.1 2.3 %collective-permute-start.2 = (bf16[64,128]{1,0:T(8,128)(2,1)S(1)}, bf16[64,128]{1,0:T(8,128)(2,1)S(1)}, u32[]{:S(2)}, u32[]{:S(2)}) collective-permute-start(bf16[64,128]{1,0:T(8,128)(2,1)S(1)} %get-tuple-element.9), channel_id=1, source_target_pairs={{0,16},{1,48},{2,80},{3,112},{4,144},{5,176},{6,208},{7,240},{8,27... | collective-permute-start | bytes 49160 | tf_op jit(solution)/shard_map/ppermute | solution.py:37
  108.3 15.7 %all-to-all-done.6 = bf16[32,32,128]{2,1,0:T(8,128)(2,1)S(1)} async-done(((bf16[32,32,128]{2,1,0:T(8,128)(2,1)}), bf16[32,32,128]{2,1,0:T(8,128)(2,1)S(1)}, u32[]{:S(2)}, u32[]{:S(2)}) %all-to-all-start.6) | async-done | bytes 262176 | tf_op jit(solution)/shard_map/all_to_all | solution.py:12
  124.1 11.5 %all-to-all-start.7 = ((f32[32,4,128]{2,1,0:T(4,128)}), f32[32,4,128]{2,1,0:T(4,128)S(1)}, u32[]{:S(2)}, u32[]{:S(2)}) async-start(f32[32,4,128]{2,1,0:T(4,128)} %bitcast.19), calls=%async_computation.7 | async-start | bytes 131072 | tf_op jit(solution)/shard_map/all_to_all | solution.py:12
  135.6 0.0 collective-permute-done.3
  135.6 0.0 collective-permute-done.2
  135.6 1.0 convolution_convert_fusion
  136.6 12.2 %all-to-all-done.7 = f32[32,4,128]{2,1,0:T(4,128)S(1)} async-done(((f32[32,4,128]{2,1,0:T(4,128)}), f32[32,4,128]{2,1,0:T(4,128)S(1)}, u32[]{:S(2)}, u32[]{:S(2)}) %all-to-all-start.7) | async-done | bytes 65568 | tf_op jit(solution)/shard_map/all_to_all | solution.py:12
  148.8 3.5 %all-to-all-start.4 = ((bf16[16,32,256]{2,1,0:T(8,128)(2,1)}), bf16[16,32,256]{2,1,0:T(8,128)(2,1)S(1)}, u32[]{:S(2)}, u32[]{:S(2)}) async-start(bf16[16,32,256]{2,1,0:T(8,128)(2,1)} %bitcast.13), calls=%async_computation.4 | async-start | bytes 524288 | tf_op jit(solution)/shard_map/all_to_all | solution.py:12
  152.4 9.5 %all-to-all-done.4 = bf16[16,32,256]{2,1,0:T(8,128)(2,1)S(1)} async-done(((bf16[16,32,256]{2,1,0:T(8,128)(2,1)}), bf16[16,32,256]{2,1,0:T(8,128)(2,1)S(1)}, u32[]{:S(2)}, u32[]{:S(2)}) %all-to-all-start.4) | async-done | bytes 262176 | tf_op jit(solution)/shard_map/all_to_all | solution.py:12
  161.8 0.6 broadcast_in_dim.33
  162.5 4.3 %all-to-all-start.8 = ((f32[32,4,128]{2,1,0:T(4,128)}), f32[32,4,128]{2,1,0:T(4,128)S(1)}, u32[]{:S(2)}, u32[]{:S(2)}) async-start(f32[32,4,128]{2,1,0:T(4,128)} %broadcast_in_dim.33), calls=%async_computation.8 | async-start | bytes 131072 | tf_op jit(solution)/shard_map/all_to_all | solution.py:12
  166.8 1.0 convolution_convert_fusion.3
  167.8 12.3 %all-to-all-done.8 = f32[32,4,128]{2,1,0:T(4,128)S(1)} async-done(((f32[32,4,128]{2,1,0:T(4,128)}), f32[32,4,128]{2,1,0:T(4,128)S(1)}, u32[]{:S(2)}, u32[]{:S(2)}) %all-to-all-start.8) | async-done | bytes 65568 | tf_op jit(solution)/shard_map/all_to_all | solution.py:12
  180.1 4.4 %all-to-all-start.5 = ((bf16[32,32,128]{2,1,0:T(8,128)(2,1)}), bf16[32,32,128]{2,1,0:T(8,128)(2,1)S(1)}, u32[]{:S(2)}, u32[]{:S(2)}) async-start(bf16[32,32,128]{2,1,0:T(8,128)(2,1)} %bitcast.15), calls=%async_computation.5 | async-start | bytes 524288 | tf_op jit(solution)/shard_map/all_to_all | solution.py:12
  184.5 0.1 copy.17
  184.6 0.1 copy.20
  184.8 0.1 copy.18
  184.9 20.0 %all-to-all-done.5 = bf16[32,32,128]{2,1,0:T(8,128)(2,1)S(1)} async-done(((bf16[32,32,128]{2,1,0:T(8,128)(2,1)}), bf16[32,32,128]{2,1,0:T(8,128)(2,1)S(1)}, u32[]{:S(2)}, u32[]{:S(2)}) %all-to-all-start.5) | async-done | bytes 262176 | tf_op jit(solution)/shard_map/all_to_all | solution.py:12
  205.0 0.1 copy.19
  205.1 2.3 %fusion = bf16[1,1,32,128,128]{4,3,2,1,0:T(8,128)(2,1)} fusion(bf16[1,1,32,128,128]{4,3,2,1,0:T(8,128)(2,1)S(1)} %copy-done, bf16[32,32,128]{2,0,1:T(8,128)(2,1)S(1)} %copy.18, bf16[32,32,128]{2,0,1:T(8,128)(2,1)S(1)} %copy.17, bf16[32,32,128]{2,0,1:T(8,128)(2,1)S(1)} %copy.20, bf16[32,32,128]{2,0,1:T(8,128)(2,1)S(1)} %copy.19), kind=kOutput, calls=%fused_computation.1 | convolution fusion | flops 73924608 | bytes 3145728 | tf_op jit(solution)/shard_map/nki,nkj->kij/dot_general | solution.py:90
  207.3 0.6 copy.24
  (10 shorter events, 0.2 us)
Async XLA Ops:
  0.6 49.5 %copy-start.2 = (s32[1,1,32]{2,1,0:T(1,128)S(1)}, s32[1,1,32]{2,1,0:T(1,128)}, u32[]{:S(2)}) copy-start(s32[1,1,32]{2,1,0:T(1,128)} %param.9) | copy-start | bytes 388
  1.7 61.4 %copy-start = (bf16[1,1,32,128,128]{4,3,2,1,0:T(8,128)(2,1)S(1)}, bf16[1,1,32,128,128]{4,3,2,1,0:T(8,128)(2,1)}, u32[]{:S(2)}) copy-start(bf16[1,1,32,128,128]{4,3,2,1,0:T(8,128)(2,1)} %param.6) | copy-start | bytes 3145732
  1.7 34.0 %collective-permute-start.1 = (bf16[64,128]{1,0:T(8,128)(2,1)S(1)}, bf16[64,128]{1,0:T(8,128)(2,1)S(1)}, u32[]{:S(2)}, u32[]{:S(2)}) collective-permute-start(bf16[64,128]{1,0:T(8,128)(2,1)S(1)} %get-tuple-element.12), channel_id=1, source_target_pairs={{0,0},{1,32},{2,64},{3,96},{4,128},{5,160},{6,192},{7,224},{8,256}... | collective-permute-start | bytes 49160 | tf_op jit(solution)/shard_map/ppermute | solution.py:37
  2.5 33.2 %collective-permute-start = (bf16[64,128]{1,0:T(8,128)(2,1)S(1)}, bf16[64,128]{1,0:T(8,128)(2,1)S(1)}, u32[]{:S(2)}, u32[]{:S(2)}) collective-permute-start(bf16[64,128]{1,0:T(8,128)(2,1)S(1)} %get-tuple-element.13), channel_id=1, source_target_pairs={{0,16},{1,48},{2,80},{3,112},{4,144},{5,176},{6,208},{7,240},{8,27... | collective-permute-start | bytes 49160 | tf_op jit(solution)/shard_map/ppermute | solution.py:37
  11.6 22.7 %all-to-all-start = ((s32[16,1,32]{2,1,0:T(1,128)}), s32[16,1,32]{2,1,0:T(1,128)S(1)}, u32[]{:S(2)}, u32[]{:S(2)}) async-start(s32[16,1,32]{2,1,0:T(1,128)} %broadcast_in_dim.28), calls=%async_computation | async-start | bytes 16384 | tf_op jit(solution)/shard_map/all_to_all | solution.py:12
  50.8 24.3 %all-to-all-start.2 = ((s32[32,1,32]{2,1,0:T(1,128)}), s32[32,1,32]{2,1,0:T(1,128)S(1)}, u32[]{:S(2)}, u32[]{:S(2)}) async-start(s32[32,1,32]{2,1,0:T(1,128)} %broadcast_in_dim.30), calls=%async_computation.2 | async-start | bytes 32768 | tf_op jit(solution)/shard_map/all_to_all | solution.py:12
  63.5 40.8 %copy-start.1 = (f32[16384]{0:T(1024)S(1)}, f32[16384]{0:T(1024)}, u32[]{:S(2)}) copy-start(f32[16384]{0:T(1024)} %param.7) | copy-start | bytes 196612
  75.1 25.1 %all-to-all-start.3 = ((bf16[32,32,128]{2,1,0:T(8,128)(2,1)}), bf16[32,32,128]{2,1,0:T(8,128)(2,1)S(1)}, u32[]{:S(2)}, u32[]{:S(2)}) async-start(bf16[32,32,128]{2,1,0:T(8,128)(2,1)} %copy.16), calls=%async_computation.3 | async-start | bytes 524288 | tf_op jit(solution)/shard_map/all_to_all | solution.py:12
  100.2 23.9 %all-to-all-start.6 = ((bf16[32,32,128]{2,1,0:T(8,128)(2,1)}), bf16[32,32,128]{2,1,0:T(8,128)(2,1)S(1)}, u32[]{:S(2)}, u32[]{:S(2)}) async-start(bf16[32,32,128]{2,1,0:T(8,128)(2,1)} %bitcast.16), calls=%async_computation.6 | async-start | bytes 524288 | tf_op jit(solution)/shard_map/all_to_all | solution.py:12
  105.4 30.2 %collective-permute-start.3 = (bf16[64,128]{1,0:T(8,128)(2,1)S(1)}, bf16[64,128]{1,0:T(8,128)(2,1)S(1)}, u32[]{:S(2)}, u32[]{:S(2)}) collective-permute-start(bf16[64,128]{1,0:T(8,128)(2,1)S(1)} %get-tuple-element.8), channel_id=1, source_target_pairs={{0,0},{1,32},{2,64},{3,96},{4,128},{5,160},{6,192},{7,224},{8,256}... | collective-permute-start | bytes 49160 | tf_op jit(solution)/shard_map/ppermute | solution.py:37
  106.1 29.5 %collective-permute-start.2 = (bf16[64,128]{1,0:T(8,128)(2,1)S(1)}, bf16[64,128]{1,0:T(8,128)(2,1)S(1)}, u32[]{:S(2)}, u32[]{:S(2)}) collective-permute-start(bf16[64,128]{1,0:T(8,128)(2,1)S(1)} %get-tuple-element.9), channel_id=1, source_target_pairs={{0,16},{1,48},{2,80},{3,112},{4,144},{5,176},{6,208},{7,240},{8,27... | collective-permute-start | bytes 49160 | tf_op jit(solution)/shard_map/ppermute | solution.py:37
  124.1 24.7 %all-to-all-start.7 = ((f32[32,4,128]{2,1,0:T(4,128)}), f32[32,4,128]{2,1,0:T(4,128)S(1)}, u32[]{:S(2)}, u32[]{:S(2)}) async-start(f32[32,4,128]{2,1,0:T(4,128)} %bitcast.19), calls=%async_computation.7 | async-start | bytes 131072 | tf_op jit(solution)/shard_map/all_to_all | solution.py:12
  148.8 13.1 %all-to-all-start.4 = ((bf16[16,32,256]{2,1,0:T(8,128)(2,1)}), bf16[16,32,256]{2,1,0:T(8,128)(2,1)S(1)}, u32[]{:S(2)}, u32[]{:S(2)}) async-start(bf16[16,32,256]{2,1,0:T(8,128)(2,1)} %bitcast.13), calls=%async_computation.4 | async-start | bytes 524288 | tf_op jit(solution)/shard_map/all_to_all | solution.py:12
  162.5 17.6 %all-to-all-start.8 = ((f32[32,4,128]{2,1,0:T(4,128)}), f32[32,4,128]{2,1,0:T(4,128)S(1)}, u32[]{:S(2)}, u32[]{:S(2)}) async-start(f32[32,4,128]{2,1,0:T(4,128)} %broadcast_in_dim.33), calls=%async_computation.8 | async-start | bytes 131072 | tf_op jit(solution)/shard_map/all_to_all | solution.py:12
  180.1 24.9 %all-to-all-start.5 = ((bf16[32,32,128]{2,1,0:T(8,128)(2,1)}), bf16[32,32,128]{2,1,0:T(8,128)(2,1)S(1)}, u32[]{:S(2)}, u32[]{:S(2)}) async-start(bf16[32,32,128]{2,1,0:T(8,128)(2,1)} %bitcast.15), calls=%async_computation.5 | async-start | bytes 524288 | tf_op jit(solution)/shard_map/all_to_all | solution.py:12

commit v2 on v1

--- a/solution.py
+++ b/solution.py
@@ -44,54 +44,77 @@
     return jnp.concatenate(out, axis=1)
 
 
+def halves(v):
+    high = lax.reduce_precision(v, 8, 7)
+    return high.astype(BF), (v - high).astype(BF)
+
+
 def on_device(samples, blocks, diagonal, block_rows, block_cols):
     nrow, ncol = lax.axis_size("row"), lax.axis_size("col")
+    rindex = lax.axis_index("row")
     ratio = nrow // ncol
     width = samples.shape[1]
     b = blocks.shape[-1]
     cb = width // b
     rb = cb // ratio
+    own = cb // nrow
     rows, cols, local = block_rows[0, 0], block_cols[0, 0], blocks[0, 0]
     k = rows.shape[0]
     x = samples.reshape(cb, b)
     diag = diagonal.reshape(cb, b)
 
-    pick_r = pick(spread(rows[None], "col"), rb)
-    pick_c = pick(spread(cols[None], "row"), cb)
-
-    def to_rows(v):
-        t = turned(v, nrow, ncol)
-        out = jnp.dot(pick_r, t, preferred_element_type=jnp.float32).astype(BF)
-        got = exchange(out.reshape(ncol, k, ratio * b), "col")
+    def by_sample(got):
         return got.reshape(ncol, k, ratio, b).transpose(0, 2, 1, 3).reshape(nrow, k, b)
 
-    def to_cols(v):
-        out = jnp.dot(pick_c, v, preferred_element_type=jnp.float32).astype(BF)
-        return exchange(out.reshape(nrow, k, b), "row")
+    xt = turned(x, nrow, ncol)
+    tail = jnp.zeros((8, ratio * b), BF).at[0, :k].set(rows.astype(BF))
+    got = spread(jnp.concatenate([xt, tail])[None], "col").reshape(ncol, rb + 8, ratio * b)
+    pick_r = pick(got[:, rb, :k].astype(jnp.int32), rb)
+    pick_own = pick(rows, rb + 8)
+    xr = by_sample(jnp.einsum("sb,dbl->dsl", pick_own, got, preferred_element_type=jnp.float32).astype(BF))
 
-    xr = to_rows(x)
-    xc = to_cols(x)
-    prod = jnp.einsum("nki,kij->nkj", xr, local, preferred_element_type=jnp.float32)
-    terms = exchange(prod.astype(BF), "row").reshape(nrow * k, b)
-    total = lax.dot_general(pick_c, terms, (((0,), (0,)), ((), ())), preferred_element_type=jnp.float32)
-    xf = x.astype(jnp.float32)
-    mixed = (total + xf * diag).astype(BF)
+    prod = jnp.einsum("nki,kij->nkj", xr, local, preferred_element_type=jnp.float32).astype(BF)
+    tail = jnp.zeros((8, b), BF).at[0, :k].set(cols.astype(BF))
+    got = exchange(jnp.concatenate([prod, jnp.broadcast_to(tail[None], (nrow, 8, b))], axis=1), "row")
+    named = jnp.pad(got[:, k, :k].astype(jnp.int32), ((0, 0), (0, 8)), constant_values=-1)
+    pick_c = pick(named, cb)
+    total = lax.dot_general(
+        pick_c, got.reshape(nrow * (k + 8), b), (((0,), (0,)), ((), ())), preferred_element_type=jnp.float32
+    )
+    mixed = (total + x.astype(jnp.float32) * diag).astype(BF)
 
-    quads = exchange((xf * mixed.astype(jnp.float32)).reshape(nrow, cb // nrow, b), "row")
-    quad = jnp.sum(quads, axis=0)
-    mine = lax.dynamic_index_in_dim(diag.reshape(nrow, cb // nrow, b), lax.axis_index("row"), 0, keepdims=False)
+    mt = turned(mixed, nrow, ncol)
+    wr = jnp.dot(pick_r, mt, preferred_element_type=jnp.float32).astype(BF).reshape(ncol, k, ratio * b)
+    both = xt.astype(jnp.float32) * mt.astype(jnp.float32)
+    quad = jnp.sum(both.reshape(rb, ratio, b), axis=1).reshape(ncol, own, b)
+    tail = jnp.pad(jnp.concatenate(halves(quad), axis=2), ((0, 0), (0, 8 - own), (0, 0)))
+    got = exchange(jnp.concatenate([wr, tail], axis=1), "col")
+    wr = by_sample(got[:, :k])
+    quad = jnp.sum(got[:, k : k + own].astype(jnp.float32), axis=0)
+    quad = quad[:, :b] + quad[:, b:]
+    perm = []
+    for r in range(nrow):
+        for c in range(ncol):
+            perm.append((r * ncol + c, (r % ratio * ncol + c) * ncol + r // ratio))
+    quad = lax.ppermute(quad, ("row", "col"), perm)
+    mine = lax.dynamic_slice_in_dim(diag, rindex * own, own, 0)
     diag_grad = -1.0 / mine + quad / nrow
-    new_diagonal = spread(mine - TAU * diag_grad, "row").reshape(width)
+    tail = jnp.concatenate(halves(mine - TAU * diag_grad), axis=0)
 
-    wr = to_rows(mixed)
-    wc = to_cols(mixed)
+    out = jnp.dot(pick_c, jnp.concatenate([mixed, x], axis=1), preferred_element_type=jnp.float32).astype(BF)
+    out = out.reshape(nrow, k + 8, 2 * b)[:, :k]
+    out = jnp.concatenate([out[..., :b], jnp.broadcast_to(tail[None], (nrow, 8, b)), out[..., b:]], axis=1)
+    got = exchange(out, "row")
+    wc, xc = got[:, :k], got[:, k + 8 :]
+    new_diagonal = got[:, k : k + own].astype(jnp.float32) + got[:, k + own : k + 2 * own].astype(jnp.float32)
+
     left = jnp.concatenate([xr, wr], axis=0)
     right = jnp.concatenate([wc, xc], axis=0)
     both = jnp.einsum("nki,nkj->kij", left, right, preferred_element_type=jnp.float32)
     grad = both * (0.5 / nrow)
     moved = local.astype(jnp.float32) - TAU * grad
     shrunk = jnp.sign(moved) * jnp.maximum(jnp.abs(moved) - TAU * PENALTY, 0.0)
-    return shrunk.astype(BF)[None, None], new_diagonal
+    return shrunk.astype(BF)[None, None], new_diagonal.reshape(width)
 
 
 def solution(mesh):

time: 209 us -> 188 us (0.90)
  waiting for transfers between devices: 106 us -> 61.5 us
  blocking collectives: 14.2 us -> 31.2 us
  starting transfers between devices: 71.6 us -> 83.9 us
  local copies, waits for them, and re-layouts: 5.25 us -> 1.9 us
  matrix products: 7.07 us -> 4.1 us
    all_to_all x8 -> x3, waiting for transfers between devices: 106 us -> 56.1 us  [exchange(): return lax.all_to_all(x, axis, 0, 0, tiled=True)]
    all_to_all x1, blocking collectives: 14.2 us -> 31.2 us  [exchange(): return lax.all_to_all(x, axis, 0, 0, tiled=True)]
    ppermute x0 -> x1, starting transfers between devices: none -> 10.4 us  [on_device(): quad = lax.ppermute(quad, ('row', 'col'), perm)]
    ppermute x4, waiting for transfers between devices: 0.01 us -> 4.15 us  [turned(): got.append(lax.ppermute(part, ('row', 'col'), perm))]
    dot_general x5 -> x4, matrix products: 4.44 us -> 1.48 us  [the longest x1 0.54 us: on_device(): lax.dot_general(pick_c, got.reshape(nrow * (k + 8), b), (((0,), (0,)), ((...]
    all_to_all x8 -> x3, starting transfers between devices: 60.1 us -> 61.9 us  [exchange(): return lax.all_to_all(x, axis, 0, 0, tiled=True)]
  transfers between devices with their start and end apart: 12 -> 8, of which waited for: 8 -> 6; matrix products, arithmetic and copies ran while one was open for 4% -> 1% of each run, Pallas kernels for 0% -> 0%
where the time goes in v2:
time: 188 us
  starting transfers between devices  83.9 us (45%)
  waiting for transfers between devices  61.5 us (33%)
  blocking collectives  31.2 us (17%)
  other arithmetic  4.19 us (2%)
  matrix products  4.1 us (2%)
  local copies, waits for them, and re-layouts  1.9 us (1%)
    all_to_all x3, starting transfers between devices, exchange(): return lax.all_to_all(x, axis, 0, 0, tiled=True)  61.9 us
    all_to_all x3, waiting for transfers between devices, exchange(): return lax.all_to_all(x, axis, 0, 0, tiled=True)  56.1 us
    all_to_all x1, blocking collectives, exchange(): return lax.all_to_all(x, axis, 0, 0, tiled=True)  31.2 us
    ppermute x4, starting transfers between devices, turned(): got.append(lax.ppermute(part, ('row', 'col'), perm))  11.6 us
    ppermute x1, starting transfers between devices, on_device(): quad = lax.ppermute(quad, ('row', 'col'), perm)  10.4 us
    ppermute x4, waiting for transfers between devices, turned(): got.append(lax.ppermute(part, ('row', 'col'), perm))  4.15 us
  transfers between devices with their start and end apart: 8, of which 6 were waited for; matrix products, arithmetic and copies ran while one was open for 1% of the time, Pallas kernels for 0%

profile of v2, /device:TPU:2, one launch (start us, length us, event | category | flops | bytes accessed | tf_op | source)
XLA Modules:
  0.0 187.8 jit_solution(10278583379198072154)
XLA Ops:
  0.7 1.0 reduce.4
  1.7 0.0 copy-start.3
  1.7 0.0 copy-start.1
  1.7 0.7 collective-permute-start.1
  2.4 7.8 %collective-permute-start = (bf16[64,128]{1,0:T(8,128)(2,1)S(1)}, bf16[64,128]{1,0:T(8,128)(2,1)S(1)}, u32[]{:S(2)}, u32[]{:S(2)}) collective-permute-start(bf16[64,128]{1,0:T(8,128)(2,1)S(1)} %get-tuple-element.45), channel_id=1, source_target_pairs={{0,16},{1,48},{2,80},{3,112},{4,144},{5,176},{6,208},{7,240},{8,27... | collective-permute-start | bytes 49160 | tf_op jit(solution)/shard_map/ppermute | solution.py:37
  10.2 0.7 convert_bitcast_fusion
  10.9 0.0 collective-permute-done.1
  10.9 1.1 collective-permute-done
  12.0 0.9 broadcast_in_dim.10
  12.9 28.4 %all-to-all-start = ((bf16[16,1,72,256]{3,2,1,0:T(8,128)(2,1)}), bf16[16,1,72,256]{3,2,1,0:T(8,128)(2,1)S(1)}, u32[]{:S(2)}, u32[]{:S(2)}) async-start(bf16[16,1,72,256]{3,2,1,0:T(8,128)(2,1)} %broadcast_in_dim.10), calls=%async_computation | async-start | bytes 1179648 | tf_op jit(solution)/shard_map/all_to_all | solution.py:12
  41.3 0.0 copy-done.3
  41.3 0.0 copy-start
  41.3 13.1 %all-to-all-done = bf16[16,1,72,256]{3,2,1,0:T(8,128)(2,1)S(1)} async-done(((bf16[16,1,72,256]{3,2,1,0:T(8,128)(2,1)}), bf16[16,1,72,256]{3,2,1,0:T(8,128)(2,1)S(1)}, u32[]{:S(2)}, u32[]{:S(2)}) %all-to-all-start) | async-done | bytes 589856 | tf_op jit(solution)/shard_map/all_to_all | solution.py:12
  54.4 0.0 copy-done.1
  54.4 0.3 fusion.1
  54.8 0.0 copy-done
  54.8 0.4 fusion.2
  55.2 0.0 copy-start.2
  55.2 0.1 copy.25
  55.4 31.2 %all_to_all.20 = bf16[32,40,128]{2,1,0:T(8,128)(2,1)S(1)} all-to-all(bf16[32,40,128]{2,1,0:T(8,128)(2,1)S(1)} %copy.25), channel_id=1, replica_groups=mesh['row'=32,'col'=16] {'row'}, dimensions={0} | all-to-all | bytes 655360 | tf_op jit(solution)/shard_map/all_to_all | solution.py:12
  86.6 0.1 reshape.136
  86.7 0.0 copy-done.2
  86.7 0.5 fusion.3
  87.3 0.7 collective-permute-start.3
  87.9 2.5 %collective-permute-start.2 = (bf16[64,128]{1,0:T(8,128)(2,1)S(1)}, bf16[64,128]{1,0:T(8,128)(2,1)S(1)}, u32[]{:S(2)}, u32[]{:S(2)}) collective-permute-start(bf16[64,128]{1,0:T(8,128)(2,1)S(1)} %get-tuple-element.41), channel_id=1, source_target_pairs={{0,16},{1,48},{2,80},{3,112},{4,144},{5,176},{6,208},{7,240},{8,27... | collective-permute-start | bytes 49160 | tf_op jit(solution)/shard_map/ppermute | solution.py:37
  90.4 0.1 reshape.135
  90.5 0.0 collective-permute-done.3
  90.5 3.0 %collective-permute-done.2 = bf16[64,128]{1,0:T(8,128)(2,1)S(1)} collective-permute-done((bf16[64,128]{1,0:T(8,128)(2,1)S(1)}, bf16[64,128]{1,0:T(8,128)(2,1)S(1)}, u32[]{:S(2)}, u32[]{:S(2)}) %collective-permute-start.2) | collective-permute-done | bytes 16416 | tf_op jit(solution)/shard_map/ppermute | solution.py:37
  93.6 0.3 convolution_convert_fusion.1
  93.9 0.7 pad_maximum_fusion.2
  94.7 19.6 %all-to-all-start.2 = ((bf16[16,40,256]{2,1,0:T(8,128)(2,1)}), bf16[16,40,256]{2,1,0:T(8,128)(2,1)S(1)}, u32[]{:S(2)}, u32[]{:S(2)}) async-start(bf16[16,40,256]{2,1,0:T(8,128)(2,1)} %pad_maximum_fusion.2), calls=%async_computation.2 | async-start | bytes 655360 | tf_op jit(solution)/shard_map/all_to_all | solution.py:12
  114.3 0.4 convolution_convert_fusion
  114.7 9.9 %all-to-all-done.2 = bf16[16,40,256]{2,1,0:T(8,128)(2,1)S(1)} async-done(((bf16[16,40,256]{2,1,0:T(8,128)(2,1)}), bf16[16,40,256]{2,1,0:T(8,128)(2,1)S(1)}, u32[]{:S(2)}, u32[]{:S(2)}) %all-to-all-start.2) | async-done | bytes 327712 | tf_op jit(solution)/shard_map/all_to_all | solution.py:12
  124.6 10.4 %collective-permute-start.4 = (f32[4,128]{1,0:T(4,128)S(1)}, f32[4,128]{1,0:T(4,128)S(1)}, u32[]{:S(2)}, u32[]{:S(2)}) collective-permute-start(f32[4,128]{1,0:T(4,128)S(1)} %slice_add_fusion), channel_id=1, source_target_pairs={{0,0},{1,16},{2,32},{3,48},{4,64},{5,80},{6,96},{7,112},{8,128},{9... | collective-permute-start | bytes 6152 | tf_op jit(solution)/shard_map/ppermute | solution.py:99
  135.0 0.1 fusion.36
  135.1 1.2 collective-permute-done.4
  136.4 0.9 pad_maximum_fusion
  137.2 13.9 %all-to-all-start.3 = ((bf16[32,72,128]{2,1,0:T(8,128)(2,1)}), bf16[32,72,128]{2,1,0:T(8,128)(2,1)S(1)}, u32[]{:S(2)}, u32[]{:S(2)}) async-start(bf16[32,72,128]{2,1,0:T(8,128)(2,1)} %pad_maximum_fusion), calls=%async_computation.3 | async-start | bytes 1179648 | tf_op jit(solution)/shard_map/all_to_all | solution.py:12
  151.1 0.1 copy.27
  151.3 0.1 copy.28
  151.4 33.2 %all-to-all-done.3 = bf16[32,72,128]{2,1,0:T(8,128)(2,1)S(1)} async-done(((bf16[32,72,128]{2,1,0:T(8,128)(2,1)}), bf16[32,72,128]{2,1,0:T(8,128)(2,1)S(1)}, u32[]{:S(2)}, u32[]{:S(2)}) %all-to-all-start.3) | async-done | bytes 589856 | tf_op jit(solution)/shard_map/all_to_all | solution.py:12
  184.7 0.1 copy.32
  184.8 0.1 copy.33
  184.9 2.2 %fusion = bf16[1,1,32,128,128]{4,3,2,1,0:T(8,128)(2,1)} fusion(bf16[1,1,32,128,128]{4,3,2,1,0:T(8,128)(2,1)S(1)} %copy-done, bf16[32,32,128]{2,0,1:T(8,128)(2,1)S(1)} %copy.28, bf16[32,32,128]{2,0,1:T(8,128)(2,1)S(1)} %copy.27, bf16[32,32,128]{2,0,1:T(8,128)(2,1)S(1)} %copy.33, bf16[32,32,128]{2,0,1:T(8,128)(2,1)S(1)} %copy.32), kind=kOutput, calls=%fused_computation.2 | convolution fusion | flops 73924608 | bytes 3145728 | tf_op jit(solution)/shard_map/nki,nkj->kij/dot_general | solution.py:113
  187.1 0.6 convert_add_fusion
  (27 shorter events, 0.5 us)
Async XLA Ops:
  1.7 39.6 %copy-start.3 = (s32[1,1,32]{2,1,0:T(1,128)S(1)}, s32[1,1,32]{2,1,0:T(1,128)}, u32[]{:S(2)}) copy-start(s32[1,1,32]{2,1,0:T(1,128)} %param.13) | copy-start | bytes 388
  1.7 52.7 %copy-start.1 = (s32[1,1,32]{2,1,0:T(1,128)S(1)}, s32[1,1,32]{2,1,0:T(1,128)}, u32[]{:S(2)}) copy-start(s32[1,1,32]{2,1,0:T(1,128)} %param.12) | copy-start | bytes 388
  1.7 9.2 %collective-permute-start.1 = (bf16[64,128]{1,0:T(8,128)(2,1)S(1)}, bf16[64,128]{1,0:T(8,128)(2,1)S(1)}, u32[]{:S(2)}, u32[]{:S(2)}) collective-permute-start(bf16[64,128]{1,0:T(8,128)(2,1)S(1)} %get-tuple-element.44), channel_id=1, source_target_pairs={{0,0},{1,32},{2,64},{3,96},{4,128},{5,160},{6,192},{7,224},{8,256}... | collective-permute-start | bytes 49160 | tf_op jit(solution)/shard_map/ppermute | solution.py:37
  2.4 9.6 %collective-permute-start = (bf16[64,128]{1,0:T(8,128)(2,1)S(1)}, bf16[64,128]{1,0:T(8,128)(2,1)S(1)}, u32[]{:S(2)}, u32[]{:S(2)}) collective-permute-start(bf16[64,128]{1,0:T(8,128)(2,1)S(1)} %get-tuple-element.45), channel_id=1, source_target_pairs={{0,16},{1,48},{2,80},{3,112},{4,144},{5,176},{6,208},{7,240},{8,27... | collective-permute-start | bytes 49160 | tf_op jit(solution)/shard_map/ppermute | solution.py:37
  12.9 41.5 %all-to-all-start = ((bf16[16,1,72,256]{3,2,1,0:T(8,128)(2,1)}), bf16[16,1,72,256]{3,2,1,0:T(8,128)(2,1)S(1)}, u32[]{:S(2)}, u32[]{:S(2)}) async-start(bf16[16,1,72,256]{3,2,1,0:T(8,128)(2,1)} %broadcast_in_dim.10), calls=%async_computation | async-start | bytes 1179648 | tf_op jit(solution)/shard_map/all_to_all | solution.py:12
  41.3 13.5 %copy-start = (bf16[1,1,32,128,128]{4,3,2,1,0:T(8,128)(2,1)S(1)}, bf16[1,1,32,128,128]{4,3,2,1,0:T(8,128)(2,1)}, u32[]{:S(2)}) copy-start(bf16[1,1,32,128,128]{4,3,2,1,0:T(8,128)(2,1)} %param.10) | copy-start | bytes 3145732
  55.2 31.5 %copy-start.2 = (f32[16384]{0:T(1024)S(1)}, f32[16384]{0:T(1024)}, u32[]{:S(2)}) copy-start(f32[16384]{0:T(1024)} %param.11) | copy-start | bytes 196612
  87.3 3.3 %collective-permute-start.3 = (bf16[64,128]{1,0:T(8,128)(2,1)S(1)}, bf16[64,128]{1,0:T(8,128)(2,1)S(1)}, u32[]{:S(2)}, u32[]{:S(2)}) collective-permute-start(bf16[64,128]{1,0:T(8,128)(2,1)S(1)} %get-tuple-element.40), channel_id=1, source_target_pairs={{0,0},{1,32},{2,64},{3,96},{4,128},{5,160},{6,192},{7,224},{8,256}... | collective-permute-start | bytes 49160 | tf_op jit(solution)/shard_map/ppermute | solution.py:37
  87.9 5.6 %collective-permute-start.2 = (bf16[64,128]{1,0:T(8,128)(2,1)S(1)}, bf16[64,128]{1,0:T(8,128)(2,1)S(1)}, u32[]{:S(2)}, u32[]{:S(2)}) collective-permute-start(bf16[64,128]{1,0:T(8,128)(2,1)S(1)} %get-tuple-element.41), channel_id=1, source_target_pairs={{0,16},{1,48},{2,80},{3,112},{4,144},{5,176},{6,208},{7,240},{8,27... | collective-permute-start | bytes 49160 | tf_op jit(solution)/shard_map/ppermute | solution.py:37
  94.7 29.8 %all-to-all-start.2 = ((bf16[16,40,256]{2,1,0:T(8,128)(2,1)}), bf16[16,40,256]{2,1,0:T(8,128)(2,1)S(1)}, u32[]{:S(2)}, u32[]{:S(2)}) async-start(bf16[16,40,256]{2,1,0:T(8,128)(2,1)} %pad_maximum_fusion.2), calls=%async_computation.2 | async-start | bytes 655360 | tf_op jit(solution)/shard_map/all_to_all | solution.py:12
  124.6 11.7 %collective-permute-start.4 = (f32[4,128]{1,0:T(4,128)S(1)}, f32[4,128]{1,0:T(4,128)S(1)}, u32[]{:S(2)}, u32[]{:S(2)}) collective-permute-start(f32[4,128]{1,0:T(4,128)S(1)} %slice_add_fusion), channel_id=1, source_target_pairs={{0,0},{1,16},{2,32},{3,48},{4,64},{5,80},{6,96},{7,112},{8,128},{9... | collective-permute-start | bytes 6152 | tf_op jit(solution)/shard_map/ppermute | solution.py:99
  137.2 47.4 %all-to-all-start.3 = ((bf16[32,72,128]{2,1,0:T(8,128)(2,1)}), bf16[32,72,128]{2,1,0:T(8,128)(2,1)S(1)}, u32[]{:S(2)}, u32[]{:S(2)}) async-start(bf16[32,72,128]{2,1,0:T(8,128)(2,1)} %pad_maximum_fusion), calls=%async_computation.3 | async-start | bytes 1179648 | tf_op jit(solution)/shard_map/all_to_all | solution.py:12

commit v3 on v1

v3 whole, which is shorter than its diff:
```python
import jax
import jax.numpy as jnp
from jax import lax
from jax.sharding import PartitionSpec as P

TAU = 0.5
PENALTY = 0.1
BF = jnp.bfloat16


def exchange(x, axis):
    return lax.all_to_all(x, axis, 0, 0, tiled=True)


def spread(x, axis):
    return exchange(jnp.broadcast_to(x[None], (lax.axis_size(axis),) + x.shape), axis)


def pick(index, size):
    return (index.reshape(-1, 1) == jnp.arange(size, dtype=index.dtype)[None, :]).astype(BF)


def halves(v):
    high = lax.reduce_precision(v, 8, 7)
    return high.astype(BF), (v - high).astype(BF)


def on_device(samples, blocks, diagonal, block_rows, block_cols):
    nrow, ncol = lax.axis_size("row"), lax.axis_size("col")
    ratio = nrow // ncol
    width = samples.shape[1]
    b = blocks.shape[-1]
    cb = width // b
    rb = cb // ratio
    own = cb // nrow
    rows, cols, local = block_rows[0, 0], block_cols[0, 0], blocks[0, 0]
    k = rows.shape[0]
    x = samples.reshape(cb, b)
    diag = diagonal.reshape(cb, b)

    groups = [[(ratio * g + n % ratio) * ncol + n // ratio for n in range(nrow)] for g in range(ncol)]
    perm = [(n * ncol + g, groups[g][n]) for n in range(nrow) for g in range(ncol)]

    def turned(v):
        return lax.ppermute(v, ("row", "col"), perm)

    def in_group(v):
        return lax.all_to_all(v, ("row", "col"), 0, 0, tiled=True, axis_index_groups=groups)

    tail = jnp.zeros((8, b), BF).at[0, :k].set(rows.astype(BF))
    parts = turned(x).reshape(ratio, rb, b)
    parts = jnp.concatenate([parts, jnp.broadcast_to(tail[None], (ratio, 8, b))], axis=1)
    got = in_group(jnp.broadcast_to(parts[None], (ncol, ratio, rb + 8, b)).reshape(nrow, rb + 8, b))
    named = got[:, rb, :k].astype(jnp.int32) + rb * (jnp.arange(nrow, dtype=jnp.int32) % ratio)[:, None]
    pick_r = pick(named, cb)
    xr = jnp.einsum("sb,nbl->nsl", pick(rows, rb + 8), got, preferred_element_type=jnp.float32).astype(BF)

    prod = jnp.einsum("nki,kij->nkj", xr, local, preferred_element_type=jnp.float32).astype(BF)
    tail = jnp.zeros((8, b), BF).at[0, :k].set(cols.astype(BF))
    got = exchange(jnp.concatenate([prod, jnp.broadcast_to(tail[None], (nrow, 8, b))], axis=1), "row")
    named = jnp.pad(got[:, k, :k].astype(jnp.int32), ((0, 0), (0, 8)), constant_values=-1)
    pick_c = pick(named, cb)
    total = lax.dot_general(
        pick_c, got.reshape(nrow * (k + 8), b), (((0,), (0,)), ((), ())), preferred_element_type=jnp.float32
    )
    xf = x.astype(jnp.float32)
    mixed = (total + xf * diag).astype(BF)
    mt = turned(mixed)

    quad = (xf * mixed.astype(jnp.float32)).reshape(nrow, own, b)
    out = jnp.dot(pick_c, jnp.concatenate([mixed, x], axis=1), preferred_element_type=jnp.float32).astype(BF)
    out = out.reshape(nrow, k + 8, 2 * b)[:, :k]
    got = exchange(jnp.concatenate([out[..., :b], *halves(quad), out[..., b:]], axis=1), "row")
    got, mt = lax.optimization_barrier((got, mt))
    wc, xc = got[:, :k], got[:, k + 2 * own :]
    quad = jnp.sum(got[:, k : k + 2 * own].astype(jnp.float32), axis=0)
    quad = quad[:own] + quad[own:]
    mine = lax.dynamic_slice_in_dim(diag, lax.axis_index("row") * own, own, 0)
    diag_grad = -1.0 / mine + quad / nrow
    mine = mine - TAU * diag_grad

    wr = in_group(jnp.dot(pick_r, mt, preferred_element_type=jnp.float32).astype(BF).reshape(nrow, k, b))
    wr, mine = lax.optimization_barrier((wr, mine))
    new_diagonal = spread(mine, "row").reshape(width)

    left = jnp.concatenate([xr, wr], axis=0)
    right = jnp.concatenate([wc, xc], axis=0)
    both = jnp.einsum("nki,nkj->kij", left, right, preferred_element_type=jnp.float32)
    grad = both * (0.5 / nrow)
    moved = local.astype(jnp.float32) - TAU * grad
    shrunk = jnp.sign(moved) * jnp.maximum(jnp.abs(moved) - TAU * PENALTY, 0.0)
    return shrunk.astype(BF)[None, None], new_diagonal


def solution(mesh):
    in_specs = (
        P("row", "col"),
        P("row", "col", None, None, None),
        P("col"),
        P("row", "col", None),
        P("row", "col", None),
    )
    out_specs = (P("row", "col", None, None, None), P("col"))
    return jax.shard_map(
        on_device, mesh=mesh, in_specs=in_specs, out_specs=out_specs, check_vma=False
    )
```

time: 209 us -> 158 us (0.76)
  waiting for transfers between devices: 106 us -> 62.3 us
  starting transfers between devices: 71.6 us -> 46.1 us
  blocking collectives: 14.2 us -> 38.1 us
  local copies, waits for them, and re-layouts: 5.25 us -> 2.89 us
  matrix products: 7.07 us -> 4.86 us
    all_to_all x8 -> x2, waiting for transfers between devices: 106 us -> 44.2 us  [exchange(): return lax.all_to_all(x, axis, 0, 0, tiled=True)]
    all_to_all x8 -> x2, starting transfers between devices: 60.1 us -> 11.1 us  [exchange(): return lax.all_to_all(x, axis, 0, 0, tiled=True)]
    all_to_all x0 -> x2, starting transfers between devices: none -> 33.7 us  [in_group(): lax.all_to_all(v, ('row', 'col'), 0, 0, tiled=True, axis_index_groups=gro...]
    all_to_all x1, blocking collectives: 14.2 us -> 38.1 us  [exchange(): return lax.all_to_all(x, axis, 0, 0, tiled=True)]
    all_to_all x0 -> x2, waiting for transfers between devices: none -> 18 us  [in_group(): lax.all_to_all(v, ('row', 'col'), 0, 0, tiled=True, axis_index_groups=gro...]
    ppermute x4 -> x2, starting transfers between devices: 11.5 us -> 1.32 us  [turned(): return lax.ppermute(v, ('row', 'col'), perm)]
    dot_general x5 -> x4, matrix products: 4.44 us -> 2.23 us  [the longest x1 1.02 us: on_device(): jnp.dot(pick_r, mt, preferred_element_type=jnp.float32).astype(BF)]
  transfers between devices with their start and end apart: 12 -> 6, of which waited for: 8 -> 4; matrix products, arithmetic and copies ran while one was open for 4% -> 2% of each run, Pallas kernels for 0% -> 0%
where the time goes in v3:
time: 158 us
  waiting for transfers between devices  62.3 us (39%)
  starting transfers between devices  46.1 us (29%)
  blocking collectives  38.1 us (24%)
  matrix products  4.86 us (3%)
  local copies, waits for them, and re-layouts  2.89 us (2%)
  other arithmetic  2.82 us (2%)
    all_to_all x2, waiting for transfers between devices, exchange(): return lax.all_to_all(x, axis, 0, 0, tiled=True)  44.2 us
    all_to_all x1, blocking collectives, exchange(): return lax.all_to_all(x, axis, 0, 0, tiled=True)  38.1 us
    all_to_all x2, starting transfers between devices, in_group(): lax.all_to_all(v, ('row', 'col'), 0, 0, tiled=True, axis_index_groups=gro...  33.7 us
    all_to_all x2, waiting for transfers between devices, in_group(): lax.all_to_all(v, ('row', 'col'), 0, 0, tiled=True, axis_index_groups=gro...  18 us
    all_to_all x2, starting transfers between devices, exchange(): return lax.all_to_all(x, axis, 0, 0, tiled=True)  11.1 us
  transfers between devices with their start and end apart: 6, of which 4 were waited for; matrix products, arithmetic and copies ran while one was open for 2% of the time, Pallas kernels for 0%

profile of v3, /device:TPU:2, one launch (start us, length us, event | category | flops | bytes accessed | tf_op | source)
XLA Modules:
  0.0 157.9 jit_solution(12161358072502849974)
XLA Ops:
  0.6 0.0 copy-start.1
  0.6 0.0 copy-start.3
  0.7 1.0 reduce.4
  1.7 0.7 collective-permute-start
  2.3 0.7 convert_element_type.68
  3.0 0.0 collective-permute-done
  3.0 0.9 broadcast_in_dim.16
  3.9 0.0 copy-start
  3.9 24.1 %all-to-all-start = ((bf16[32,72,128]{2,1,0:T(8,128)(2,1)}), bf16[32,72,128]{2,1,0:T(8,128)(2,1)S(1)}, u32[]{:S(2)}, u32[]{:S(2)}) async-start(bf16[32,72,128]{2,1,0:T(8,128)(2,1)} %bitcast.3), calls=%async_computation | async-start | bytes 1179648 | tf_op jit(solution)/shard_map/all_to_all | solution.py:48
  28.0 0.0 copy-done.3
  28.1 10.6 %all-to-all-done = bf16[32,72,128]{2,1,0:T(8,128)(2,1)S(1)} async-done(((bf16[32,72,128]{2,1,0:T(8,128)(2,1)}), bf16[32,72,128]{2,1,0:T(8,128)(2,1)S(1)}, u32[]{:S(2)}, u32[]{:S(2)}) %all-to-all-start) | async-done | bytes 589856 | tf_op jit(solution)/shard_map/all_to_all | solution.py:48
  38.6 0.0 copy-done.1
  38.6 0.3 fusion.1
  38.9 0.0 copy-done
  38.9 0.4 fusion.2
  39.3 0.0 copy-start.2
  39.4 0.1 copy.26
  39.5 38.1 %all_to_all.25 = bf16[32,40,128]{2,1,0:T(8,128)(2,1)S(1)} all-to-all(bf16[32,40,128]{2,1,0:T(8,128)(2,1)S(1)} %copy.26), channel_id=1, replica_groups=mesh['row'=32,'col'=16] {'row'}, dimensions={0} | all-to-all | bytes 655360 | tf_op jit(solution)/shard_map/all_to_all | solution.py:12
  77.6 0.1 reshape.132
  77.7 0.0 copy-done.2
  77.7 0.5 convert_multiply_fusion
  78.3 0.4 convolution_convert_fusion
  78.7 0.1 fusion.24
  78.8 0.9 pad_maximum_fusion
  79.7 4.1 %all-to-all-start.2 = ((bf16[32,72,128]{2,1,0:T(8,128)(2,1)}), bf16[32,72,128]{2,1,0:T(8,128)(2,1)S(1)}, u32[]{:S(2)}, u32[]{:S(2)}) async-start(bf16[32,72,128]{2,1,0:T(8,128)(2,1)} %pad_maximum_fusion), calls=%async_computation.2 | async-start | bytes 1179648 | tf_op jit(solution)/shard_map/all_to_all | solution.py:12
  83.8 0.1 add.48
  83.9 0.1 add.49
  84.0 0.7 collective-permute-start.1
  84.6 0.1 fusion.17
  84.7 0.1 reshape.131
  84.8 0.0 collective-permute-done.1
  84.8 33.3 %all-to-all-done.2 = bf16[32,72,128]{2,1,0:T(8,128)(2,1)S(1)} async-done(((bf16[32,72,128]{2,1,0:T(8,128)(2,1)}), bf16[32,72,128]{2,1,0:T(8,128)(2,1)S(1)}, u32[]{:S(2)}, u32[]{:S(2)}) %all-to-all-start.2) | async-done | bytes 589856 | tf_op jit(solution)/shard_map/all_to_all | solution.py:12
  118.1 1.0 convolution_convert_fusion.1
  119.1 9.7 %all-to-all-start.3 = ((bf16[32,32,128]{2,1,0:T(8,128)(2,1)}), bf16[32,32,128]{2,1,0:T(8,128)(2,1)S(1)}, u32[]{:S(2)}, u32[]{:S(2)}) async-start(bf16[32,32,128]{2,1,0:T(8,128)(2,1)} %bitcast.14), calls=%async_computation.3 | async-start | bytes 524288 | tf_op jit(solution)/shard_map/all_to_all | solution.py:48
  128.8 0.1 copy.28
  128.9 7.5 %all-to-all-done.3 = bf16[32,32,128]{2,1,0:T(8,128)(2,1)S(1)} async-done(((bf16[32,32,128]{2,1,0:T(8,128)(2,1)}), bf16[32,32,128]{2,1,0:T(8,128)(2,1)S(1)}, u32[]{:S(2)}, u32[]{:S(2)}) %all-to-all-start.3) | async-done | bytes 262176 | tf_op jit(solution)/shard_map/all_to_all | solution.py:48
  136.5 0.6 broadcast_in_dim.20
  137.1 7.0 %all-to-all-start.4 = ((f32[32,4,128]{2,1,0:T(4,128)}), f32[32,4,128]{2,1,0:T(4,128)S(1)}, u32[]{:S(2)}, u32[]{:S(2)}) async-start(f32[32,4,128]{2,1,0:T(4,128)} %broadcast_in_dim.20), calls=%async_computation.4 | async-start | bytes 131072 | tf_op jit(solution)/shard_map/all_to_all | solution.py:12
  144.1 2.3 %fusion = bf16[1,1,32,128,128]{4,3,2,1,0:T(8,128)(2,1)} fusion(bf16[1,1,32,128,128]{4,3,2,1,0:T(8,128)(2,1)S(1)} %copy-done, bf16[32,32,128]{2,0,1:T(8,128)(2,1)S(1)} %get-tuple-element.37, bf16[32,32,128]{2,0,1:T(8,128)(2,1)S(1)} %get-tuple-element.36, bf16[64,32,128]{2,1,0:T(8,128)(2,1)S(1)} %pad_maximum_fusion.1), kind=kOutput, calls=%fused_computation.2 | convolution fusion | flops 72876032 | bytes 3145728 | tf_op jit(solution)/shard_map/nki,nkj->kij/dot_general | solution.py:88
  146.3 10.9 %all-to-all-done.4 = f32[32,4,128]{2,1,0:T(4,128)S(1)} async-done(((f32[32,4,128]{2,1,0:T(4,128)}), f32[32,4,128]{2,1,0:T(4,128)S(1)}, u32[]{:S(2)}, u32[]{:S(2)}) %all-to-all-start.4) | async-done | bytes 65568 | tf_op jit(solution)/shard_map/all_to_all | solution.py:12
  157.3 0.6 copy.39
  (17 shorter events, 0.3 us)
Async XLA Ops:
  0.6 38.0 %copy-start.1 = (s32[1,1,32]{2,1,0:T(1,128)S(1)}, s32[1,1,32]{2,1,0:T(1,128)}, u32[]{:S(2)}) copy-start(s32[1,1,32]{2,1,0:T(1,128)} %param.12) | copy-start | bytes 388
  0.6 27.4 %copy-start.3 = (s32[1,1,32]{2,1,0:T(1,128)S(1)}, s32[1,1,32]{2,1,0:T(1,128)}, u32[]{:S(2)}) copy-start(s32[1,1,32]{2,1,0:T(1,128)} %param.13) | copy-start | bytes 388
  1.7 1.3 collective-permute-start
  3.9 35.0 %copy-start = (bf16[1,1,32,128,128]{4,3,2,1,0:T(8,128)(2,1)S(1)}, bf16[1,1,32,128,128]{4,3,2,1,0:T(8,128)(2,1)}, u32[]{:S(2)}) copy-start(bf16[1,1,32,128,128]{4,3,2,1,0:T(8,128)(2,1)} %param.10) | copy-start | bytes 3145732
  3.9 34.7 %all-to-all-start = ((bf16[32,72,128]{2,1,0:T(8,128)(2,1)}), bf16[32,72,128]{2,1,0:T(8,128)(2,1)S(1)}, u32[]{:S(2)}, u32[]{:S(2)}) async-start(bf16[32,72,128]{2,1,0:T(8,128)(2,1)} %bitcast.3), calls=%async_computation | async-start | bytes 1179648 | tf_op jit(solution)/shard_map/all_to_all | solution.py:48
  39.3 38.4 %copy-start.2 = (f32[16384]{0:T(1024)S(1)}, f32[16384]{0:T(1024)}, u32[]{:S(2)}) copy-start(f32[16384]{0:T(1024)} %param.11) | copy-start | bytes 196612
  79.7 38.4 %all-to-all-start.2 = ((bf16[32,72,128]{2,1,0:T(8,128)(2,1)}), bf16[32,72,128]{2,1,0:T(8,128)(2,1)S(1)}, u32[]{:S(2)}, u32[]{:S(2)}) async-start(bf16[32,72,128]{2,1,0:T(8,128)(2,1)} %pad_maximum_fusion), calls=%async_computation.2 | async-start | bytes 1179648 | tf_op jit(solution)/shard_map/all_to_all | solution.py:12
  84.0 0.8 collective-permute-start.1
  119.1 17.3 %all-to-all-start.3 = ((bf16[32,32,128]{2,1,0:T(8,128)(2,1)}), bf16[32,32,128]{2,1,0:T(8,128)(2,1)S(1)}, u32[]{:S(2)}, u32[]{:S(2)}) async-start(bf16[32,32,128]{2,1,0:T(8,128)(2,1)} %bitcast.14), calls=%async_computation.3 | async-start | bytes 524288 | tf_op jit(solution)/shard_map/all_to_all | solution.py:48
  137.1 20.2 %all-to-all-start.4 = ((f32[32,4,128]{2,1,0:T(4,128)}), f32[32,4,128]{2,1,0:T(4,128)S(1)}, u32[]{:S(2)}, u32[]{:S(2)}) async-start(f32[32,4,128]{2,1,0:T(4,128)} %broadcast_in_dim.20), calls=%async_computation.4 | async-start | bytes 131072 | tf_op jit(solution)/shard_map/all_to_all | solution.py:12

commit v4 on v3

v4 whole, which is shorter than its diff:
```python
import jax
import jax.numpy as jnp
from jax import lax
from jax.sharding import PartitionSpec as P

TAU = 0.5
PENALTY = 0.1
ORDER = (16, 4, 8, 2)
BF = jnp.bfloat16


def member_order():
    order = [0]
    for bit in (1,) + ORDER:
        order = order + [n + bit for n in order]
    return order


def exchange(x):
    return lax.all_to_all(x, "row", 0, 0, tiled=True, axis_index_groups=[member_order()])


def pick(index, size):
    return (index.reshape(-1, 1) == jnp.arange(size, dtype=index.dtype)[None, :]).astype(BF)


def halves(v):
    high = lax.reduce_precision(v, 8, 7)
    return high.astype(BF), (v - high).astype(BF)


def on_device(samples, blocks, diagonal, block_rows, block_cols):
    nrow, ncol = lax.axis_size("row"), lax.axis_size("col")
    ratio = nrow // ncol
    width = samples.shape[1]
    b = blocks.shape[-1]
    cb = width // b
    rb = cb // ratio
    own = cb // nrow
    rows, cols, local = block_rows[0, 0], block_cols[0, 0], blocks[0, 0]
    k = rows.shape[0]
    x = samples.reshape(cb, b)
    diag = diagonal.reshape(cb, b)

    order = member_order()
    groups = [[(ratio * g + n % ratio) * ncol + n // ratio for n in range(nrow)] for g in range(ncol)]
    perm = [(n * ncol + g, groups[g][n]) for n in range(nrow) for g in range(ncol)]

    def turned(v):
        return lax.ppermute(v, ("row", "col"), perm)

    def in_group(v):
        return lax.all_to_all(v, ("row", "col"), 0, 0, tiled=True, axis_index_groups=[[group[n] for n in order] for group in groups])

    me = lax.axis_index("col") * ratio + lax.axis_index("row") % ratio

    def swap(v, bit):
        pairs = [(group[n], group[n ^ bit]) for group in groups for n in range(nrow)]
        return lax.ppermute(v, ("row", "col"), pairs)

    def double(v, bit):
        upper = (me & bit) == bit
        other = swap(v, bit)
        return jnp.concatenate([jnp.where(upper, other, v), jnp.where(upper, v, other)])

    def named_rows(v):
        return jnp.einsum("sb,nbl->nsl", pick_r, v, preferred_element_type=jnp.float32).astype(BF)

    parts = turned(x).reshape(1, ratio, rb, b)
    got = in_group(jnp.broadcast_to(parts, (ncol, ratio, rb, b)).reshape(nrow, rb, b))
    pick_r = pick(rows, rb)
    xr = named_rows(got)

    prod = jnp.einsum("nki,kij->nkj", xr, local, preferred_element_type=jnp.float32).astype(BF)
    tail = jnp.zeros((8, b), BF).at[0, :k].set(cols.astype(BF))
    got = exchange(jnp.concatenate([prod, jnp.broadcast_to(tail[None], (nrow, 8, b))], axis=1))
    named = jnp.pad(got[:, k, :k].astype(jnp.int32), ((0, 0), (0, 8)), constant_values=-1)
    pick_c = pick(named, cb)
    total = lax.dot_general(
        pick_c, got.reshape(nrow * (k + 8), b), (((0,), (0,)), ((), ())), preferred_element_type=jnp.float32
    )
    xf = x.astype(jnp.float32)
    mixed = (total + xf * diag).astype(BF)

    quad = (xf * mixed.astype(jnp.float32)).reshape(nrow, own, b)
    out = jnp.dot(pick_c, jnp.concatenate([mixed, x], axis=1), preferred_element_type=jnp.float32).astype(BF)
    out = out.reshape(nrow, k + 8, 2 * b)[:, :k]
    out = jnp.concatenate([out[..., :b], *halves(quad), out[..., b:]], axis=1)
    out, mixed = lax.optimization_barrier((out, mixed))
    got = exchange(out)

    mt = turned(mixed)
    upper = (me & 1) == 1
    low, high = mt[:rb], mt[rb:]
    mine, other = jnp.where(upper, high, low), swap(jnp.where(upper, low, high), 1)
    held = jnp.where(upper, jnp.stack([other, mine]), jnp.stack([mine, other]))
    for bit in ORDER[:-1]:
        held = double(held, bit)
    held, got = lax.optimization_barrier((held, got))
    other = swap(held, ORDER[-1])
    upper = (me & ORDER[-1]) == ORDER[-1]
    held, other = named_rows(held), named_rows(other)
    wr = jnp.where(upper, jnp.concatenate([other, held]), jnp.concatenate([held, other]))

    wc, xc = got[:, :k], got[:, k + 2 * own :]
    quad = jnp.sum(got[:, k : k + 2 * own].astype(jnp.float32), axis=0)
    quad = quad[:own] + quad[own:]
    place = jnp.array([order.index(n) for n in range(nrow)], jnp.int32)[lax.axis_index("row")]
    mine = lax.dynamic_slice_in_dim(diag, place * own, own, 0)
    diag_grad = -1.0 / mine + quad / nrow
    mine = mine - TAU * diag_grad

    new_diagonal = exchange(jnp.broadcast_to(mine[None], (nrow, own, b))).reshape(width)

    left = jnp.concatenate([xr, wr], axis=0)
    right = jnp.concatenate([wc, xc], axis=0)
    both = jnp.einsum("nki,nkj->kij", left, right, preferred_element_type=jnp.float32)
    grad = both * (0.5 / nrow)
    moved = local.astype(jnp.float32) - TAU * grad
    shrunk = jnp.sign(moved) * jnp.maximum(jnp.abs(moved) - TAU * PENALTY, 0.0)
    return shrunk.astype(BF)[None, None], new_diagonal


def solution(mesh):
    in_specs = (
        P("row", "col"),
        P("row", "col", None, None, None),
        P("col"),
        P("row", "col", None),
        P("row", "col", None),
    )
    out_specs = (P("row", "col", None, None, None), P("col"))
    return jax.shard_map(
        on_device, mesh=mesh, in_specs=in_specs, out_specs=out_specs, check_vma=False
    )
```

time: 158 us -> 172 us (1.089)
  starting transfers between devices: 46.1 us -> 89.3 us
  waiting for transfers between devices: 62.3 us -> 35 us
  blocking collectives: 38.1 us -> 35.2 us
    ppermute x0 -> x5, starting transfers between devices: none -> 48.7 us  [swap(): return lax.ppermute(v, ('row', 'col'), pairs)]
    all_to_all x4 -> x3, waiting for transfers between devices: 62.3 us -> 21.4 us  [the longest x1 11 us: in_group(): lax.all_to_all(v, ('row', 'col'), 0, 0, tiled=True, axis_index_groups=[[g...]
    ppermute x0 -> x5, waiting for transfers between devices: none -> 13.6 us  [swap(): return lax.ppermute(v, ('row', 'col'), pairs)]
    all_to_all x4 -> x3, starting transfers between devices: 44.8 us -> 39.3 us  [the longest x1 24.8 us: in_group(): lax.all_to_all(v, ('row', 'col'), 0, 0, tiled=True, axis_index_groups=[[g...]
    all_to_all x1, blocking collectives: 38.1 us -> 35.2 us  [exchange(): lax.all_to_all(x, 'row', 0, 0, tiled=True, axis_index_groups=[member_orde...]
  transfers between devices with their start and end apart: 6 -> 10, of which waited for: 4 -> 6; matrix products, arithmetic and copies ran while one was open for 2% -> 1% of each run, Pallas kernels for 0% -> 0%
where the time goes in v4:
time: 172 us; the launch traced here: 171 us
  starting transfers between devices  89.3 us (52%)
  blocking collectives  35.2 us (20%)
  waiting for transfers between devices  35 us (20%)
  matrix products  4.3 us (2%)
  local copies, waits for them, and re-layouts  3.28 us (2%)
  other arithmetic  2.24 us (1%)
    ppermute x5, starting transfers between devices, swap(): return lax.ppermute(v, ('row', 'col'), pairs)  48.7 us
    all_to_all x1, blocking collectives, exchange(): lax.all_to_all(x, 'row', 0, 0, tiled=True, axis_index_groups=[member_orde...  35.2 us
    all_to_all x1, starting transfers between devices, in_group(): lax.all_to_all(v, ('row', 'col'), 0, 0, tiled=True, axis_index_groups=[[g...  24.8 us
    all_to_all x2, starting transfers between devices, exchange(): lax.all_to_all(x, 'row', 0, 0, tiled=True, axis_index_groups=[member_orde...  14.5 us
    ppermute x5, waiting for transfers between devices, swap(): return lax.ppermute(v, ('row', 'col'), pairs)  13.6 us
    all_to_all x1, waiting for transfers between devices, in_group(): lax.all_to_all(v, ('row', 'col'), 0, 0, tiled=True, axis_index_groups=[[g...  11 us
    all_to_all x2, waiting for transfers between devices, exchange(): lax.all_to_all(x, 'row', 0, 0, tiled=True, axis_index_groups=[member_orde...  10.4 us
  transfers between devices with their start and end apart: 10, of which 6 were waited for; matrix products, arithmetic and copies ran while one was open for 1% of the time, Pallas kernels for 0%

profile of v4, /device:TPU:2, one launch (start us, length us, event | category | flops | bytes accessed | tf_op | source)
XLA Modules:
  0.0 170.9 jit_solution(8028724936027232477)
XLA Ops:
  0.6 0.0 copy-start.3
  0.6 0.0 copy-start.1
  0.6 1.0 reduce.2
  1.7 0.7 collective-permute-start
  2.3 0.0 collective-permute-done
  2.4 0.9 broadcast_in_dim.11
  3.3 0.0 copy-start
  3.3 24.8 %all-to-all-start = ((bf16[32,64,128]{2,1,0:T(8,128)(2,1)}), bf16[32,64,128]{2,1,0:T(8,128)(2,1)S(1)}, u32[]{:S(2)}, u32[]{:S(2)}) async-start(bf16[32,64,128]{2,1,0:T(8,128)(2,1)} %bitcast.4), calls=%async_computation | async-start | bytes 1048576 | tf_op jit(solution)/shard_map/all_to_all | solution.py:53
  28.0 0.0 copy-done.3
  28.1 11.0 %all-to-all-done = bf16[32,64,128]{2,1,0:T(8,128)(2,1)S(1)} async-done(((bf16[32,64,128]{2,1,0:T(8,128)(2,1)}), bf16[32,64,128]{2,1,0:T(8,128)(2,1)S(1)}, u32[]{:S(2)}, u32[]{:S(2)}) %all-to-all-start) | async-done | bytes 524320 | tf_op jit(solution)/shard_map/all_to_all | solution.py:53
  39.1 0.0 copy-done.1
  39.1 0.3 fusion.1
  39.3 0.0 copy-done
  39.3 0.4 fusion.2
  39.8 0.0 copy-start.2
  39.8 0.1 copy.27
  39.9 35.2 %all_to_all.20 = bf16[32,40,128]{2,1,0:T(8,128)(2,1)S(1)} all-to-all(bf16[32,40,128]{2,1,0:T(8,128)(2,1)S(1)} %copy.27), channel_id=1, replica_groups={{0,16,256,272,64,80,320,336,128,144,384,400,192,208,448,464,32,48,288,3..., dimensions={0} | all-to-all | bytes 655360 | tf_op jit(solution)/shard_map/all_to_all | solution.py:20
  75.2 0.1 reshape.84
  75.2 0.0 copy-done.2
  75.3 0.5 convert_multiply_fusion
  75.8 0.4 convolution_convert_fusion
  76.2 0.1 fusion.27
  76.3 0.9 pad_maximum_fusion
  77.2 0.0 copy-start.4
  77.2 6.7 %all-to-all-start.2 = ((bf16[32,72,128]{2,1,0:T(8,128)(2,1)}), bf16[32,72,128]{2,1,0:T(8,128)(2,1)S(1)}, u32[]{:S(2)}, u32[]{:S(2)}) async-start(bf16[32,72,128]{2,1,0:T(8,128)(2,1)} %pad_maximum_fusion), calls=%async_computation.2 | async-start | bytes 1179648 | tf_op jit(solution)/shard_map/all_to_all | solution.py:20
  84.0 0.7 collective-permute-start.1
  84.7 0.0 collective-permute-done.1
  84.7 2.1 %collective-permute-start.2 = (bf16[64,128]{1,0:T(8,128)(2,1)S(1)}, bf16[64,128]{1,0:T(8,128)(2,1)S(1)}, u32[]{:S(2)}, u32[]{:S(2)}) collective-permute-start(bf16[64,128]{1,0:T(8,128)(2,1)S(1)} %get-tuple-element.34), channel_id=1, source_target_pairs={{0,16},{16,0},{1,17},{17,1},{2,18},{18,2},{3,19},{19,3},{4,20},{20... | collective-permute-start | bytes 49160 | tf_op jit(solution)/shard_map/ppermute | solution.py:59
  86.8 3.5 %collective-permute-done.2 = bf16[64,128]{1,0:T(8,128)(2,1)S(1)} collective-permute-done((bf16[64,128]{1,0:T(8,128)(2,1)S(1)}, bf16[64,128]{1,0:T(8,128)(2,1)S(1)}, u32[]{:S(2)}, u32[]{:S(2)}) %collective-permute-start.2) | collective-permute-done | bytes 16416 | tf_op jit(solution)/shard_map/ppermute | solution.py:59
  90.3 39.7 %collective-permute-start.3 = (bf16[2,64,128]{2,1,0:T(8,128)(2,1)S(1)}, bf16[2,64,128]{2,1,0:T(8,128)(2,1)S(1)}, u32[]{:S(2)}, u32[]{:S(2)}) collective-permute-start(bf16[2,64,128]{2,1,0:T(8,128)(2,1)S(1)} %maximum_select_fusion.1), channel_id=1, source_target_pairs={{0,8},{16,24},{1,9},{17,25},{2,10},{18,26},{3,11},{19,27},{4,12},{... | collective-permute-start | bytes 98312 | tf_op jit(solution)/shard_map/ppermute | solution.py:59
  130.0 1.9 %collective-permute-done.3 = bf16[2,64,128]{2,1,0:T(8,128)(2,1)S(1)} collective-permute-done((bf16[2,64,128]{2,1,0:T(8,128)(2,1)S(1)}, bf16[2,64,128]{2,1,0:T(8,128)(2,1)S(1)}, u32[]{:S(2)}, u32[]{:S(2)}) %collective-permute-start.3) | collective-permute-done | bytes 32800 | tf_op jit(solution)/shard_map/ppermute | solution.py:59
  131.9 3.1 %collective-permute-start.4 = (bf16[4,64,128]{2,1,0:T(8,128)(2,1)S(1)}, bf16[4,64,128]{2,1,0:T(8,128)(2,1)S(1)}, u32[]{:S(2)}, u32[]{:S(2)}) collective-permute-start(bf16[4,64,128]{2,1,0:T(8,128)(2,1)S(1)} %pad_maximum_fusion.5), channel_id=1, source_target_pairs={{0,2},{16,18},{1,3},{17,19},{2,0},{18,16},{3,1},{19,17},{4,6},{20,... | collective-permute-start | bytes 196616 | tf_op jit(solution)/shard_map/ppermute | solution.py:59
  135.0 4.6 %collective-permute-done.4 = bf16[4,64,128]{2,1,0:T(8,128)(2,1)S(1)} collective-permute-done((bf16[4,64,128]{2,1,0:T(8,128)(2,1)S(1)}, bf16[4,64,128]{2,1,0:T(8,128)(2,1)S(1)}, u32[]{:S(2)}, u32[]{:S(2)}) %collective-permute-start.4) | collective-permute-done | bytes 65568 | tf_op jit(solution)/shard_map/ppermute | solution.py:59
  139.6 1.9 %collective-permute-start.5 = (bf16[8,64,128]{2,1,0:T(8,128)(2,1)S(1)}, bf16[8,64,128]{2,1,0:T(8,128)(2,1)S(1)}, u32[]{:S(2)}, u32[]{:S(2)}) collective-permute-start(bf16[8,64,128]{2,1,0:T(8,128)(2,1)S(1)} %pad_maximum_fusion.4), channel_id=1, source_target_pairs={{0,4},{16,20},{1,5},{17,21},{2,6},{18,22},{3,7},{19,23},{4,0},{20,... | collective-permute-start | bytes 393224 | tf_op jit(solution)/shard_map/ppermute | solution.py:59
  141.5 0.0 copy-done.4
  141.5 0.6 dynamic_slice.6
  142.8 3.7 %collective-permute-done.5 = bf16[8,64,128]{2,1,0:T(8,128)(2,1)S(1)} collective-permute-done((bf16[8,64,128]{2,1,0:T(8,128)(2,1)S(1)}, bf16[8,64,128]{2,1,0:T(8,128)(2,1)S(1)}, u32[]{:S(2)}, u32[]{:S(2)}) %collective-permute-start.5) | collective-permute-done | bytes 131104 | tf_op jit(solution)/shard_map/ppermute | solution.py:59
  146.5 0.0 all-to-all-done.2
  146.6 0.6 broadcast_in_dim.14
  147.2 7.8 %all-to-all-start.3 = ((f32[32,4,128]{2,1,0:T(4,128)}), f32[32,4,128]{2,1,0:T(4,128)S(1)}, u32[]{:S(2)}, u32[]{:S(2)}) async-start(f32[32,4,128]{2,1,0:T(4,128)} %broadcast_in_dim.14), calls=%async_computation.3 | async-start | bytes 131072 | tf_op jit(solution)/shard_map/all_to_all | solution.py:20
  155.0 1.9 %collective-permute-start.6 = (bf16[16,64,128]{2,1,0:T(8,128)(2,1)S(1)}, bf16[16,64,128]{2,1,0:T(8,128)(2,1)S(1)}, u32[]{:S(2)}, u32[]{:S(2)}) collective-permute-start(bf16[16,64,128]{2,1,0:T(8,128)(2,1)S(1)} %pad_maximum_fusion.3), channel_id=1, source_target_pairs={{0,1},{16,17},{1,0},{17,16},{2,3},{18,19},{3,2},{19,18},{4,5},{20,... | collective-permute-start | bytes 786440 | tf_op jit(solution)/shard_map/ppermute | solution.py:59
  156.9 0.2 fusion.4
  157.2 0.1 copy.29
  157.3 10.4 %all-to-all-done.3 = f32[32,4,128]{2,1,0:T(4,128)S(1)} async-done(((f32[32,4,128]{2,1,0:T(4,128)}), f32[32,4,128]{2,1,0:T(4,128)S(1)}, u32[]{:S(2)}, u32[]{:S(2)}) %all-to-all-start.3) | async-done | bytes 65568 | tf_op jit(solution)/shard_map/all_to_all | solution.py:20
  167.7 0.0 collective-permute-done.6
  167.7 0.2 fusion.3
  168.0 2.3 %fusion = bf16[1,1,32,128,128]{4,3,2,1,0:T(8,128)(2,1)} fusion(bf16[1,1,32,128,128]{4,3,2,1,0:T(8,128)(2,1)S(1)} %copy-done, bf16[32,32,128]{2,0,1:T(8,128)(2,1)S(1)} %get-tuple-element.25, bf16[32,32,128]{2,0,1:T(8,128)(2,1)S(1)} %get-tuple-element.24, bf16[64,32,128]{2,1,0:T(8,128)(2,1)S(1)} %pad_maximum_fusion.1), kind=kOutput, calls=%fused_computation.2 | convolution fusion | flops 72876032 | bytes 3145728 | tf_op jit(solution)/shard_map/nki,nkj->kij/dot_general | solution.py:117
  170.3 0.6 copy.40
  (21 shorter events, 0.4 us)
Async XLA Ops:
  0.6 27.4 %copy-start.3 = (s32[1,1,32]{2,1,0:T(1,128)S(1)}, s32[1,1,32]{2,1,0:T(1,128)}, u32[]{:S(2)}) copy-start(s32[1,1,32]{2,1,0:T(1,128)} %param.12) | copy-start | bytes 388
  0.6 38.4 %copy-start.1 = (s32[1,1,32]{2,1,0:T(1,128)S(1)}, s32[1,1,32]{2,1,0:T(1,128)}, u32[]{:S(2)}) copy-start(s32[1,1,32]{2,1,0:T(1,128)} %param.11) | copy-start | bytes 388
  1.7 0.7 collective-permute-start
  3.3 36.1 %copy-start = (bf16[1,1,32,128,128]{4,3,2,1,0:T(8,128)(2,1)S(1)}, bf16[1,1,32,128,128]{4,3,2,1,0:T(8,128)(2,1)}, u32[]{:S(2)}) copy-start(bf16[1,1,32,128,128]{4,3,2,1,0:T(8,128)(2,1)} %param.9) | copy-start | bytes 3145732
  3.3 35.8 %all-to-all-start = ((bf16[32,64,128]{2,1,0:T(8,128)(2,1)}), bf16[32,64,128]{2,1,0:T(8,128)(2,1)S(1)}, u32[]{:S(2)}, u32[]{:S(2)}) async-start(bf16[32,64,128]{2,1,0:T(8,128)(2,1)} %bitcast.4), calls=%async_computation | async-start | bytes 1048576 | tf_op jit(solution)/shard_map/all_to_all | solution.py:53
  39.8 35.5 %copy-start.2 = (f32[16384]{0:T(1024)S(1)}, f32[16384]{0:T(1024)}, u32[]{:S(2)}) copy-start(f32[16384]{0:T(1024)} %param.10) | copy-start | bytes 196612
  77.2 64.3 %copy-start.4 = (s32[32]{0:T(128)S(1)}, s32[32]{0:T(128)}, u32[]{:S(2)}) copy-start(s32[32]{0:T(128)} %constant.87.clone) | copy-start | bytes 388
  77.2 69.3 %all-to-all-start.2 = ((bf16[32,72,128]{2,1,0:T(8,128)(2,1)}), bf16[32,72,128]{2,1,0:T(8,128)(2,1)S(1)}, u32[]{:S(2)}, u32[]{:S(2)}) async-start(bf16[32,72,128]{2,1,0:T(8,128)(2,1)} %pad_maximum_fusion), calls=%async_computation.2 | async-start | bytes 1179648 | tf_op jit(solution)/shard_map/all_to_all | solution.py:20
  84.0 0.7 collective-permute-start.1
  84.7 5.6 %collective-permute-start.2 = (bf16[64,128]{1,0:T(8,128)(2,1)S(1)}, bf16[64,128]{1,0:T(8,128)(2,1)S(1)}, u32[]{:S(2)}, u32[]{:S(2)}) collective-permute-start(bf16[64,128]{1,0:T(8,128)(2,1)S(1)} %get-tuple-element.34), channel_id=1, source_target_pairs={{0,16},{16,0},{1,17},{17,1},{2,18},{18,2},{3,19},{19,3},{4,20},{20... | collective-permute-start | bytes 49160 | tf_op jit(solution)/shard_map/ppermute | solution.py:59
  90.3 41.5 %collective-permute-start.3 = (bf16[2,64,128]{2,1,0:T(8,128)(2,1)S(1)}, bf16[2,64,128]{2,1,0:T(8,128)(2,1)S(1)}, u32[]{:S(2)}, u32[]{:S(2)}) collective-permute-start(bf16[2,64,128]{2,1,0:T(8,128)(2,1)S(1)} %maximum_select_fusion.1), channel_id=1, source_target_pairs={{0,8},{16,24},{1,9},{17,25},{2,10},{18,26},{3,11},{19,27},{4,12},{... | collective-permute-start | bytes 98312 | tf_op jit(solution)/shard_map/ppermute | solution.py:59
  131.9 7.7 %collective-permute-start.4 = (bf16[4,64,128]{2,1,0:T(8,128)(2,1)S(1)}, bf16[4,64,128]{2,1,0:T(8,128)(2,1)S(1)}, u32[]{:S(2)}, u32[]{:S(2)}) collective-permute-start(bf16[4,64,128]{2,1,0:T(8,128)(2,1)S(1)} %pad_maximum_fusion.5), channel_id=1, source_target_pairs={{0,2},{16,18},{1,3},{17,19},{2,0},{18,16},{3,1},{19,17},{4,6},{20,... | collective-permute-start | bytes 196616 | tf_op jit(solution)/shard_map/ppermute | solution.py:59
  139.6 6.9 %collective-permute-start.5 = (bf16[8,64,128]{2,1,0:T(8,128)(2,1)S(1)}, bf16[8,64,128]{2,1,0:T(8,128)(2,1)S(1)}, u32[]{:S(2)}, u32[]{:S(2)}) collective-permute-start(bf16[8,64,128]{2,1,0:T(8,128)(2,1)S(1)} %pad_maximum_fusion.4), channel_id=1, source_target_pairs={{0,4},{16,20},{1,5},{17,21},{2,6},{18,22},{3,7},{19,23},{4,0},{20,... | collective-permute-start | bytes 393224 | tf_op jit(solution)/shard_map/ppermute | solution.py:59
  147.2 20.4 %all-to-all-start.3 = ((f32[32,4,128]{2,1,0:T(4,128)}), f32[32,4,128]{2,1,0:T(4,128)S(1)}, u32[]{:S(2)}, u32[]{:S(2)}) async-start(f32[32,4,128]{2,1,0:T(4,128)} %broadcast_in_dim.14), calls=%async_computation.3 | async-start | bytes 131072 | tf_op jit(solution)/shard_map/all_to_all | solution.py:20
  155.0 12.7 %collective-permute-start.6 = (bf16[16,64,128]{2,1,0:T(8,128)(2,1)S(1)}, bf16[16,64,128]{2,1,0:T(8,128)(2,1)S(1)}, u32[]{:S(2)}, u32[]{:S(2)}) collective-permute-start(bf16[16,64,128]{2,1,0:T(8,128)(2,1)S(1)} %pad_maximum_fusion.3), channel_id=1, source_target_pairs={{0,1},{16,17},{1,0},{17,16},{2,3},{18,19},{3,2},{19,18},{4,5},{20,... | collective-permute-start | bytes 786440 | tf_op jit(solution)/shard_map/ppermute | solution.py:59

commit v5 on v4

--- a/solution.py
+++ b/solution.py
@@ -5,15 +5,15 @@
 
 TAU = 0.5
 PENALTY = 0.1
-ORDER = (16, 4, 8, 2)
+COL_BITS = (8, 2, 4, 1)
 BF = jnp.bfloat16
 
 
 def member_order():
     order = [0]
-    for bit in (1,) + ORDER:
-        order = order + [n + bit for n in order]
-    return order
+    for bit in COL_BITS:
+        order = order + [c + bit for c in order]
+    return [2 * c + e for c in order for e in range(2)]
 
 
 def exchange(x):
@@ -52,30 +52,24 @@
     def in_group(v):
         return lax.all_to_all(v, ("row", "col"), 0, 0, tiled=True, axis_index_groups=[[group[n] for n in order] for group in groups])
 
-    me = lax.axis_index("col") * ratio + lax.axis_index("row") % ratio
-
-    def swap(v, bit):
-        pairs = [(group[n], group[n ^ bit]) for group in groups for n in range(nrow)]
-        return lax.ppermute(v, ("row", "col"), pairs)
-
-    def double(v, bit):
-        upper = (me & bit) == bit
-        other = swap(v, bit)
-        return jnp.concatenate([jnp.where(upper, other, v), jnp.where(upper, v, other)])
-
-    def named_rows(v):
-        return jnp.einsum("sb,nbl->nsl", pick_r, v, preferred_element_type=jnp.float32).astype(BF)
+    def gathered(v):
+        v = v[None]
+        for bit in COL_BITS:
+            other = lax.ppermute(v, "col", [(c, c ^ bit) for c in range(ncol)])
+            upper = (lax.axis_index("col") & bit) == bit
+            v = jnp.concatenate([jnp.where(upper, other, v), jnp.where(upper, v, other)])
+        return v
 
     parts = turned(x).reshape(1, ratio, rb, b)
     got = in_group(jnp.broadcast_to(parts, (ncol, ratio, rb, b)).reshape(nrow, rb, b))
-    pick_r = pick(rows, rb)
-    xr = named_rows(got)
+    xr = jnp.einsum("sb,nbl->nsl", pick(rows, rb), got, preferred_element_type=jnp.float32).astype(BF)
 
     prod = jnp.einsum("nki,kij->nkj", xr, local, preferred_element_type=jnp.float32).astype(BF)
-    tail = jnp.zeros((8, b), BF).at[0, :k].set(cols.astype(BF))
+    tail = jnp.zeros((8, b), BF).at[0, :k].set(cols.astype(BF)).at[1, :k].set(rows.astype(BF))
     got = exchange(jnp.concatenate([prod, jnp.broadcast_to(tail[None], (nrow, 8, b))], axis=1))
     named = jnp.pad(got[:, k, :k].astype(jnp.int32), ((0, 0), (0, 8)), constant_values=-1)
     pick_c = pick(named, cb)
+    pick_r = pick(got[:, k + 1, :k].astype(jnp.int32), rb).reshape(nrow, k, rb)
     total = lax.dot_general(
         pick_c, got.reshape(nrow * (k + 8), b), (((0,), (0,)), ((), ())), preferred_element_type=jnp.float32
     )
@@ -89,18 +83,9 @@
     out, mixed = lax.optimization_barrier((out, mixed))
     got = exchange(out)
 
-    mt = turned(mixed)
-    upper = (me & 1) == 1
-    low, high = mt[:rb], mt[rb:]
-    mine, other = jnp.where(upper, high, low), swap(jnp.where(upper, low, high), 1)
-    held = jnp.where(upper, jnp.stack([other, mine]), jnp.stack([mine, other]))
-    for bit in ORDER[:-1]:
-        held = double(held, bit)
-    held, got = lax.optimization_barrier((held, got))
-    other = swap(held, ORDER[-1])
-    upper = (me & ORDER[-1]) == ORDER[-1]
-    held, other = named_rows(held), named_rows(other)
-    wr = jnp.where(upper, jnp.concatenate([other, held]), jnp.concatenate([held, other]))
+    held = gathered(mixed).reshape(nrow, rb, b)
+    out = jnp.einsum("tsb,tbl->tsl", pick_r, held, preferred_element_type=jnp.float32).astype(BF)
+    out, got = lax.optimization_barrier((out, got))
 
     wc, xc = got[:, :k], got[:, k + 2 * own :]
     quad = jnp.sum(got[:, k : k + 2 * own].astype(jnp.float32), axis=0)
@@ -110,7 +95,10 @@
     diag_grad = -1.0 / mine + quad / nrow
     mine = mine - TAU * diag_grad
 
-    new_diagonal = exchange(jnp.broadcast_to(mine[None], (nrow, own, b))).reshape(width)
+    mine = jnp.concatenate(halves(mine))
+    got = exchange(jnp.concatenate([out, jnp.broadcast_to(mine[None], (nrow, 2 * own, b))], axis=1))
+    wr = got[:, :k]
+    new_diagonal = got[:, k : k + own].astype(jnp.float32) + got[:, k + own :].astype(jnp.float32)
 
     left = jnp.concatenate([xr, wr], axis=0)
     right = jnp.concatenate([wc, xc], axis=0)
@@ -118,7 +106,7 @@
     grad = both * (0.5 / nrow)
     moved = local.astype(jnp.float32) - TAU * grad
     shrunk = jnp.sign(moved) * jnp.maximum(jnp.abs(moved) - TAU * PENALTY, 0.0)
-    return shrunk.astype(BF)[None, None], new_diagonal
+    return shrunk.astype(BF)[None, None], new_diagonal.reshape(width)
 
 
 def solution(mesh):

time: 172 us -> 151 us (0.88)
  the two profiles are of different devices: /device:TPU:2 before, /device:TPU:32 now
where the time goes in v5:
time: 151 us
  waiting for transfers between devices  61.3 us (41%)
  starting transfers between devices  41.6 us (28%)
  blocking collectives  36.1 us (24%)
  matrix products  4.17 us (3%)
  other arithmetic  3.74 us (2%)
  local copies, waits for them, and re-layouts  2.17 us (1%)
  between operations  1.65 us (1%)
    all_to_all x1, blocking collectives, exchange(): lax.all_to_all(x, 'row', 0, 0, tiled=True, axis_index_groups=[member_orde...  36.1 us
    all_to_all x2, waiting for transfers between devices, exchange(): lax.all_to_all(x, 'row', 0, 0, tiled=True, axis_index_groups=[member_orde...  32.4 us
    all_to_all x1, starting transfers between devices, in_group(): lax.all_to_all(v, ('row', 'col'), 0, 0, tiled=True, axis_index_groups=[[g...  20.1 us
    ppermute x4, waiting for transfers between devices, gathered(): other = lax.ppermute(v, 'col', [(c, c ^ bit) for c in range(ncol)])  13.3 us
    all_to_all x1, waiting for transfers between devices, in_group(): lax.all_to_all(v, ('row', 'col'), 0, 0, tiled=True, axis_index_groups=[[g...  12.2 us
    ppermute x4, starting transfers between devices, gathered(): other = lax.ppermute(v, 'col', [(c, c ^ bit) for c in range(ncol)])  10.8 us
    all_to_all x2, starting transfers between devices, exchange(): lax.all_to_all(x, 'row', 0, 0, tiled=True, axis_index_groups=[member_orde...  8.72 us
    ppermute x1, waiting for transfers between devices, turned(): return lax.ppermute(v, ('row', 'col'), perm)  3.31 us
  transfers between devices with their start and end apart: 8, of which 8 were waited for; matrix products, arithmetic and copies ran while one was open for 1% of the time, Pallas kernels for 0%

profile of v5, /device:TPU:32, one launch (start us, length us, event | category | flops | bytes accessed | tf_op | source)
XLA Modules:
  0.0 150.7 jit_solution(10898873676995534714)
XLA Ops:
  0.6 0.0 copy-start.3
  0.6 0.0 copy-start.1
  0.6 1.0 reduce.4
  1.7 1.9 %collective-permute-start = (bf16[128,128]{1,0:T(8,128)(2,1)S(1)}, bf16[128,128]{1,0:T(8,128)(2,1)S(1)}, u32[]{:S(2)}, u32[]{:S(2)}) collective-permute-start(bf16[128,128]{1,0:T(8,128)(2,1)S(1)} %bitcast.44), channel_id=1, source_target_pairs={{0,0},{1,32},{2,64},{3,96},{4,128},{5,160},{6,192},{7,224},{8,256}... | collective-permute-start | bytes 98312 | tf_op jit(solution)/shard_map/ppermute | solution.py:50
  3.6 3.3 %collective-permute-done = bf16[128,128]{1,0:T(8,128)(2,1)S(1)} collective-permute-done((bf16[128,128]{1,0:T(8,128)(2,1)S(1)}, bf16[128,128]{1,0:T(8,128)(2,1)S(1)}, u32[]{:S(2)}, u32[]{:S(2)}) %collective-permute-start) | collective-permute-done | bytes 32800 | tf_op jit(solution)/shard_map/ppermute | solution.py:50
  6.9 0.9 broadcast_in_dim.13
  7.8 0.0 copy-start
  7.8 20.1 %all-to-all-start = ((bf16[32,64,128]{2,1,0:T(8,128)(2,1)}), bf16[32,64,128]{2,1,0:T(8,128)(2,1)S(1)}, u32[]{:S(2)}, u32[]{:S(2)}) async-start(bf16[32,64,128]{2,1,0:T(8,128)(2,1)} %bitcast.4), calls=%async_computation | async-start | bytes 1048576 | tf_op jit(solution)/shard_map/all_to_all | solution.py:53
  27.9 0.0 copy-done.3
  28.0 0.0 copy-done.1
  28.0 0.2 scatter.9
  28.2 12.2 %all-to-all-done = bf16[32,64,128]{2,1,0:T(8,128)(2,1)S(1)} async-done(((bf16[32,64,128]{2,1,0:T(8,128)(2,1)}), bf16[32,64,128]{2,1,0:T(8,128)(2,1)S(1)}, u32[]{:S(2)}, u32[]{:S(2)}) %all-to-all-start) | async-done | bytes 524320 | tf_op jit(solution)/shard_map/all_to_all | solution.py:53
  40.4 0.3 fusion.1
  40.6 0.0 copy-done
  40.6 0.4 fusion.2
  41.1 0.0 copy-start.2
  41.1 0.1 copy.27
  41.2 36.1 %all_to_all.20 = bf16[32,40,128]{2,1,0:T(8,128)(2,1)S(1)} all-to-all(bf16[32,40,128]{2,1,0:T(8,128)(2,1)S(1)} %copy.27), channel_id=1, replica_groups={{0,16,256,272,64,80,320,336,128,144,384,400,192,208,448,464,32,48,288,3..., dimensions={0} | all-to-all | bytes 655360 | tf_op jit(solution)/shard_map/all_to_all | solution.py:20
  77.4 0.1 reshape.141
  77.5 0.0 copy-done.2
  77.5 0.5 convert_multiply_fusion
  78.1 0.4 convolution_convert_fusion
  78.5 0.1 fusion.23
  78.6 0.9 pad_maximum_fusion
  79.5 4.0 %all-to-all-start.2 = ((bf16[32,72,128]{2,1,0:T(8,128)(2,1)}), bf16[32,72,128]{2,1,0:T(8,128)(2,1)S(1)}, u32[]{:S(2)}, u32[]{:S(2)}) async-start(bf16[32,72,128]{2,1,0:T(8,128)(2,1)} %pad_maximum_fusion), calls=%async_computation.2 | async-start | bytes 1179648 | tf_op jit(solution)/shard_map/all_to_all | solution.py:20
  83.4 0.0 copy-start.4
  83.5 2.8 %collective-permute-start.1 = (bf16[1,128,128]{2,1,0:T(8,128)(2,1)S(1)}, bf16[1,128,128]{2,1,0:T(8,128)(2,1)S(1)}, u32[]{:S(2)}, u32[]{:S(2)}) collective-permute-start(bf16[1,128,128]{2,1,0:T(8,128)(2,1)S(1)} %bitcast.46), channel_id=1, source_target_pairs={{0,8},{1,9},{2,10},{3,11},{4,12},{5,13},{6,14},{7,15},{8,0},{9,1},... | collective-permute-start | bytes 98312 | tf_op jit(solution)/shard_map/ppermute | solution.py:58
  86.2 4.5 %collective-permute-done.1 = bf16[1,128,128]{2,1,0:T(8,128)(2,1)S(1)} collective-permute-done((bf16[1,128,128]{2,1,0:T(8,128)(2,1)S(1)}, bf16[1,128,128]{2,1,0:T(8,128)(2,1)S(1)}, u32[]{:S(2)}, u32[]{:S(2)}) %collective-permute-start.1) | collective-permute-done | bytes 32800 | tf_op jit(solution)/shard_map/ppermute | solution.py:58
  90.8 3.6 %collective-permute-start.2 = (bf16[2,128,128]{2,1,0:T(8,128)(2,1)S(1)}, bf16[2,128,128]{2,1,0:T(8,128)(2,1)S(1)}, u32[]{:S(2)}, u32[]{:S(2)}) collective-permute-start(bf16[2,128,128]{2,1,0:T(8,128)(2,1)S(1)} %pad_maximum_fusion.7), channel_id=1, source_target_pairs={{0,2},{1,3},{2,0},{3,1},{4,6},{5,7},{6,4},{7,5},{8,10},{9,11},{10,... | collective-permute-start | bytes 196616 | tf_op jit(solution)/shard_map/ppermute | solution.py:58
  94.4 4.3 %collective-permute-done.2 = bf16[2,128,128]{2,1,0:T(8,128)(2,1)S(1)} collective-permute-done((bf16[2,128,128]{2,1,0:T(8,128)(2,1)S(1)}, bf16[2,128,128]{2,1,0:T(8,128)(2,1)S(1)}, u32[]{:S(2)}, u32[]{:S(2)}) %collective-permute-start.2) | collective-permute-done | bytes 65568 | tf_op jit(solution)/shard_map/ppermute | solution.py:58
  98.7 2.6 %collective-permute-start.3 = (bf16[4,128,128]{2,1,0:T(8,128)(2,1)S(1)}, bf16[4,128,128]{2,1,0:T(8,128)(2,1)S(1)}, u32[]{:S(2)}, u32[]{:S(2)}) collective-permute-start(bf16[4,128,128]{2,1,0:T(8,128)(2,1)S(1)} %pad_maximum_fusion.6), channel_id=1, source_target_pairs={{0,4},{1,5},{2,6},{3,7},{4,0},{5,1},{6,2},{7,3},{8,12},{9,13},{10,... | collective-permute-start | bytes 393224 | tf_op jit(solution)/shard_map/ppermute | solution.py:58
  101.3 4.3 %collective-permute-done.3 = bf16[4,128,128]{2,1,0:T(8,128)(2,1)S(1)} collective-permute-done((bf16[4,128,128]{2,1,0:T(8,128)(2,1)S(1)}, bf16[4,128,128]{2,1,0:T(8,128)(2,1)S(1)}, u32[]{:S(2)}, u32[]{:S(2)}) %collective-permute-start.3) | collective-permute-done | bytes 131104 | tf_op jit(solution)/shard_map/ppermute | solution.py:58
  105.6 1.9 %collective-permute-start.4 = (bf16[8,128,128]{2,1,0:T(8,128)(2,1)S(1)}, bf16[8,128,128]{2,1,0:T(8,128)(2,1)S(1)}, u32[]{:S(2)}, u32[]{:S(2)}) collective-permute-start(bf16[8,128,128]{2,1,0:T(8,128)(2,1)S(1)} %pad_maximum_fusion.5), channel_id=1, source_target_pairs={{0,1},{1,0},{2,3},{3,2},{4,5},{5,4},{6,7},{7,6},{8,9},{9,8},{10,11... | collective-permute-start | bytes 786440 | tf_op jit(solution)/shard_map/ppermute | solution.py:58
  107.6 0.0 copy-done.4
  107.6 0.6 dynamic_slice.6
  108.8 0.2 collective-permute-done.4
  109.2 0.3 convolution_convert_fusion.1
  109.5 8.2 %all-to-all-done.2 = bf16[32,72,128]{2,1,0:T(8,128)(2,1)S(1)} async-done(((bf16[32,72,128]{2,1,0:T(8,128)(2,1)}), bf16[32,72,128]{2,1,0:T(8,128)(2,1)S(1)}, u32[]{:S(2)}, u32[]{:S(2)}) %all-to-all-start.2) | async-done | bytes 589856 | tf_op jit(solution)/shard_map/all_to_all | solution.py:20
  117.8 0.8 pad_maximum_fusion.4
  118.6 4.8 %all-to-all-start.3 = ((bf16[32,40,128]{2,1,0:T(8,128)(2,1)}), bf16[32,40,128]{2,1,0:T(8,128)(2,1)S(1)}, u32[]{:S(2)}, u32[]{:S(2)}) async-start(bf16[32,40,128]{2,1,0:T(8,128)(2,1)} %pad_maximum_fusion.4), calls=%async_computation.3 | async-start | bytes 655360 | tf_op jit(solution)/shard_map/all_to_all | solution.py:20
  123.3 0.1 copy.29
  123.5 24.2 %all-to-all-done.3 = bf16[32,40,128]{2,1,0:T(8,128)(2,1)S(1)} async-done(((bf16[32,40,128]{2,1,0:T(8,128)(2,1)}), bf16[32,40,128]{2,1,0:T(8,128)(2,1)S(1)}, u32[]{:S(2)}, u32[]{:S(2)}) %all-to-all-start.3) | async-done | bytes 327712 | tf_op jit(solution)/shard_map/all_to_all | solution.py:20
  147.7 2.3 %fusion = bf16[1,1,32,128,128]{4,3,2,1,0:T(8,128)(2,1)} fusion(bf16[1,1,32,128,128]{4,3,2,1,0:T(8,128)(2,1)S(1)} %copy-done, bf16[32,32,128]{2,0,1:T(8,128)(2,1)S(1)} %get-tuple-element.39, bf16[32,32,128]{2,0,1:T(8,128)(2,1)S(1)} %get-tuple-element.38, bf16[64,32,128]{2,1,0:T(8,128)(2,1)S(1)} %pad_maximum_fusion.2), kind=kOutput, calls=%fused_computation.2 | convolution fusion | flops 72876032 | bytes 3145728 | tf_op jit(solution)/shard_map/nki,nkj->kij/dot_general | solution.py:105
  150.0 0.6 convert_add_fusion
  (25 shorter events, 0.5 us)
Async XLA Ops:
  0.6 27.3 %copy-start.3 = (s32[1,1,32]{2,1,0:T(1,128)S(1)}, s32[1,1,32]{2,1,0:T(1,128)}, u32[]{:S(2)}) copy-start(s32[1,1,32]{2,1,0:T(1,128)} %param.14) | copy-start | bytes 388
  0.6 27.3 %copy-start.1 = (s32[1,1,32]{2,1,0:T(1,128)S(1)}, s32[1,1,32]{2,1,0:T(1,128)}, u32[]{:S(2)}) copy-start(s32[1,1,32]{2,1,0:T(1,128)} %param.13) | copy-start | bytes 388
  1.7 5.2 %collective-permute-start = (bf16[128,128]{1,0:T(8,128)(2,1)S(1)}, bf16[128,128]{1,0:T(8,128)(2,1)S(1)}, u32[]{:S(2)}, u32[]{:S(2)}) collective-permute-start(bf16[128,128]{1,0:T(8,128)(2,1)S(1)} %bitcast.44), channel_id=1, source_target_pairs={{0,0},{1,32},{2,64},{3,96},{4,128},{5,160},{6,192},{7,224},{8,256}... | collective-permute-start | bytes 98312 | tf_op jit(solution)/shard_map/ppermute | solution.py:50
  7.8 32.8 %copy-start = (bf16[1,1,32,128,128]{4,3,2,1,0:T(8,128)(2,1)S(1)}, bf16[1,1,32,128,128]{4,3,2,1,0:T(8,128)(2,1)}, u32[]{:S(2)}) copy-start(bf16[1,1,32,128,128]{4,3,2,1,0:T(8,128)(2,1)} %param.11) | copy-start | bytes 3145732
  7.8 32.5 %all-to-all-start = ((bf16[32,64,128]{2,1,0:T(8,128)(2,1)}), bf16[32,64,128]{2,1,0:T(8,128)(2,1)S(1)}, u32[]{:S(2)}, u32[]{:S(2)}) async-start(bf16[32,64,128]{2,1,0:T(8,128)(2,1)} %bitcast.4), calls=%async_computation | async-start | bytes 1048576 | tf_op jit(solution)/shard_map/all_to_all | solution.py:53
  41.1 36.4 %copy-start.2 = (f32[16384]{0:T(1024)S(1)}, f32[16384]{0:T(1024)}, u32[]{:S(2)}) copy-start(f32[16384]{0:T(1024)} %param.12) | copy-start | bytes 196612
  79.5 38.2 %all-to-all-start.2 = ((bf16[32,72,128]{2,1,0:T(8,128)(2,1)}), bf16[32,72,128]{2,1,0:T(8,128)(2,1)S(1)}, u32[]{:S(2)}, u32[]{:S(2)}) async-start(bf16[32,72,128]{2,1,0:T(8,128)(2,1)} %pad_maximum_fusion), calls=%async_computation.2 | async-start | bytes 1179648 | tf_op jit(solution)/shard_map/all_to_all | solution.py:20
  83.4 24.1 %copy-start.4 = (s32[32]{0:T(128)S(1)}, s32[32]{0:T(128)}, u32[]{:S(2)}) copy-start(s32[32]{0:T(128)} %constant.103.clone) | copy-start | bytes 388
  83.5 7.3 %collective-permute-start.1 = (bf16[1,128,128]{2,1,0:T(8,128)(2,1)S(1)}, bf16[1,128,128]{2,1,0:T(8,128)(2,1)S(1)}, u32[]{:S(2)}, u32[]{:S(2)}) collective-permute-start(bf16[1,128,128]{2,1,0:T(8,128)(2,1)S(1)} %bitcast.46), channel_id=1, source_target_pairs={{0,8},{1,9},{2,10},{3,11},{4,12},{5,13},{6,14},{7,15},{8,0},{9,1},... | collective-permute-start | bytes 98312 | tf_op jit(solution)/shard_map/ppermute | solution.py:58
  90.8 7.9 %collective-permute-start.2 = (bf16[2,128,128]{2,1,0:T(8,128)(2,1)S(1)}, bf16[2,128,128]{2,1,0:T(8,128)(2,1)S(1)}, u32[]{:S(2)}, u32[]{:S(2)}) collective-permute-start(bf16[2,128,128]{2,1,0:T(8,128)(2,1)S(1)} %pad_maximum_fusion.7), channel_id=1, source_target_pairs={{0,2},{1,3},{2,0},{3,1},{4,6},{5,7},{6,4},{7,5},{8,10},{9,11},{10,... | collective-permute-start | bytes 196616 | tf_op jit(solution)/shard_map/ppermute | solution.py:58
  98.7 6.9 %collective-permute-start.3 = (bf16[4,128,128]{2,1,0:T(8,128)(2,1)S(1)}, bf16[4,128,128]{2,1,0:T(8,128)(2,1)S(1)}, u32[]{:S(2)}, u32[]{:S(2)}) collective-permute-start(bf16[4,128,128]{2,1,0:T(8,128)(2,1)S(1)} %pad_maximum_fusion.6), channel_id=1, source_target_pairs={{0,4},{1,5},{2,6},{3,7},{4,0},{5,1},{6,2},{7,3},{8,12},{9,13},{10,... | collective-permute-start | bytes 393224 | tf_op jit(solution)/shard_map/ppermute | solution.py:58
  105.6 3.4 %collective-permute-start.4 = (bf16[8,128,128]{2,1,0:T(8,128)(2,1)S(1)}, bf16[8,128,128]{2,1,0:T(8,128)(2,1)S(1)}, u32[]{:S(2)}, u32[]{:S(2)}) collective-permute-start(bf16[8,128,128]{2,1,0:T(8,128)(2,1)S(1)} %pad_maximum_fusion.5), channel_id=1, source_target_pairs={{0,1},{1,0},{2,3},{3,2},{4,5},{5,4},{6,7},{7,6},{8,9},{9,8},{10,11... | collective-permute-start | bytes 786440 | tf_op jit(solution)/shard_map/ppermute | solution.py:58
  118.6 29.1 %all-to-all-start.3 = ((bf16[32,40,128]{2,1,0:T(8,128)(2,1)}), bf16[32,40,128]{2,1,0:T(8,128)(2,1)S(1)}, u32[]{:S(2)}, u32[]{:S(2)}) async-start(bf16[32,40,128]{2,1,0:T(8,128)(2,1)} %pad_maximum_fusion.4), calls=%async_computation.3 | async-start | bytes 655360 | tf_op jit(solution)/shard_map/all_to_all | solution.py:20

commit v6 on v5

--- a/solution.py
+++ b/solution.py
@@ -14,6 +14,21 @@
     for bit in COL_BITS:
         order = order + [c + bit for c in order]
     return [2 * c + e for c in order for e in range(2)]
+
+
+def seats(ncol):
+    def ring(a, b, size):
+        return min((a - b) % size, (b - a) % size)
+
+    def within(a, b):
+        return ring(a // 4, b // 4, 4) + (2 if (a ^ b) & 2 else 0)
+
+    out = []
+    for g in range(ncol):
+        planes = sorted(range(ncol), key=lambda m: (-ring(m, g, ncol), m))
+        places = sorted(range(ncol), key=lambda c: (within(c, g), c))
+        out.append([places[planes.index(m)] for m in range(ncol)])
+    return out
 
 
 def exchange(x):
@@ -43,7 +58,8 @@
     diag = diagonal.reshape(cb, b)
 
     order = member_order()
-    groups = [[(ratio * g + n % ratio) * ncol + n // ratio for n in range(nrow)] for g in range(ncol)]
+    seat = seats(ncol)
+    groups = [[(ratio * g + n % ratio) * ncol + seat[g][n // ratio] for n in range(nrow)] for g in range(ncol)]
     perm = [(n * ncol + g, groups[g][n]) for n in range(nrow) for g in range(ncol)]
 
     def turned(v):

time: 151 us -> 148 us (0.980)
  starting transfers between devices: 41.6 us -> 37.2 us
  blocking collectives: 36.1 us -> 38.8 us
  waiting for transfers between devices: 61.3 us -> 59.5 us
    all_to_all x1, starting transfers between devices: 20.1 us -> 7.81 us  [in_group(): lax.all_to_all(v, ('row', 'col'), 0, 0, tiled=True, axis_index_groups=[[g...]
    ppermute x1, waiting for transfers between devices: 3.31 us -> 9.48 us  [turned(): return lax.ppermute(v, ('row', 'col'), perm)]
    all_to_all x1, waiting for transfers between devices: 12.2 us -> 7.32 us  [in_group(): lax.all_to_all(v, ('row', 'col'), 0, 0, tiled=True, axis_index_groups=[[g...]
    ppermute x1, starting transfers between devices: 1.92 us -> 6.37 us  [turned(): return lax.ppermute(v, ('row', 'col'), perm)]
    ppermute x4, waiting for transfers between devices: 13.3 us -> 10.1 us  [gathered(): other = lax.ppermute(v, 'col', [(c, c ^ bit) for c in range(ncol)])]
    ppermute x4, starting transfers between devices: 10.8 us -> 13.9 us  [gathered(): other = lax.ppermute(v, 'col', [(c, c ^ bit) for c in range(ncol)])]
    all_to_all x1, blocking collectives: 36.1 us -> 38.8 us  [exchange(): lax.all_to_all(x, 'row', 0, 0, tiled=True, axis_index_groups=[member_orde...]
where the time goes in v6:
time: 148 us; the launch traced here: 147 us
  waiting for transfers between devices  59.5 us (40%)
  blocking collectives  38.8 us (26%)
  starting transfers between devices  37.2 us (25%)
  matrix products  4.16 us (3%)
  other arithmetic  3.74 us (3%)
  local copies, waits for them, and re-layouts  2.17 us (1%)
  between operations  1.65 us (1%)
    all_to_all x1, blocking collectives, exchange(): lax.all_to_all(x, 'row', 0, 0, tiled=True, axis_index_groups=[member_orde...  38.8 us
    all_to_all x2, waiting for transfers between devices, exchange(): lax.all_to_all(x, 'row', 0, 0, tiled=True, axis_index_groups=[member_orde...  32.6 us
    ppermute x4, starting transfers between devices, gathered(): other = lax.ppermute(v, 'col', [(c, c ^ bit) for c in range(ncol)])  13.9 us
    ppermute x4, waiting for transfers between devices, gathered(): other = lax.ppermute(v, 'col', [(c, c ^ bit) for c in range(ncol)])  10.1 us
    ppermute x1, waiting for transfers between devices, turned(): return lax.ppermute(v, ('row', 'col'), perm)  9.48 us
    all_to_all x2, starting transfers between devices, exchange(): lax.all_to_all(x, 'row', 0, 0, tiled=True, axis_index_groups=[member_orde...  9.19 us
    all_to_all x1, starting transfers between devices, in_group(): lax.all_to_all(v, ('row', 'col'), 0, 0, tiled=True, axis_index_groups=[[g...  7.81 us
    all_to_all x1, waiting for transfers between devices, in_group(): lax.all_to_all(v, ('row', 'col'), 0, 0, tiled=True, axis_index_groups=[[g...  7.32 us
  transfers between devices with their start and end apart: 8, of which 8 were waited for; matrix products, arithmetic and copies ran while one was open for 1% of the time, Pallas kernels for 0%

profile of v6, /device:TPU:32, one launch (start us, length us, event | category | flops | bytes accessed | tf_op | source)
XLA Modules:
  0.0 147.3 jit_solution(9209613446226600810)
XLA Ops:
  0.6 0.0 copy-start.3
  0.6 0.0 copy-start.1
  0.6 1.0 reduce.4
  1.7 6.4 %collective-permute-start = (bf16[128,128]{1,0:T(8,128)(2,1)S(1)}, bf16[128,128]{1,0:T(8,128)(2,1)S(1)}, u32[]{:S(2)}, u32[]{:S(2)}) collective-permute-start(bf16[128,128]{1,0:T(8,128)(2,1)S(1)} %bitcast.44), channel_id=1, source_target_pairs={{0,11},{1,47},{2,69},{3,107},{4,135},{5,169},{6,195},{7,231},{8,26... | collective-permute-start | bytes 98312 | tf_op jit(solution)/shard_map/ppermute | solution.py:66
  8.1 9.5 %collective-permute-done = bf16[128,128]{1,0:T(8,128)(2,1)S(1)} collective-permute-done((bf16[128,128]{1,0:T(8,128)(2,1)S(1)}, bf16[128,128]{1,0:T(8,128)(2,1)S(1)}, u32[]{:S(2)}, u32[]{:S(2)}) %collective-permute-start) | collective-permute-done | bytes 32800 | tf_op jit(solution)/shard_map/ppermute | solution.py:66
  17.5 0.9 broadcast_in_dim.13
  18.4 0.0 copy-start
  18.4 7.8 %all-to-all-start = ((bf16[32,64,128]{2,1,0:T(8,128)(2,1)}), bf16[32,64,128]{2,1,0:T(8,128)(2,1)S(1)}, u32[]{:S(2)}, u32[]{:S(2)}) async-start(bf16[32,64,128]{2,1,0:T(8,128)(2,1)} %bitcast.4), calls=%async_computation | async-start | bytes 1048576 | tf_op jit(solution)/shard_map/all_to_all | solution.py:69
  26.3 0.0 copy-done.3
  26.3 0.0 copy-done.1
  26.3 0.2 scatter.9
  26.5 7.3 %all-to-all-done = bf16[32,64,128]{2,1,0:T(8,128)(2,1)S(1)} async-done(((bf16[32,64,128]{2,1,0:T(8,128)(2,1)}), bf16[32,64,128]{2,1,0:T(8,128)(2,1)S(1)}, u32[]{:S(2)}, u32[]{:S(2)}) %all-to-all-start) | async-done | bytes 524320 | tf_op jit(solution)/shard_map/all_to_all | solution.py:69
  33.8 0.3 fusion.1
  34.1 0.0 copy-done
  34.1 0.4 fusion.2
  34.5 0.0 copy-start.2
  34.6 0.1 copy.27
  34.7 38.8 %all_to_all.20 = bf16[32,40,128]{2,1,0:T(8,128)(2,1)S(1)} all-to-all(bf16[32,40,128]{2,1,0:T(8,128)(2,1)S(1)} %copy.27), channel_id=1, replica_groups={{0,16,256,272,64,80,320,336,128,144,384,400,192,208,448,464,32,48,288,3..., dimensions={0} | all-to-all | bytes 655360 | tf_op jit(solution)/shard_map/all_to_all | solution.py:35
  73.6 0.1 reshape.141
  73.7 0.0 copy-done.2
  73.7 0.5 convert_multiply_fusion
  74.3 0.4 convolution_convert_fusion
  74.7 0.1 fusion.23
  74.8 0.9 pad_maximum_fusion
  75.7 4.0 %all-to-all-start.2 = ((bf16[32,72,128]{2,1,0:T(8,128)(2,1)}), bf16[32,72,128]{2,1,0:T(8,128)(2,1)S(1)}, u32[]{:S(2)}, u32[]{:S(2)}) async-start(bf16[32,72,128]{2,1,0:T(8,128)(2,1)} %pad_maximum_fusion), calls=%async_computation.2 | async-start | bytes 1179648 | tf_op jit(solution)/shard_map/all_to_all | solution.py:35
  79.6 0.0 copy-start.4
  79.7 3.8 %collective-permute-start.1 = (bf16[1,128,128]{2,1,0:T(8,128)(2,1)S(1)}, bf16[1,128,128]{2,1,0:T(8,128)(2,1)S(1)}, u32[]{:S(2)}, u32[]{:S(2)}) collective-permute-start(bf16[1,128,128]{2,1,0:T(8,128)(2,1)S(1)} %bitcast.46), channel_id=1, source_target_pairs={{0,8},{1,9},{2,10},{3,11},{4,12},{5,13},{6,14},{7,15},{8,0},{9,1},... | collective-permute-start | bytes 98312 | tf_op jit(solution)/shard_map/ppermute | solution.py:74
  83.5 3.5 %collective-permute-done.1 = bf16[1,128,128]{2,1,0:T(8,128)(2,1)S(1)} collective-permute-done((bf16[1,128,128]{2,1,0:T(8,128)(2,1)S(1)}, bf16[1,128,128]{2,1,0:T(8,128)(2,1)S(1)}, u32[]{:S(2)}, u32[]{:S(2)}) %collective-permute-start.1) | collective-permute-done | bytes 32800 | tf_op jit(solution)/shard_map/ppermute | solution.py:74
  87.0 4.8 %collective-permute-start.2 = (bf16[2,128,128]{2,1,0:T(8,128)(2,1)S(1)}, bf16[2,128,128]{2,1,0:T(8,128)(2,1)S(1)}, u32[]{:S(2)}, u32[]{:S(2)}) collective-permute-start(bf16[2,128,128]{2,1,0:T(8,128)(2,1)S(1)} %pad_maximum_fusion.7), channel_id=1, source_target_pairs={{0,2},{1,3},{2,0},{3,1},{4,6},{5,7},{6,4},{7,5},{8,10},{9,11},{10,... | collective-permute-start | bytes 196616 | tf_op jit(solution)/shard_map/ppermute | solution.py:74
  91.8 2.9 %collective-permute-done.2 = bf16[2,128,128]{2,1,0:T(8,128)(2,1)S(1)} collective-permute-done((bf16[2,128,128]{2,1,0:T(8,128)(2,1)S(1)}, bf16[2,128,128]{2,1,0:T(8,128)(2,1)S(1)}, u32[]{:S(2)}, u32[]{:S(2)}) %collective-permute-start.2) | collective-permute-done | bytes 65568 | tf_op jit(solution)/shard_map/ppermute | solution.py:74
  94.7 3.4 %collective-permute-start.3 = (bf16[4,128,128]{2,1,0:T(8,128)(2,1)S(1)}, bf16[4,128,128]{2,1,0:T(8,128)(2,1)S(1)}, u32[]{:S(2)}, u32[]{:S(2)}) collective-permute-start(bf16[4,128,128]{2,1,0:T(8,128)(2,1)S(1)} %pad_maximum_fusion.6), channel_id=1, source_target_pairs={{0,4},{1,5},{2,6},{3,7},{4,0},{5,1},{6,2},{7,3},{8,12},{9,13},{10,... | collective-permute-start | bytes 393224 | tf_op jit(solution)/shard_map/ppermute | solution.py:74
  98.1 3.5 %collective-permute-done.3 = bf16[4,128,128]{2,1,0:T(8,128)(2,1)S(1)} collective-permute-done((bf16[4,128,128]{2,1,0:T(8,128)(2,1)S(1)}, bf16[4,128,128]{2,1,0:T(8,128)(2,1)S(1)}, u32[]{:S(2)}, u32[]{:S(2)}) %collective-permute-start.3) | collective-permute-done | bytes 131104 | tf_op jit(solution)/shard_map/ppermute | solution.py:74
  101.7 1.9 %collective-permute-start.4 = (bf16[8,128,128]{2,1,0:T(8,128)(2,1)S(1)}, bf16[8,128,128]{2,1,0:T(8,128)(2,1)S(1)}, u32[]{:S(2)}, u32[]{:S(2)}) collective-permute-start(bf16[8,128,128]{2,1,0:T(8,128)(2,1)S(1)} %pad_maximum_fusion.5), channel_id=1, source_target_pairs={{0,1},{1,0},{2,3},{3,2},{4,5},{5,4},{6,7},{7,6},{8,9},{9,8},{10,11... | collective-permute-start | bytes 786440 | tf_op jit(solution)/shard_map/ppermute | solution.py:74
  103.6 0.0 copy-done.4
  103.6 0.6 dynamic_slice.6
  104.9 0.2 collective-permute-done.4
  105.2 0.3 convolution_convert_fusion.1
  105.5 8.3 %all-to-all-done.2 = bf16[32,72,128]{2,1,0:T(8,128)(2,1)S(1)} async-done(((bf16[32,72,128]{2,1,0:T(8,128)(2,1)}), bf16[32,72,128]{2,1,0:T(8,128)(2,1)S(1)}, u32[]{:S(2)}, u32[]{:S(2)}) %all-to-all-start.2) | async-done | bytes 589856 | tf_op jit(solution)/shard_map/all_to_all | solution.py:35
  114.0 0.8 pad_maximum_fusion.4
  114.7 5.2 %all-to-all-start.3 = ((bf16[32,40,128]{2,1,0:T(8,128)(2,1)}), bf16[32,40,128]{2,1,0:T(8,128)(2,1)S(1)}, u32[]{:S(2)}, u32[]{:S(2)}) async-start(bf16[32,40,128]{2,1,0:T(8,128)(2,1)} %pad_maximum_fusion.4), calls=%async_computation.3 | async-start | bytes 655360 | tf_op jit(solution)/shard_map/all_to_all | solution.py:35
  120.0 0.1 copy.29
  120.1 24.2 %all-to-all-done.3 = bf16[32,40,128]{2,1,0:T(8,128)(2,1)S(1)} async-done(((bf16[32,40,128]{2,1,0:T(8,128)(2,1)}), bf16[32,40,128]{2,1,0:T(8,128)(2,1)S(1)}, u32[]{:S(2)}, u32[]{:S(2)}) %all-to-all-start.3) | async-done | bytes 327712 | tf_op jit(solution)/shard_map/all_to_all | solution.py:35
  144.4 2.3 %fusion = bf16[1,1,32,128,128]{4,3,2,1,0:T(8,128)(2,1)} fusion(bf16[1,1,32,128,128]{4,3,2,1,0:T(8,128)(2,1)S(1)} %copy-done, bf16[32,32,128]{2,0,1:T(8,128)(2,1)S(1)} %get-tuple-element.39, bf16[32,32,128]{2,0,1:T(8,128)(2,1)S(1)} %get-tuple-element.38, bf16[64,32,128]{2,1,0:T(8,128)(2,1)S(1)} %pad_maximum_fusion.2), kind=kOutput, calls=%fused_computation.2 | convolution fusion | flops 72876032 | bytes 3145728 | tf_op jit(solution)/shard_map/nki,nkj->kij/dot_general | solution.py:121
  146.6 0.6 convert_add_fusion
  (25 shorter events, 0.5 us)
Async XLA Ops:
  0.6 25.6 %copy-start.3 = (s32[1,1,32]{2,1,0:T(1,128)S(1)}, s32[1,1,32]{2,1,0:T(1,128)}, u32[]{:S(2)}) copy-start(s32[1,1,32]{2,1,0:T(1,128)} %param.14) | copy-start | bytes 388
  0.6 25.7 %copy-start.1 = (s32[1,1,32]{2,1,0:T(1,128)S(1)}, s32[1,1,32]{2,1,0:T(1,128)}, u32[]{:S(2)}) copy-start(s32[1,1,32]{2,1,0:T(1,128)} %param.13) | copy-start | bytes 388
  1.7 15.9 %collective-permute-start = (bf16[128,128]{1,0:T(8,128)(2,1)S(1)}, bf16[128,128]{1,0:T(8,128)(2,1)S(1)}, u32[]{:S(2)}, u32[]{:S(2)}) collective-permute-start(bf16[128,128]{1,0:T(8,128)(2,1)S(1)} %bitcast.44), channel_id=1, source_target_pairs={{0,11},{1,47},{2,69},{3,107},{4,135},{5,169},{6,195},{7,231},{8,26... | collective-permute-start | bytes 98312 | tf_op jit(solution)/shard_map/ppermute | solution.py:66
  18.4 15.6 %copy-start = (bf16[1,1,32,128,128]{4,3,2,1,0:T(8,128)(2,1)S(1)}, bf16[1,1,32,128,128]{4,3,2,1,0:T(8,128)(2,1)}, u32[]{:S(2)}) copy-start(bf16[1,1,32,128,128]{4,3,2,1,0:T(8,128)(2,1)} %param.11) | copy-start | bytes 3145732
  18.4 15.4 %all-to-all-start = ((bf16[32,64,128]{2,1,0:T(8,128)(2,1)}), bf16[32,64,128]{2,1,0:T(8,128)(2,1)S(1)}, u32[]{:S(2)}, u32[]{:S(2)}) async-start(bf16[32,64,128]{2,1,0:T(8,128)(2,1)} %bitcast.4), calls=%async_computation | async-start | bytes 1048576 | tf_op jit(solution)/shard_map/all_to_all | solution.py:69
  34.5 39.2 %copy-start.2 = (f32[16384]{0:T(1024)S(1)}, f32[16384]{0:T(1024)}, u32[]{:S(2)}) copy-start(f32[16384]{0:T(1024)} %param.12) | copy-start | bytes 196612
  75.7 38.2 %all-to-all-start.2 = ((bf16[32,72,128]{2,1,0:T(8,128)(2,1)}), bf16[32,72,128]{2,1,0:T(8,128)(2,1)S(1)}, u32[]{:S(2)}, u32[]{:S(2)}) async-start(bf16[32,72,128]{2,1,0:T(8,128)(2,1)} %pad_maximum_fusion), calls=%async_computation.2 | async-start | bytes 1179648 | tf_op jit(solution)/shard_map/all_to_all | solution.py:35
  79.6 24.0 %copy-start.4 = (s32[32]{0:T(128)S(1)}, s32[32]{0:T(128)}, u32[]{:S(2)}) copy-start(s32[32]{0:T(128)} %constant.103.clone) | copy-start | bytes 388
  79.7 7.3 %collective-permute-start.1 = (bf16[1,128,128]{2,1,0:T(8,128)(2,1)S(1)}, bf16[1,128,128]{2,1,0:T(8,128)(2,1)S(1)}, u32[]{:S(2)}, u32[]{:S(2)}) collective-permute-start(bf16[1,128,128]{2,1,0:T(8,128)(2,1)S(1)} %bitcast.46), channel_id=1, source_target_pairs={{0,8},{1,9},{2,10},{3,11},{4,12},{5,13},{6,14},{7,15},{8,0},{9,1},... | collective-permute-start | bytes 98312 | tf_op jit(solution)/shard_map/ppermute | solution.py:74
  87.0 7.7 %collective-permute-start.2 = (bf16[2,128,128]{2,1,0:T(8,128)(2,1)S(1)}, bf16[2,128,128]{2,1,0:T(8,128)(2,1)S(1)}, u32[]{:S(2)}, u32[]{:S(2)}) collective-permute-start(bf16[2,128,128]{2,1,0:T(8,128)(2,1)S(1)} %pad_maximum_fusion.7), channel_id=1, source_target_pairs={{0,2},{1,3},{2,0},{3,1},{4,6},{5,7},{6,4},{7,5},{8,10},{9,11},{10,... | collective-permute-start | bytes 196616 | tf_op jit(solution)/shard_map/ppermute | solution.py:74
  94.7 6.9 %collective-permute-start.3 = (bf16[4,128,128]{2,1,0:T(8,128)(2,1)S(1)}, bf16[4,128,128]{2,1,0:T(8,128)(2,1)S(1)}, u32[]{:S(2)}, u32[]{:S(2)}) collective-permute-start(bf16[4,128,128]{2,1,0:T(8,128)(2,1)S(1)} %pad_maximum_fusion.6), channel_id=1, source_target_pairs={{0,4},{1,5},{2,6},{3,7},{4,0},{5,1},{6,2},{7,3},{8,12},{9,13},{10,... | collective-permute-start | bytes 393224 | tf_op jit(solution)/shard_map/ppermute | solution.py:74
  101.7 3.4 %collective-permute-start.4 = (bf16[8,128,128]{2,1,0:T(8,128)(2,1)S(1)}, bf16[8,128,128]{2,1,0:T(8,128)(2,1)S(1)}, u32[]{:S(2)}, u32[]{:S(2)}) collective-permute-start(bf16[8,128,128]{2,1,0:T(8,128)(2,1)S(1)} %pad_maximum_fusion.5), channel_id=1, source_target_pairs={{0,1},{1,0},{2,3},{3,2},{4,5},{5,4},{6,7},{7,6},{8,9},{9,8},{10,11... | collective-permute-start | bytes 786440 | tf_op jit(solution)/shard_map/ppermute | solution.py:74
  114.7 29.6 %all-to-all-start.3 = ((bf16[32,40,128]{2,1,0:T(8,128)(2,1)}), bf16[32,40,128]{2,1,0:T(8,128)(2,1)S(1)}, u32[]{:S(2)}, u32[]{:S(2)}) async-start(bf16[32,40,128]{2,1,0:T(8,128)(2,1)} %pad_maximum_fusion.4), calls=%async_computation.3 | async-start | bytes 655360 | tf_op jit(solution)/shard_map/all_to_all | solution.py:35

commit v7 on v6

--- a/solution.py
+++ b/solution.py
@@ -35,13 +35,13 @@
     return lax.all_to_all(x, "row", 0, 0, tiled=True, axis_index_groups=[member_order()])
 
 
+def joined_exchange(*parts):
+    parts = [part.reshape(part.shape[0], -1, 4, part.shape[-1]) for part in parts]
+    return exchange(jnp.concatenate(parts, axis=1))
+
+
 def pick(index, size):
     return (index.reshape(-1, 1) == jnp.arange(size, dtype=index.dtype)[None, :]).astype(BF)
-
-
-def halves(v):
-    high = lax.reduce_precision(v, 8, 7)
-    return high.astype(BF), (v - high).astype(BF)
 
 
 def on_device(samples, blocks, diagonal, block_rows, block_cols):
@@ -81,40 +81,35 @@
     xr = jnp.einsum("sb,nbl->nsl", pick(rows, rb), got, preferred_element_type=jnp.float32).astype(BF)
 
     prod = jnp.einsum("nki,kij->nkj", xr, local, preferred_element_type=jnp.float32).astype(BF)
-    tail = jnp.zeros((8, b), BF).at[0, :k].set(cols.astype(BF)).at[1, :k].set(rows.astype(BF))
-    got = exchange(jnp.concatenate([prod, jnp.broadcast_to(tail[None], (nrow, 8, b))], axis=1))
-    named = jnp.pad(got[:, k, :k].astype(jnp.int32), ((0, 0), (0, 8)), constant_values=-1)
-    pick_c = pick(named, cb)
-    pick_r = pick(got[:, k + 1, :k].astype(jnp.int32), rb).reshape(nrow, k, rb)
+    tail = jnp.zeros((4, b), BF).at[0, :k].set(cols.astype(BF)).at[1, :k].set(rows.astype(BF))
+    got = joined_exchange(prod, jnp.broadcast_to(tail[None], (nrow, 4, b)))
+    named = got[:, k // 4, :2, :k].astype(jnp.int32)
+    spread = jnp.pad(named[:, 0], ((0, 0), (0, 4)), constant_values=-1)
     total = lax.dot_general(
-        pick_c, got.reshape(nrow * (k + 8), b), (((0,), (0,)), ((), ())), preferred_element_type=jnp.float32
+        pick(spread, cb), got.reshape(nrow * (k + 4), b), (((0,), (0,)), ((), ())), preferred_element_type=jnp.float32
     )
+    pick_c = pick(named[:, 0], cb)
+    pick_r = pick(named[:, 1], rb).reshape(nrow, k, rb)
     xf = x.astype(jnp.float32)
     mixed = (total + xf * diag).astype(BF)
 
     quad = (xf * mixed.astype(jnp.float32)).reshape(nrow, own, b)
     out = jnp.dot(pick_c, jnp.concatenate([mixed, x], axis=1), preferred_element_type=jnp.float32).astype(BF)
-    out = out.reshape(nrow, k + 8, 2 * b)[:, :k]
-    out = jnp.concatenate([out[..., :b], *halves(quad), out[..., b:]], axis=1)
-    out, mixed = lax.optimization_barrier((out, mixed))
-    got = exchange(out)
+    out = out.reshape(nrow, k, 2 * b)
+    out, quad, mixed = lax.optimization_barrier((out, quad.astype(BF), mixed))
+    got = joined_exchange(out[..., :b], quad, out[..., b:])
 
     held = gathered(mixed).reshape(nrow, rb, b)
     out = jnp.einsum("tsb,tbl->tsl", pick_r, held, preferred_element_type=jnp.float32).astype(BF)
     out, got = lax.optimization_barrier((out, got))
 
-    wc, xc = got[:, :k], got[:, k + 2 * own :]
-    quad = jnp.sum(got[:, k : k + 2 * own].astype(jnp.float32), axis=0)
-    quad = quad[:own] + quad[own:]
-    place = jnp.array([order.index(n) for n in range(nrow)], jnp.int32)[lax.axis_index("row")]
-    mine = lax.dynamic_slice_in_dim(diag, place * own, own, 0)
-    diag_grad = -1.0 / mine + quad / nrow
-    mine = mine - TAU * diag_grad
-
-    mine = jnp.concatenate(halves(mine))
-    got = exchange(jnp.concatenate([out, jnp.broadcast_to(mine[None], (nrow, 2 * own, b))], axis=1))
-    wr = got[:, :k]
-    new_diagonal = got[:, k : k + own].astype(jnp.float32) + got[:, k + own :].astype(jnp.float32)
+    wc, xc = got[:, : k // 4].reshape(nrow, k, b), got[:, -k // 4 :].reshape(nrow, k, b)
+    quad = jnp.sum(got[:, k // 4 : -k // 4].astype(jnp.float32), axis=0).reshape(own, b).astype(BF)
+    got = joined_exchange(out, jnp.broadcast_to(quad[None], (nrow, own, b)))
+    wr = got[:, : k // 4].reshape(nrow, k, b)
+    quad = got[:, k // 4 :].reshape(cb, b).astype(jnp.float32)
+    diag_grad = -1.0 / diag + quad / nrow
+    new_diagonal = diag - TAU * diag_grad
 
     left = jnp.concatenate([xr, wr], axis=0)
     right = jnp.concatenate([wc, xc], axis=0)

time: 148 us -> 146 us (0.986)
  waiting for transfers between devices: 59.5 us -> 57.8 us
    all_to_all x2, waiting for transfers between devices: 32.6 us -> 29.3 us  [exchange(): lax.all_to_all(x, 'row', 0, 0, tiled=True, axis_index_groups=[member_orde...]
    ppermute x4, waiting for transfers between devices: 10.1 us -> 11.7 us  [gathered(): other = lax.ppermute(v, 'col', [(c, c ^ bit) for c in range(ncol)])]
where the time goes in v7:
time: 146 us; the launch traced here: 145 us
  waiting for transfers between devices  57.8 us (40%)
  starting transfers between devices  38.2 us (26%)
  blocking collectives  37.4 us (26%)
  other arithmetic  4.3 us (3%)
  matrix products  4.12 us (3%)
  local copies, waits for them, and re-layouts  2.08 us (1%)
    all_to_all x1, blocking collectives, exchange(): lax.all_to_all(x, 'row', 0, 0, tiled=True, axis_index_groups=[member_orde...  37.4 us
    all_to_all x2, waiting for transfers between devices, exchange(): lax.all_to_all(x, 'row', 0, 0, tiled=True, axis_index_groups=[member_orde...  29.3 us
    ppermute x4, starting transfers between devices, gathered(): other = lax.ppermute(v, 'col', [(c, c ^ bit) for c in range(ncol)])  13.7 us
    ppermute x4, waiting for transfers between devices, gathered(): other = lax.ppermute(v, 'col', [(c, c ^ bit) for c in range(ncol)])  11.7 us
    all_to_all x2, starting transfers between devices, exchange(): lax.all_to_all(x, 'row', 0, 0, tiled=True, axis_index_groups=[member_orde...  10.3 us
    ppermute x1, waiting for transfers between devices, turned(): return lax.ppermute(v, ('row', 'col'), perm)  9.48 us
    all_to_all x1, starting transfers between devices, in_group(): lax.all_to_all(v, ('row', 'col'), 0, 0, tiled=True, axis_index_groups=[[g...  7.81 us
    all_to_all x1, waiting for transfers between devices, in_group(): lax.all_to_all(v, ('row', 'col'), 0, 0, tiled=True, axis_index_groups=[[g...  7.32 us
  transfers between devices with their start and end apart: 8, of which 8 were waited for; matrix products, arithmetic and copies ran while one was open for 1% of the time, Pallas kernels for 0%

profile of v7, /device:TPU:32, one launch (start us, length us, event | category | flops | bytes accessed | tf_op | source)
XLA Modules:
  0.0 144.9 jit_solution(6468292499153728759)
XLA Ops:
  0.6 0.0 copy-start.3
  0.6 0.0 copy-start.2
  0.6 1.0 reduce.6
  1.7 6.4 %collective-permute-start = (bf16[128,128]{1,0:T(8,128)(2,1)S(1)}, bf16[128,128]{1,0:T(8,128)(2,1)S(1)}, u32[]{:S(2)}, u32[]{:S(2)}) collective-permute-start(bf16[128,128]{1,0:T(8,128)(2,1)S(1)} %bitcast.62), channel_id=1, source_target_pairs={{0,11},{1,47},{2,69},{3,107},{4,135},{5,169},{6,195},{7,231},{8,26... | collective-permute-start | bytes 98312 | tf_op jit(solution)/shard_map/ppermute | solution.py:66
  8.1 9.5 %collective-permute-done = bf16[128,128]{1,0:T(8,128)(2,1)S(1)} collective-permute-done((bf16[128,128]{1,0:T(8,128)(2,1)S(1)}, bf16[128,128]{1,0:T(8,128)(2,1)S(1)}, u32[]{:S(2)}, u32[]{:S(2)}) %collective-permute-start) | collective-permute-done | bytes 32800 | tf_op jit(solution)/shard_map/ppermute | solution.py:66
  17.5 0.9 broadcast_in_dim.9
  18.4 0.0 copy-start
  18.4 7.8 %all-to-all-start = ((bf16[32,64,128]{2,1,0:T(8,128)(2,1)}), bf16[32,64,128]{2,1,0:T(8,128)(2,1)S(1)}, u32[]{:S(2)}, u32[]{:S(2)}) async-start(bf16[32,64,128]{2,1,0:T(8,128)(2,1)} %bitcast.4), calls=%async_computation | async-start | bytes 1048576 | tf_op jit(solution)/shard_map/all_to_all | solution.py:69
  26.3 0.0 copy-done.3
  26.3 0.0 copy-done.2
  26.3 0.2 scatter.9
  26.5 7.3 %all-to-all-done = bf16[32,64,128]{2,1,0:T(8,128)(2,1)S(1)} async-done(((bf16[32,64,128]{2,1,0:T(8,128)(2,1)}), bf16[32,64,128]{2,1,0:T(8,128)(2,1)S(1)}, u32[]{:S(2)}, u32[]{:S(2)}) %all-to-all-start) | async-done | bytes 524320 | tf_op jit(solution)/shard_map/all_to_all | solution.py:69
  33.8 0.3 fusion.1
  34.1 0.0 copy-done
  34.1 0.4 convolution_convert_fusion.2
  34.5 0.0 copy-start.1
  34.5 0.1 copy.19
  34.6 0.2 pad_maximum_fusion.3
  34.9 37.4 %all_to_all.20 = bf16[32,9,4,128]{3,2,1,0:T(4,128)(2,1)S(1)} all-to-all(bf16[32,9,4,128]{3,2,1,0:T(4,128)(2,1)S(1)} %pad_maximum_fusion.3), channel_id=1, replica_groups={{0,16,256,272,64,80,320,336,128,144,384,400,192,208,448,464,32,48,288,3..., dimensions={0} | all-to-all | bytes 589824 | tf_op jit(solution)/shard_map/all_to_all | solution.py:35
  72.3 0.1 fusion.24
  72.4 0.1 eq.85
  72.5 0.1 eq.89
  72.6 0.0 copy-done.1
  72.6 0.5 fusion.12
  73.1 0.4 convolution_convert_fusion
  73.5 0.1 fusion.23
  73.6 1.2 pad_maximum_fusion
  74.8 4.0 %all-to-all-start.2 = ((bf16[32,17,4,128]{3,2,1,0:T(4,128)(2,1)}), bf16[32,17,4,128]{3,2,1,0:T(4,128)(2,1)S(1)}, u32[]{:S(2)}, u32[]{:S(2)}) async-start(bf16[32,17,4,128]{3,2,1,0:T(4,128)(2,1)} %pad_maximum_fusion), calls=%async_computation.2 | async-start | bytes 1114112 | tf_op jit(solution)/shard_map/all_to_all | solution.py:35
  78.8 3.8 %collective-permute-start.1 = (bf16[1,128,128]{2,1,0:T(8,128)(2,1)S(1)}, bf16[1,128,128]{2,1,0:T(8,128)(2,1)S(1)}, u32[]{:S(2)}, u32[]{:S(2)}) collective-permute-start(bf16[1,128,128]{2,1,0:T(8,128)(2,1)S(1)} %bitcast.64), channel_id=1, source_target_pairs={{0,8},{1,9},{2,10},{3,11},{4,12},{5,13},{6,14},{7,15},{8,0},{9,1},... | collective-permute-start | bytes 98312 | tf_op jit(solution)/shard_map/ppermute | solution.py:74
  82.5 3.5 %collective-permute-done.1 = bf16[1,128,128]{2,1,0:T(8,128)(2,1)S(1)} collective-permute-done((bf16[1,128,128]{2,1,0:T(8,128)(2,1)S(1)}, bf16[1,128,128]{2,1,0:T(8,128)(2,1)S(1)}, u32[]{:S(2)}, u32[]{:S(2)}) %collective-permute-start.1) | collective-permute-done | bytes 32800 | tf_op jit(solution)/shard_map/ppermute | solution.py:74
  86.1 4.8 %collective-permute-start.2 = (bf16[2,128,128]{2,1,0:T(8,128)(2,1)S(1)}, bf16[2,128,128]{2,1,0:T(8,128)(2,1)S(1)}, u32[]{:S(2)}, u32[]{:S(2)}) collective-permute-start(bf16[2,128,128]{2,1,0:T(8,128)(2,1)S(1)} %pad_maximum_fusion.7), channel_id=1, source_target_pairs={{0,2},{1,3},{2,0},{3,1},{4,6},{5,7},{6,4},{7,5},{8,10},{9,11},{10,... | collective-permute-start | bytes 196616 | tf_op jit(solution)/shard_map/ppermute | solution.py:74
  90.9 3.0 %collective-permute-done.2 = bf16[2,128,128]{2,1,0:T(8,128)(2,1)S(1)} collective-permute-done((bf16[2,128,128]{2,1,0:T(8,128)(2,1)S(1)}, bf16[2,128,128]{2,1,0:T(8,128)(2,1)S(1)}, u32[]{:S(2)}, u32[]{:S(2)}) %collective-permute-start.2) | collective-permute-done | bytes 65568 | tf_op jit(solution)/shard_map/ppermute | solution.py:74
  94.0 3.2 %collective-permute-start.3 = (bf16[4,128,128]{2,1,0:T(8,128)(2,1)S(1)}, bf16[4,128,128]{2,1,0:T(8,128)(2,1)S(1)}, u32[]{:S(2)}, u32[]{:S(2)}) collective-permute-start(bf16[4,128,128]{2,1,0:T(8,128)(2,1)S(1)} %pad_maximum_fusion.6), channel_id=1, source_target_pairs={{0,4},{1,5},{2,6},{3,7},{4,0},{5,1},{6,2},{7,3},{8,12},{9,13},{10,... | collective-permute-start | bytes 393224 | tf_op jit(solution)/shard_map/ppermute | solution.py:74
  97.2 3.7 %collective-permute-done.3 = bf16[4,128,128]{2,1,0:T(8,128)(2,1)S(1)} collective-permute-done((bf16[4,128,128]{2,1,0:T(8,128)(2,1)S(1)}, bf16[4,128,128]{2,1,0:T(8,128)(2,1)S(1)}, u32[]{:S(2)}, u32[]{:S(2)}) %collective-permute-start.3) | collective-permute-done | bytes 131104 | tf_op jit(solution)/shard_map/ppermute | solution.py:74
  100.9 1.9 %collective-permute-start.4 = (bf16[8,128,128]{2,1,0:T(8,128)(2,1)S(1)}, bf16[8,128,128]{2,1,0:T(8,128)(2,1)S(1)}, u32[]{:S(2)}, u32[]{:S(2)}) collective-permute-start(bf16[8,128,128]{2,1,0:T(8,128)(2,1)S(1)} %pad_maximum_fusion.5), channel_id=1, source_target_pairs={{0,1},{1,0},{2,3},{3,2},{4,5},{5,4},{6,7},{7,6},{8,9},{9,8},{10,11... | collective-permute-start | bytes 786440 | tf_op jit(solution)/shard_map/ppermute | solution.py:74
  102.9 1.5 %collective-permute-done.4 = bf16[8,128,128]{2,1,0:T(8,128)(2,1)S(1)} collective-permute-done((bf16[8,128,128]{2,1,0:T(8,128)(2,1)S(1)}, bf16[8,128,128]{2,1,0:T(8,128)(2,1)S(1)}, u32[]{:S(2)}, u32[]{:S(2)}) %collective-permute-start.4) | collective-permute-done | bytes 262176 | tf_op jit(solution)/shard_map/ppermute | solution.py:74
  104.5 0.3 convolution_convert_fusion.1
  104.8 6.8 %all-to-all-done.2 = bf16[32,17,4,128]{3,2,1,0:T(4,128)(2,1)S(1)} async-done(((bf16[32,17,4,128]{3,2,1,0:T(4,128)(2,1)}), bf16[32,17,4,128]{3,2,1,0:T(4,128)(2,1)S(1)}, u32[]{:S(2)}, u32[]{:S(2)}) %all-to-all-start.2) | async-done | bytes 557088 | tf_op jit(solution)/shard_map/all_to_all | solution.py:35
  111.7 0.9 pad_maximum_fusion.4
  112.6 6.4 %all-to-all-start.3 = ((bf16[32,9,4,128]{3,2,1,0:T(4,128)(2,1)}), bf16[32,9,4,128]{3,2,1,0:T(4,128)(2,1)S(1)}, u32[]{:S(2)}, u32[]{:S(2)}) async-start(bf16[32,9,4,128]{3,2,1,0:T(4,128)(2,1)} %pad_maximum_fusion.4), calls=%async_computation.3 | async-start | bytes 589824 | tf_op jit(solution)/shard_map/all_to_all | solution.py:35
  119.0 0.2 fusion.22
  119.2 0.1 copy.20
  119.3 0.1 copy.21
  119.4 22.4 %all-to-all-done.3 = bf16[32,9,4,128]{3,2,1,0:T(4,128)(2,1)S(1)} async-done(((bf16[32,9,4,128]{3,2,1,0:T(4,128)(2,1)}), bf16[32,9,4,128]{3,2,1,0:T(4,128)(2,1)S(1)}, u32[]{:S(2)}, u32[]{:S(2)}) %all-to-all-start.3) | async-done | bytes 294944 | tf_op jit(solution)/shard_map/all_to_all | solution.py:35
  141.8 0.1 slice.79
  142.0 0.6 multiply_subtract_fusion
  142.6 2.3 %fusion = bf16[1,1,32,128,128]{4,3,2,1,0:T(8,128)(2,1)} fusion(bf16[1,1,32,128,128]{4,3,2,1,0:T(8,128)(2,1)S(1)} %copy-done, bf16[32,32,128]{2,0,1:T(8,128)(2,1)S(1)} %bitcast.61, bf16[32,32,128]{2,0,1:T(8,128)(2,1)S(1)} %bitcast.60, bf16[64,32,128]{2,1,0:T(8,128)(2,1)S(1)} %pad_maximum_fusion.2), kind=kOutput, calls=%fused_computation.1 | convolution fusion | flops 72876032 | bytes 3145728 | tf_op jit(solution)/shard_map/nki,nkj->kij/dot_general | solution.py:116
  (18 shorter events, 0.4 us)
Async XLA Ops:
  0.6 25.6 %copy-start.3 = (s32[1,1,32]{2,1,0:T(1,128)S(1)}, s32[1,1,32]{2,1,0:T(1,128)}, u32[]{:S(2)}) copy-start(s32[1,1,32]{2,1,0:T(1,128)} %param.13) | copy-start | bytes 388
  0.6 25.7 %copy-start.2 = (s32[1,1,32]{2,1,0:T(1,128)S(1)}, s32[1,1,32]{2,1,0:T(1,128)}, u32[]{:S(2)}) copy-start(s32[1,1,32]{2,1,0:T(1,128)} %param.12) | copy-start | bytes 388
  1.7 15.9 %collective-permute-start = (bf16[128,128]{1,0:T(8,128)(2,1)S(1)}, bf16[128,128]{1,0:T(8,128)(2,1)S(1)}, u32[]{:S(2)}, u32[]{:S(2)}) collective-permute-start(bf16[128,128]{1,0:T(8,128)(2,1)S(1)} %bitcast.62), channel_id=1, source_target_pairs={{0,11},{1,47},{2,69},{3,107},{4,135},{5,169},{6,195},{7,231},{8,26... | collective-permute-start | bytes 98312 | tf_op jit(solution)/shard_map/ppermute | solution.py:66
  18.4 15.6 %copy-start = (bf16[1,1,32,128,128]{4,3,2,1,0:T(8,128)(2,1)S(1)}, bf16[1,1,32,128,128]{4,3,2,1,0:T(8,128)(2,1)}, u32[]{:S(2)}) copy-start(bf16[1,1,32,128,128]{4,3,2,1,0:T(8,128)(2,1)} %param.10) | copy-start | bytes 3145732
  18.4 15.4 %all-to-all-start = ((bf16[32,64,128]{2,1,0:T(8,128)(2,1)}), bf16[32,64,128]{2,1,0:T(8,128)(2,1)S(1)}, u32[]{:S(2)}, u32[]{:S(2)}) async-start(bf16[32,64,128]{2,1,0:T(8,128)(2,1)} %bitcast.4), calls=%async_computation | async-start | bytes 1048576 | tf_op jit(solution)/shard_map/all_to_all | solution.py:69
  34.5 38.1 %copy-start.1 = (f32[16384]{0:T(1024)S(1)}, f32[16384]{0:T(1024)}, u32[]{:S(2)}) copy-start(f32[16384]{0:T(1024)} %param.11) | copy-start | bytes 196612
  74.8 36.9 %all-to-all-start.2 = ((bf16[32,17,4,128]{3,2,1,0:T(4,128)(2,1)}), bf16[32,17,4,128]{3,2,1,0:T(4,128)(2,1)S(1)}, u32[]{:S(2)}, u32[]{:S(2)}) async-start(bf16[32,17,4,128]{3,2,1,0:T(4,128)(2,1)} %pad_maximum_fusion), calls=%async_computation.2 | async-start | bytes 1114112 | tf_op jit(solution)/shard_map/all_to_all | solution.py:35
  78.8 7.3 %collective-permute-start.1 = (bf16[1,128,128]{2,1,0:T(8,128)(2,1)S(1)}, bf16[1,128,128]{2,1,0:T(8,128)(2,1)S(1)}, u32[]{:S(2)}, u32[]{:S(2)}) collective-permute-start(bf16[1,128,128]{2,1,0:T(8,128)(2,1)S(1)} %bitcast.64), channel_id=1, source_target_pairs={{0,8},{1,9},{2,10},{3,11},{4,12},{5,13},{6,14},{7,15},{8,0},{9,1},... | collective-permute-start | bytes 98312 | tf_op jit(solution)/shard_map/ppermute | solution.py:74
  86.1 7.9 %collective-permute-start.2 = (bf16[2,128,128]{2,1,0:T(8,128)(2,1)S(1)}, bf16[2,128,128]{2,1,0:T(8,128)(2,1)S(1)}, u32[]{:S(2)}, u32[]{:S(2)}) collective-permute-start(bf16[2,128,128]{2,1,0:T(8,128)(2,1)S(1)} %pad_maximum_fusion.7), channel_id=1, source_target_pairs={{0,2},{1,3},{2,0},{3,1},{4,6},{5,7},{6,4},{7,5},{8,10},{9,11},{10,... | collective-permute-start | bytes 196616 | tf_op jit(solution)/shard_map/ppermute | solution.py:74
  94.0 6.9 %collective-permute-start.3 = (bf16[4,128,128]{2,1,0:T(8,128)(2,1)S(1)}, bf16[4,128,128]{2,1,0:T(8,128)(2,1)S(1)}, u32[]{:S(2)}, u32[]{:S(2)}) collective-permute-start(bf16[4,128,128]{2,1,0:T(8,128)(2,1)S(1)} %pad_maximum_fusion.6), channel_id=1, source_target_pairs={{0,4},{1,5},{2,6},{3,7},{4,0},{5,1},{6,2},{7,3},{8,12},{9,13},{10,... | collective-permute-start | bytes 393224 | tf_op jit(solution)/shard_map/ppermute | solution.py:74
  100.9 3.4 %collective-permute-start.4 = (bf16[8,128,128]{2,1,0:T(8,128)(2,1)S(1)}, bf16[8,128,128]{2,1,0:T(8,128)(2,1)S(1)}, u32[]{:S(2)}, u32[]{:S(2)}) collective-permute-start(bf16[8,128,128]{2,1,0:T(8,128)(2,1)S(1)} %pad_maximum_fusion.5), channel_id=1, source_target_pairs={{0,1},{1,0},{2,3},{3,2},{4,5},{5,4},{6,7},{7,6},{8,9},{9,8},{10,11... | collective-permute-start | bytes 786440 | tf_op jit(solution)/shard_map/ppermute | solution.py:74
  112.6 29.2 %all-to-all-start.3 = ((bf16[32,9,4,128]{3,2,1,0:T(4,128)(2,1)}), bf16[32,9,4,128]{3,2,1,0:T(4,128)(2,1)S(1)}, u32[]{:S(2)}, u32[]{:S(2)}) async-start(bf16[32,9,4,128]{3,2,1,0:T(4,128)(2,1)} %pad_maximum_fusion.4), calls=%async_computation.3 | async-start | bytes 589824 | tf_op jit(solution)/shard_map/all_to_all | solution.py:35

commit v8 on v7

--- a/solution.py
+++ b/solution.py
@@ -5,7 +5,7 @@
 
 TAU = 0.5
 PENALTY = 0.1
-COL_BITS = (8, 2, 4, 1)
+COL_BITS = (1, 8, 2, 4)
 BF = jnp.bfloat16
 
 

time: 146 us -> 144 us (0.986)
  the two profiles are of different devices: /device:TPU:32 before, /device:TPU:38 now
where the time goes in v8:
time: 144 us; the launch traced here: 143 us
  waiting for transfers between devices  53.5 us (37%)
  starting transfers between devices  42.5 us (30%)
  blocking collectives  36 us (25%)
  other arithmetic  4.3 us (3%)
  matrix products  4.13 us (3%)
  local copies, waits for them, and re-layouts  2.08 us (1%)
    all_to_all x1, blocking collectives, exchange(): lax.all_to_all(x, 'row', 0, 0, tiled=True, axis_index_groups=[member_orde...  36 us
    all_to_all x2, waiting for transfers between devices, exchange(): lax.all_to_all(x, 'row', 0, 0, tiled=True, axis_index_groups=[member_orde...  21 us
    all_to_all x2, starting transfers between devices, exchange(): lax.all_to_all(x, 'row', 0, 0, tiled=True, axis_index_groups=[member_orde...  16.1 us
    ppermute x4, waiting for transfers between devices, gathered(): other = lax.ppermute(v, 'col', [(c, c ^ bit) for c in range(ncol)])  15.3 us
    ppermute x4, starting transfers between devices, gathered(): other = lax.ppermute(v, 'col', [(c, c ^ bit) for c in range(ncol)])  12.7 us
    all_to_all x1, waiting for transfers between devices, in_group(): lax.all_to_all(v, ('row', 'col'), 0, 0, tiled=True, axis_index_groups=[[g...  9.37 us
    ppermute x1, waiting for transfers between devices, turned(): return lax.ppermute(v, ('row', 'col'), perm)  7.74 us
    all_to_all x1, starting transfers between devices, in_group(): lax.all_to_all(v, ('row', 'col'), 0, 0, tiled=True, axis_index_groups=[[g...  7.18 us
  transfers between devices with their start and end apart: 8, of which 8 were waited for; matrix products, arithmetic and copies ran while one was open for 1% of the time, Pallas kernels for 0%

profile of v8, /device:TPU:38, one launch (start us, length us, event | category | flops | bytes accessed | tf_op | source)
XLA Modules:
  0.0 143.4 jit_solution(8605215704749140039)
XLA Ops:
  0.6 0.0 copy-start.3
  0.6 0.0 copy-start.2
  0.6 1.0 reduce.6
  1.7 6.6 %collective-permute-start = (bf16[128,128]{1,0:T(8,128)(2,1)S(1)}, bf16[128,128]{1,0:T(8,128)(2,1)S(1)}, u32[]{:S(2)}, u32[]{:S(2)}) collective-permute-start(bf16[128,128]{1,0:T(8,128)(2,1)S(1)} %bitcast.62), channel_id=1, source_target_pairs={{0,11},{1,47},{2,69},{3,107},{4,135},{5,169},{6,195},{7,231},{8,26... | collective-permute-start | bytes 98312 | tf_op jit(solution)/shard_map/ppermute | solution.py:66
  8.2 7.7 %collective-permute-done = bf16[128,128]{1,0:T(8,128)(2,1)S(1)} collective-permute-done((bf16[128,128]{1,0:T(8,128)(2,1)S(1)}, bf16[128,128]{1,0:T(8,128)(2,1)S(1)}, u32[]{:S(2)}, u32[]{:S(2)}) %collective-permute-start) | collective-permute-done | bytes 32800 | tf_op jit(solution)/shard_map/ppermute | solution.py:66
  16.0 0.9 broadcast_in_dim.9
  16.9 0.0 copy-start
  16.9 7.2 %all-to-all-start = ((bf16[32,64,128]{2,1,0:T(8,128)(2,1)}), bf16[32,64,128]{2,1,0:T(8,128)(2,1)S(1)}, u32[]{:S(2)}, u32[]{:S(2)}) async-start(bf16[32,64,128]{2,1,0:T(8,128)(2,1)} %bitcast.4), calls=%async_computation | async-start | bytes 1048576 | tf_op jit(solution)/shard_map/all_to_all | solution.py:69
  24.1 0.0 copy-done.3
  24.1 0.0 copy-done.2
  24.1 0.2 scatter.9
  24.3 9.4 %all-to-all-done = bf16[32,64,128]{2,1,0:T(8,128)(2,1)S(1)} async-done(((bf16[32,64,128]{2,1,0:T(8,128)(2,1)}), bf16[32,64,128]{2,1,0:T(8,128)(2,1)S(1)}, u32[]{:S(2)}, u32[]{:S(2)}) %all-to-all-start) | async-done | bytes 524320 | tf_op jit(solution)/shard_map/all_to_all | solution.py:69
  33.7 0.3 fusion.1
  34.0 0.0 copy-done
  34.0 0.4 convolution_convert_fusion.2
  34.3 0.0 copy-start.1
  34.3 0.1 copy.19
  34.5 0.2 pad_maximum_fusion.3
  34.7 36.0 %all_to_all.20 = bf16[32,9,4,128]{3,2,1,0:T(4,128)(2,1)S(1)} all-to-all(bf16[32,9,4,128]{3,2,1,0:T(4,128)(2,1)S(1)} %pad_maximum_fusion.3), channel_id=1, replica_groups={{0,16,32,48,256,272,288,304,64,80,96,112,320,336,352,368,128,144,160,17..., dimensions={0} | all-to-all | bytes 589824 | tf_op jit(solution)/shard_map/all_to_all | solution.py:35
  70.7 0.1 fusion.24
  70.8 0.1 eq.85
  70.9 0.1 eq.89
  71.0 0.0 copy-done.1
  71.0 0.5 fusion.12
  71.5 0.4 convolution_convert_fusion
  71.9 0.1 fusion.23
  72.0 1.2 pad_maximum_fusion
  73.2 5.2 %all-to-all-start.2 = ((bf16[32,17,4,128]{3,2,1,0:T(4,128)(2,1)}), bf16[32,17,4,128]{3,2,1,0:T(4,128)(2,1)S(1)}, u32[]{:S(2)}, u32[]{:S(2)}) async-start(bf16[32,17,4,128]{3,2,1,0:T(4,128)(2,1)} %pad_maximum_fusion), calls=%async_computation.2 | async-start | bytes 1114112 | tf_op jit(solution)/shard_map/all_to_all | solution.py:35
  78.4 1.9 %collective-permute-start.1 = (bf16[1,128,128]{2,1,0:T(8,128)(2,1)S(1)}, bf16[1,128,128]{2,1,0:T(8,128)(2,1)S(1)}, u32[]{:S(2)}, u32[]{:S(2)}) collective-permute-start(bf16[1,128,128]{2,1,0:T(8,128)(2,1)S(1)} %bitcast.64), channel_id=1, source_target_pairs={{0,1},{1,0},{2,3},{3,2},{4,5},{5,4},{6,7},{7,6},{8,9},{9,8},{10,11... | collective-permute-start | bytes 98312 | tf_op jit(solution)/shard_map/ppermute | solution.py:74
  80.3 1.2 collective-permute-done.1
  81.5 4.3 %collective-permute-start.2 = (bf16[2,128,128]{2,1,0:T(8,128)(2,1)S(1)}, bf16[2,128,128]{2,1,0:T(8,128)(2,1)S(1)}, u32[]{:S(2)}, u32[]{:S(2)}) collective-permute-start(bf16[2,128,128]{2,1,0:T(8,128)(2,1)S(1)} %pad_maximum_fusion.7), channel_id=1, source_target_pairs={{0,8},{1,9},{2,10},{3,11},{4,12},{5,13},{6,14},{7,15},{8,0},{9,1},... | collective-permute-start | bytes 196616 | tf_op jit(solution)/shard_map/ppermute | solution.py:74
  85.8 3.4 %collective-permute-done.2 = bf16[2,128,128]{2,1,0:T(8,128)(2,1)S(1)} collective-permute-done((bf16[2,128,128]{2,1,0:T(8,128)(2,1)S(1)}, bf16[2,128,128]{2,1,0:T(8,128)(2,1)S(1)}, u32[]{:S(2)}, u32[]{:S(2)}) %collective-permute-start.2) | collective-permute-done | bytes 65568 | tf_op jit(solution)/shard_map/ppermute | solution.py:74
  89.2 3.5 %collective-permute-start.3 = (bf16[4,128,128]{2,1,0:T(8,128)(2,1)S(1)}, bf16[4,128,128]{2,1,0:T(8,128)(2,1)S(1)}, u32[]{:S(2)}, u32[]{:S(2)}) collective-permute-start(bf16[4,128,128]{2,1,0:T(8,128)(2,1)S(1)} %pad_maximum_fusion.6), channel_id=1, source_target_pairs={{0,2},{1,3},{2,0},{3,1},{4,6},{5,7},{6,4},{7,5},{8,10},{9,11},{10,... | collective-permute-start | bytes 393224 | tf_op jit(solution)/shard_map/ppermute | solution.py:74
  92.7 5.5 %collective-permute-done.3 = bf16[4,128,128]{2,1,0:T(8,128)(2,1)S(1)} collective-permute-done((bf16[4,128,128]{2,1,0:T(8,128)(2,1)S(1)}, bf16[4,128,128]{2,1,0:T(8,128)(2,1)S(1)}, u32[]{:S(2)}, u32[]{:S(2)}) %collective-permute-start.3) | collective-permute-done | bytes 131104 | tf_op jit(solution)/shard_map/ppermute | solution.py:74
  98.3 3.0 %collective-permute-start.4 = (bf16[8,128,128]{2,1,0:T(8,128)(2,1)S(1)}, bf16[8,128,128]{2,1,0:T(8,128)(2,1)S(1)}, u32[]{:S(2)}, u32[]{:S(2)}) collective-permute-start(bf16[8,128,128]{2,1,0:T(8,128)(2,1)S(1)} %pad_maximum_fusion.5), channel_id=1, source_target_pairs={{0,4},{1,5},{2,6},{3,7},{4,0},{5,1},{6,2},{7,3},{8,12},{9,13},{10,... | collective-permute-start | bytes 786440 | tf_op jit(solution)/shard_map/ppermute | solution.py:74
  101.3 5.3 %collective-permute-done.4 = bf16[8,128,128]{2,1,0:T(8,128)(2,1)S(1)} collective-permute-done((bf16[8,128,128]{2,1,0:T(8,128)(2,1)S(1)}, bf16[8,128,128]{2,1,0:T(8,128)(2,1)S(1)}, u32[]{:S(2)}, u32[]{:S(2)}) %collective-permute-start.4) | collective-permute-done | bytes 262176 | tf_op jit(solution)/shard_map/ppermute | solution.py:74
  106.7 0.3 convolution_convert_fusion.1
  107.0 2.4 %all-to-all-done.2 = bf16[32,17,4,128]{3,2,1,0:T(4,128)(2,1)S(1)} async-done(((bf16[32,17,4,128]{3,2,1,0:T(4,128)(2,1)}), bf16[32,17,4,128]{3,2,1,0:T(4,128)(2,1)S(1)}, u32[]{:S(2)}, u32[]{:S(2)}) %all-to-all-start.2) | async-done | bytes 557088 | tf_op jit(solution)/shard_map/all_to_all | solution.py:35
  109.4 0.9 pad_maximum_fusion.4
  110.3 10.9 %all-to-all-start.3 = ((bf16[32,9,4,128]{3,2,1,0:T(4,128)(2,1)}), bf16[32,9,4,128]{3,2,1,0:T(4,128)(2,1)S(1)}, u32[]{:S(2)}, u32[]{:S(2)}) async-start(bf16[32,9,4,128]{3,2,1,0:T(4,128)(2,1)} %pad_maximum_fusion.4), calls=%async_computation.3 | async-start | bytes 589824 | tf_op jit(solution)/shard_map/all_to_all | solution.py:35
  121.2 0.2 fusion.22
  121.4 0.1 copy.20
  121.5 0.1 copy.21
  121.6 18.7 %all-to-all-done.3 = bf16[32,9,4,128]{3,2,1,0:T(4,128)(2,1)S(1)} async-done(((bf16[32,9,4,128]{3,2,1,0:T(4,128)(2,1)}), bf16[32,9,4,128]{3,2,1,0:T(4,128)(2,1)S(1)}, u32[]{:S(2)}, u32[]{:S(2)}) %all-to-all-start.3) | async-done | bytes 294944 | tf_op jit(solution)/shard_map/all_to_all | solution.py:35
  140.3 0.1 slice.79
  140.5 0.6 multiply_subtract_fusion
  141.1 2.3 %fusion = bf16[1,1,32,128,128]{4,3,2,1,0:T(8,128)(2,1)} fusion(bf16[1,1,32,128,128]{4,3,2,1,0:T(8,128)(2,1)S(1)} %copy-done, bf16[32,32,128]{2,0,1:T(8,128)(2,1)S(1)} %bitcast.61, bf16[32,32,128]{2,0,1:T(8,128)(2,1)S(1)} %bitcast.60, bf16[64,32,128]{2,1,0:T(8,128)(2,1)S(1)} %pad_maximum_fusion.2), kind=kOutput, calls=%fused_computation.1 | convolution fusion | flops 72876032 | bytes 3145728 | tf_op jit(solution)/shard_map/nki,nkj->kij/dot_general | solution.py:116
  (18 shorter events, 0.4 us)
Async XLA Ops:
  0.6 23.5 %copy-start.3 = (s32[1,1,32]{2,1,0:T(1,128)S(1)}, s32[1,1,32]{2,1,0:T(1,128)}, u32[]{:S(2)}) copy-start(s32[1,1,32]{2,1,0:T(1,128)} %param.13) | copy-start | bytes 388
  0.6 23.5 %copy-start.2 = (s32[1,1,32]{2,1,0:T(1,128)S(1)}, s32[1,1,32]{2,1,0:T(1,128)}, u32[]{:S(2)}) copy-start(s32[1,1,32]{2,1,0:T(1,128)} %param.12) | copy-start | bytes 388
  1.7 14.3 %collective-permute-start = (bf16[128,128]{1,0:T(8,128)(2,1)S(1)}, bf16[128,128]{1,0:T(8,128)(2,1)S(1)}, u32[]{:S(2)}, u32[]{:S(2)}) collective-permute-start(bf16[128,128]{1,0:T(8,128)(2,1)S(1)} %bitcast.62), channel_id=1, source_target_pairs={{0,11},{1,47},{2,69},{3,107},{4,135},{5,169},{6,195},{7,231},{8,26... | collective-permute-start | bytes 98312 | tf_op jit(solution)/shard_map/ppermute | solution.py:66
  16.9 17.1 %copy-start = (bf16[1,1,32,128,128]{4,3,2,1,0:T(8,128)(2,1)S(1)}, bf16[1,1,32,128,128]{4,3,2,1,0:T(8,128)(2,1)}, u32[]{:S(2)}) copy-start(bf16[1,1,32,128,128]{4,3,2,1,0:T(8,128)(2,1)} %param.10) | copy-start | bytes 3145732
  16.9 16.8 %all-to-all-start = ((bf16[32,64,128]{2,1,0:T(8,128)(2,1)}), bf16[32,64,128]{2,1,0:T(8,128)(2,1)S(1)}, u32[]{:S(2)}, u32[]{:S(2)}) async-start(bf16[32,64,128]{2,1,0:T(8,128)(2,1)} %bitcast.4), calls=%async_computation | async-start | bytes 1048576 | tf_op jit(solution)/shard_map/all_to_all | solution.py:69
  34.3 36.6 %copy-start.1 = (f32[16384]{0:T(1024)S(1)}, f32[16384]{0:T(1024)}, u32[]{:S(2)}) copy-start(f32[16384]{0:T(1024)} %param.11) | copy-start | bytes 196612
  73.2 36.2 %all-to-all-start.2 = ((bf16[32,17,4,128]{3,2,1,0:T(4,128)(2,1)}), bf16[32,17,4,128]{3,2,1,0:T(4,128)(2,1)S(1)}, u32[]{:S(2)}, u32[]{:S(2)}) async-start(bf16[32,17,4,128]{3,2,1,0:T(4,128)(2,1)} %pad_maximum_fusion), calls=%async_computation.2 | async-start | bytes 1114112 | tf_op jit(solution)/shard_map/all_to_all | solution.py:35
  78.4 3.1 %collective-permute-start.1 = (bf16[1,128,128]{2,1,0:T(8,128)(2,1)S(1)}, bf16[1,128,128]{2,1,0:T(8,128)(2,1)S(1)}, u32[]{:S(2)}, u32[]{:S(2)}) collective-permute-start(bf16[1,128,128]{2,1,0:T(8,128)(2,1)S(1)} %bitcast.64), channel_id=1, source_target_pairs={{0,1},{1,0},{2,3},{3,2},{4,5},{5,4},{6,7},{7,6},{8,9},{9,8},{10,11... | collective-permute-start | bytes 98312 | tf_op jit(solution)/shard_map/ppermute | solution.py:74
  81.5 7.7 %collective-permute-start.2 = (bf16[2,128,128]{2,1,0:T(8,128)(2,1)S(1)}, bf16[2,128,128]{2,1,0:T(8,128)(2,1)S(1)}, u32[]{:S(2)}, u32[]{:S(2)}) collective-permute-start(bf16[2,128,128]{2,1,0:T(8,128)(2,1)S(1)} %pad_maximum_fusion.7), channel_id=1, source_target_pairs={{0,8},{1,9},{2,10},{3,11},{4,12},{5,13},{6,14},{7,15},{8,0},{9,1},... | collective-permute-start | bytes 196616 | tf_op jit(solution)/shard_map/ppermute | solution.py:74
  89.2 9.0 %collective-permute-start.3 = (bf16[4,128,128]{2,1,0:T(8,128)(2,1)S(1)}, bf16[4,128,128]{2,1,0:T(8,128)(2,1)S(1)}, u32[]{:S(2)}, u32[]{:S(2)}) collective-permute-start(bf16[4,128,128]{2,1,0:T(8,128)(2,1)S(1)} %pad_maximum_fusion.6), channel_id=1, source_target_pairs={{0,2},{1,3},{2,0},{3,1},{4,6},{5,7},{6,4},{7,5},{8,10},{9,11},{10,... | collective-permute-start | bytes 393224 | tf_op jit(solution)/shard_map/ppermute | solution.py:74
  98.3 8.3 %collective-permute-start.4 = (bf16[8,128,128]{2,1,0:T(8,128)(2,1)S(1)}, bf16[8,128,128]{2,1,0:T(8,128)(2,1)S(1)}, u32[]{:S(2)}, u32[]{:S(2)}) collective-permute-start(bf16[8,128,128]{2,1,0:T(8,128)(2,1)S(1)} %pad_maximum_fusion.5), channel_id=1, source_target_pairs={{0,4},{1,5},{2,6},{3,7},{4,0},{5,1},{6,2},{7,3},{8,12},{9,13},{10,... | collective-permute-start | bytes 786440 | tf_op jit(solution)/shard_map/ppermute | solution.py:74
  110.3 30.0 %all-to-all-start.3 = ((bf16[32,9,4,128]{3,2,1,0:T(4,128)(2,1)}), bf16[32,9,4,128]{3,2,1,0:T(4,128)(2,1)S(1)}, u32[]{:S(2)}, u32[]{:S(2)}) async-start(bf16[32,9,4,128]{3,2,1,0:T(4,128)(2,1)} %pad_maximum_fusion.4), calls=%async_computation.3 | async-start | bytes 589824 | tf_op jit(solution)/shard_map/all_to_all | solution.py:35

commit v9 on v8

--- a/solution.py
+++ b/solution.py
@@ -101,7 +101,6 @@
 
     held = gathered(mixed).reshape(nrow, rb, b)
     out = jnp.einsum("tsb,tbl->tsl", pick_r, held, preferred_element_type=jnp.float32).astype(BF)
-    out, got = lax.optimization_barrier((out, got))
 
     wc, xc = got[:, : k // 4].reshape(nrow, k, b), got[:, -k // 4 :].reshape(nrow, k, b)
     quad = jnp.sum(got[:, k // 4 : -k // 4].astype(jnp.float32), axis=0).reshape(own, b).astype(BF)

time: 144 us -> 144 us (level)
  no operation moved by 1% of the time
where the time goes in v9:
time: 144 us; the launch traced here: 143 us
  waiting for transfers between devices  53.5 us (37%)
  starting transfers between devices  42.5 us (30%)
  blocking collectives  36 us (25%)
  other arithmetic  4.3 us (3%)
  matrix products  4.13 us (3%)
  local copies, waits for them, and re-layouts  2.08 us (1%)
    all_to_all x1, blocking collectives, exchange(): lax.all_to_all(x, 'row', 0, 0, tiled=True, axis_index_groups=[member_orde...  36 us
    all_to_all x2, waiting for transfers between devices, exchange(): lax.all_to_all(x, 'row', 0, 0, tiled=True, axis_index_groups=[member_orde...  21 us
    all_to_all x2, starting transfers between devices, exchange(): lax.all_to_all(x, 'row', 0, 0, tiled=True, axis_index_groups=[member_orde...  16.1 us
    ppermute x4, waiting for transfers between devices, gathered(): other = lax.ppermute(v, 'col', [(c, c ^ bit) for c in range(ncol)])  15.3 us
    ppermute x4, starting transfers between devices, gathered(): other = lax.ppermute(v, 'col', [(c, c ^ bit) for c in range(ncol)])  12.7 us
    all_to_all x1, waiting for transfers between devices, in_group(): lax.all_to_all(v, ('row', 'col'), 0, 0, tiled=True, axis_index_groups=[[g...  9.37 us
    ppermute x1, waiting for transfers between devices, turned(): return lax.ppermute(v, ('row', 'col'), perm)  7.74 us
    all_to_all x1, starting transfers between devices, in_group(): lax.all_to_all(v, ('row', 'col'), 0, 0, tiled=True, axis_index_groups=[[g...  7.18 us
  transfers between devices with their start and end apart: 8, of which 8 were waited for; matrix products, arithmetic and copies ran while one was open for 1% of the time, Pallas kernels for 0%

profile of v9, /device:TPU:38, one launch (start us, length us, event | category | flops | bytes accessed | tf_op | source)
XLA Modules:
  0.0 143.4 jit_solution(8605215704749140039)
XLA Ops:
  0.6 0.0 copy-start.3
  0.6 0.0 copy-start.2
  0.6 1.0 reduce.6
  1.7 6.6 %collective-permute-start = (bf16[128,128]{1,0:T(8,128)(2,1)S(1)}, bf16[128,128]{1,0:T(8,128)(2,1)S(1)}, u32[]{:S(2)}, u32[]{:S(2)}) collective-permute-start(bf16[128,128]{1,0:T(8,128)(2,1)S(1)} %bitcast.62), channel_id=1, source_target_pairs={{0,11},{1,47},{2,69},{3,107},{4,135},{5,169},{6,195},{7,231},{8,26... | collective-permute-start | bytes 98312 | tf_op jit(solution)/shard_map/ppermute | solution.py:66
  8.2 7.7 %collective-permute-done = bf16[128,128]{1,0:T(8,128)(2,1)S(1)} collective-permute-done((bf16[128,128]{1,0:T(8,128)(2,1)S(1)}, bf16[128,128]{1,0:T(8,128)(2,1)S(1)}, u32[]{:S(2)}, u32[]{:S(2)}) %collective-permute-start) | collective-permute-done | bytes 32800 | tf_op jit(solution)/shard_map/ppermute | solution.py:66
  16.0 0.9 broadcast_in_dim.9
  16.9 0.0 copy-start
  16.9 7.2 %all-to-all-start = ((bf16[32,64,128]{2,1,0:T(8,128)(2,1)}), bf16[32,64,128]{2,1,0:T(8,128)(2,1)S(1)}, u32[]{:S(2)}, u32[]{:S(2)}) async-start(bf16[32,64,128]{2,1,0:T(8,128)(2,1)} %bitcast.4), calls=%async_computation | async-start | bytes 1048576 | tf_op jit(solution)/shard_map/all_to_all | solution.py:69
  24.1 0.0 copy-done.3
  24.1 0.0 copy-done.2
  24.1 0.2 scatter.9
  24.3 9.4 %all-to-all-done = bf16[32,64,128]{2,1,0:T(8,128)(2,1)S(1)} async-done(((bf16[32,64,128]{2,1,0:T(8,128)(2,1)}), bf16[32,64,128]{2,1,0:T(8,128)(2,1)S(1)}, u32[]{:S(2)}, u32[]{:S(2)}) %all-to-all-start) | async-done | bytes 524320 | tf_op jit(solution)/shard_map/all_to_all | solution.py:69
  33.7 0.3 fusion.1
  34.0 0.0 copy-done
  34.0 0.4 convolution_convert_fusion.2
  34.3 0.0 copy-start.1
  34.3 0.1 copy.19
  34.5 0.2 pad_maximum_fusion.3
  34.7 36.0 %all_to_all.20 = bf16[32,9,4,128]{3,2,1,0:T(4,128)(2,1)S(1)} all-to-all(bf16[32,9,4,128]{3,2,1,0:T(4,128)(2,1)S(1)} %pad_maximum_fusion.3), channel_id=1, replica_groups={{0,16,32,48,256,272,288,304,64,80,96,112,320,336,352,368,128,144,160,17..., dimensions={0} | all-to-all | bytes 589824 | tf_op jit(solution)/shard_map/all_to_all | solution.py:35
  70.7 0.1 fusion.24
  70.8 0.1 eq.85
  70.9 0.1 eq.89
  71.0 0.0 copy-done.1
  71.0 0.5 fusion.12
  71.5 0.4 convolution_convert_fusion
  71.9 0.1 fusion.23
  72.0 1.2 pad_maximum_fusion
  73.2 5.2 %all-to-all-start.2 = ((bf16[32,17,4,128]{3,2,1,0:T(4,128)(2,1)}), bf16[32,17,4,128]{3,2,1,0:T(4,128)(2,1)S(1)}, u32[]{:S(2)}, u32[]{:S(2)}) async-start(bf16[32,17,4,128]{3,2,1,0:T(4,128)(2,1)} %pad_maximum_fusion), calls=%async_computation.2 | async-start | bytes 1114112 | tf_op jit(solution)/shard_map/all_to_all | solution.py:35
  78.4 1.9 %collective-permute-start.1 = (bf16[1,128,128]{2,1,0:T(8,128)(2,1)S(1)}, bf16[1,128,128]{2,1,0:T(8,128)(2,1)S(1)}, u32[]{:S(2)}, u32[]{:S(2)}) collective-permute-start(bf16[1,128,128]{2,1,0:T(8,128)(2,1)S(1)} %bitcast.64), channel_id=1, source_target_pairs={{0,1},{1,0},{2,3},{3,2},{4,5},{5,4},{6,7},{7,6},{8,9},{9,8},{10,11... | collective-permute-start | bytes 98312 | tf_op jit(solution)/shard_map/ppermute | solution.py:74
  80.3 1.2 collective-permute-done.1
  81.5 4.3 %collective-permute-start.2 = (bf16[2,128,128]{2,1,0:T(8,128)(2,1)S(1)}, bf16[2,128,128]{2,1,0:T(8,128)(2,1)S(1)}, u32[]{:S(2)}, u32[]{:S(2)}) collective-permute-start(bf16[2,128,128]{2,1,0:T(8,128)(2,1)S(1)} %pad_maximum_fusion.7), channel_id=1, source_target_pairs={{0,8},{1,9},{2,10},{3,11},{4,12},{5,13},{6,14},{7,15},{8,0},{9,1},... | collective-permute-start | bytes 196616 | tf_op jit(solution)/shard_map/ppermute | solution.py:74
  85.8 3.4 %collective-permute-done.2 = bf16[2,128,128]{2,1,0:T(8,128)(2,1)S(1)} collective-permute-done((bf16[2,128,128]{2,1,0:T(8,128)(2,1)S(1)}, bf16[2,128,128]{2,1,0:T(8,128)(2,1)S(1)}, u32[]{:S(2)}, u32[]{:S(2)}) %collective-permute-start.2) | collective-permute-done | bytes 65568 | tf_op jit(solution)/shard_map/ppermute | solution.py:74
  89.2 3.5 %collective-permute-start.3 = (bf16[4,128,128]{2,1,0:T(8,128)(2,1)S(1)}, bf16[4,128,128]{2,1,0:T(8,128)(2,1)S(1)}, u32[]{:S(2)}, u32[]{:S(2)}) collective-permute-start(bf16[4,128,128]{2,1,0:T(8,128)(2,1)S(1)} %pad_maximum_fusion.6), channel_id=1, source_target_pairs={{0,2},{1,3},{2,0},{3,1},{4,6},{5,7},{6,4},{7,5},{8,10},{9,11},{10,... | collective-permute-start | bytes 393224 | tf_op jit(solution)/shard_map/ppermute | solution.py:74
  92.7 5.5 %collective-permute-done.3 = bf16[4,128,128]{2,1,0:T(8,128)(2,1)S(1)} collective-permute-done((bf16[4,128,128]{2,1,0:T(8,128)(2,1)S(1)}, bf16[4,128,128]{2,1,0:T(8,128)(2,1)S(1)}, u32[]{:S(2)}, u32[]{:S(2)}) %collective-permute-start.3) | collective-permute-done | bytes 131104 | tf_op jit(solution)/shard_map/ppermute | solution.py:74
  98.3 3.0 %collective-permute-start.4 = (bf16[8,128,128]{2,1,0:T(8,128)(2,1)S(1)}, bf16[8,128,128]{2,1,0:T(8,128)(2,1)S(1)}, u32[]{:S(2)}, u32[]{:S(2)}) collective-permute-start(bf16[8,128,128]{2,1,0:T(8,128)(2,1)S(1)} %pad_maximum_fusion.5), channel_id=1, source_target_pairs={{0,4},{1,5},{2,6},{3,7},{4,0},{5,1},{6,2},{7,3},{8,12},{9,13},{10,... | collective-permute-start | bytes 786440 | tf_op jit(solution)/shard_map/ppermute | solution.py:74
  101.3 5.3 %collective-permute-done.4 = bf16[8,128,128]{2,1,0:T(8,128)(2,1)S(1)} collective-permute-done((bf16[8,128,128]{2,1,0:T(8,128)(2,1)S(1)}, bf16[8,128,128]{2,1,0:T(8,128)(2,1)S(1)}, u32[]{:S(2)}, u32[]{:S(2)}) %collective-permute-start.4) | collective-permute-done | bytes 262176 | tf_op jit(solution)/shard_map/ppermute | solution.py:74
  106.7 0.3 convolution_convert_fusion.1
  107.0 2.4 %all-to-all-done.2 = bf16[32,17,4,128]{3,2,1,0:T(4,128)(2,1)S(1)} async-done(((bf16[32,17,4,128]{3,2,1,0:T(4,128)(2,1)}), bf16[32,17,4,128]{3,2,1,0:T(4,128)(2,1)S(1)}, u32[]{:S(2)}, u32[]{:S(2)}) %all-to-all-start.2) | async-done | bytes 557088 | tf_op jit(solution)/shard_map/all_to_all | solution.py:35
  109.4 0.9 pad_maximum_fusion.4
  110.3 10.9 %all-to-all-start.3 = ((bf16[32,9,4,128]{3,2,1,0:T(4,128)(2,1)}), bf16[32,9,4,128]{3,2,1,0:T(4,128)(2,1)S(1)}, u32[]{:S(2)}, u32[]{:S(2)}) async-start(bf16[32,9,4,128]{3,2,1,0:T(4,128)(2,1)} %pad_maximum_fusion.4), calls=%async_computation.3 | async-start | bytes 589824 | tf_op jit(solution)/shard_map/all_to_all | solution.py:35
  121.2 0.2 fusion.22
  121.4 0.1 copy.20
  121.5 0.1 copy.21
  121.6 18.7 %all-to-all-done.3 = bf16[32,9,4,128]{3,2,1,0:T(4,128)(2,1)S(1)} async-done(((bf16[32,9,4,128]{3,2,1,0:T(4,128)(2,1)}), bf16[32,9,4,128]{3,2,1,0:T(4,128)(2,1)S(1)}, u32[]{:S(2)}, u32[]{:S(2)}) %all-to-all-start.3) | async-done | bytes 294944 | tf_op jit(solution)/shard_map/all_to_all | solution.py:35
  140.3 0.1 slice.80
  140.5 0.6 multiply_subtract_fusion
  141.1 2.3 %fusion = bf16[1,1,32,128,128]{4,3,2,1,0:T(8,128)(2,1)} fusion(bf16[1,1,32,128,128]{4,3,2,1,0:T(8,128)(2,1)S(1)} %copy-done, bf16[32,32,128]{2,0,1:T(8,128)(2,1)S(1)} %bitcast.61, bf16[32,32,128]{2,0,1:T(8,128)(2,1)S(1)} %bitcast.60, bf16[64,32,128]{2,1,0:T(8,128)(2,1)S(1)} %pad_maximum_fusion.2), kind=kOutput, calls=%fused_computation.1 | convolution fusion | flops 72876032 | bytes 3145728 | tf_op jit(solution)/shard_map/nki,nkj->kij/dot_general | solution.py:115
  (18 shorter events, 0.4 us)
Async XLA Ops:
  0.6 23.5 %copy-start.3 = (s32[1,1,32]{2,1,0:T(1,128)S(1)}, s32[1,1,32]{2,1,0:T(1,128)}, u32[]{:S(2)}) copy-start(s32[1,1,32]{2,1,0:T(1,128)} %param.13) | copy-start | bytes 388
  0.6 23.5 %copy-start.2 = (s32[1,1,32]{2,1,0:T(1,128)S(1)}, s32[1,1,32]{2,1,0:T(1,128)}, u32[]{:S(2)}) copy-start(s32[1,1,32]{2,1,0:T(1,128)} %param.12) | copy-start | bytes 388
  1.7 14.3 %collective-permute-start = (bf16[128,128]{1,0:T(8,128)(2,1)S(1)}, bf16[128,128]{1,0:T(8,128)(2,1)S(1)}, u32[]{:S(2)}, u32[]{:S(2)}) collective-permute-start(bf16[128,128]{1,0:T(8,128)(2,1)S(1)} %bitcast.62), channel_id=1, source_target_pairs={{0,11},{1,47},{2,69},{3,107},{4,135},{5,169},{6,195},{7,231},{8,26... | collective-permute-start | bytes 98312 | tf_op jit(solution)/shard_map/ppermute | solution.py:66
  16.9 17.1 %copy-start = (bf16[1,1,32,128,128]{4,3,2,1,0:T(8,128)(2,1)S(1)}, bf16[1,1,32,128,128]{4,3,2,1,0:T(8,128)(2,1)}, u32[]{:S(2)}) copy-start(bf16[1,1,32,128,128]{4,3,2,1,0:T(8,128)(2,1)} %param.10) | copy-start | bytes 3145732
  16.9 16.8 %all-to-all-start = ((bf16[32,64,128]{2,1,0:T(8,128)(2,1)}), bf16[32,64,128]{2,1,0:T(8,128)(2,1)S(1)}, u32[]{:S(2)}, u32[]{:S(2)}) async-start(bf16[32,64,128]{2,1,0:T(8,128)(2,1)} %bitcast.4), calls=%async_computation | async-start | bytes 1048576 | tf_op jit(solution)/shard_map/all_to_all | solution.py:69
  34.3 36.6 %copy-start.1 = (f32[16384]{0:T(1024)S(1)}, f32[16384]{0:T(1024)}, u32[]{:S(2)}) copy-start(f32[16384]{0:T(1024)} %param.11) | copy-start | bytes 196612
  73.2 36.2 %all-to-all-start.2 = ((bf16[32,17,4,128]{3,2,1,0:T(4,128)(2,1)}), bf16[32,17,4,128]{3,2,1,0:T(4,128)(2,1)S(1)}, u32[]{:S(2)}, u32[]{:S(2)}) async-start(bf16[32,17,4,128]{3,2,1,0:T(4,128)(2,1)} %pad_maximum_fusion), calls=%async_computation.2 | async-start | bytes 1114112 | tf_op jit(solution)/shard_map/all_to_all | solution.py:35
  78.4 3.1 %collective-permute-start.1 = (bf16[1,128,128]{2,1,0:T(8,128)(2,1)S(1)}, bf16[1,128,128]{2,1,0:T(8,128)(2,1)S(1)}, u32[]{:S(2)}, u32[]{:S(2)}) collective-permute-start(bf16[1,128,128]{2,1,0:T(8,128)(2,1)S(1)} %bitcast.64), channel_id=1, source_target_pairs={{0,1},{1,0},{2,3},{3,2},{4,5},{5,4},{6,7},{7,6},{8,9},{9,8},{10,11... | collective-permute-start | bytes 98312 | tf_op jit(solution)/shard_map/ppermute | solution.py:74
  81.5 7.7 %collective-permute-start.2 = (bf16[2,128,128]{2,1,0:T(8,128)(2,1)S(1)}, bf16[2,128,128]{2,1,0:T(8,128)(2,1)S(1)}, u32[]{:S(2)}, u32[]{:S(2)}) collective-permute-start(bf16[2,128,128]{2,1,0:T(8,128)(2,1)S(1)} %pad_maximum_fusion.7), channel_id=1, source_target_pairs={{0,8},{1,9},{2,10},{3,11},{4,12},{5,13},{6,14},{7,15},{8,0},{9,1},... | collective-permute-start | bytes 196616 | tf_op jit(solution)/shard_map/ppermute | solution.py:74
  89.2 9.0 %collective-permute-start.3 = (bf16[4,128,128]{2,1,0:T(8,128)(2,1)S(1)}, bf16[4,128,128]{2,1,0:T(8,128)(2,1)S(1)}, u32[]{:S(2)}, u32[]{:S(2)}) collective-permute-start(bf16[4,128,128]{2,1,0:T(8,128)(2,1)S(1)} %pad_maximum_fusion.6), channel_id=1, source_target_pairs={{0,2},{1,3},{2,0},{3,1},{4,6},{5,7},{6,4},{7,5},{8,10},{9,11},{10,... | collective-permute-start | bytes 393224 | tf_op jit(solution)/shard_map/ppermute | solution.py:74
  98.3 8.3 %collective-permute-start.4 = (bf16[8,128,128]{2,1,0:T(8,128)(2,1)S(1)}, bf16[8,128,128]{2,1,0:T(8,128)(2,1)S(1)}, u32[]{:S(2)}, u32[]{:S(2)}) collective-permute-start(bf16[8,128,128]{2,1,0:T(8,128)(2,1)S(1)} %pad_maximum_fusion.5), channel_id=1, source_target_pairs={{0,4},{1,5},{2,6},{3,7},{4,0},{5,1},{6,2},{7,3},{8,12},{9,13},{10,... | collective-permute-start | bytes 786440 | tf_op jit(solution)/shard_map/ppermute | solution.py:74
  110.3 30.0 %all-to-all-start.3 = ((bf16[32,9,4,128]{3,2,1,0:T(4,128)(2,1)}), bf16[32,9,4,128]{3,2,1,0:T(4,128)(2,1)S(1)}, u32[]{:S(2)}, u32[]{:S(2)}) async-start(bf16[32,9,4,128]{3,2,1,0:T(4,128)(2,1)} %pad_maximum_fusion.4), calls=%async_computation.3 | async-start | bytes 589824 | tf_op jit(solution)/shard_map/all_to_all | solution.py:35

commit v10 on v9

--- a/solution.py
+++ b/solution.py
@@ -94,10 +94,10 @@
     mixed = (total + xf * diag).astype(BF)
 
     quad = (xf * mixed.astype(jnp.float32)).reshape(nrow, own, b)
-    out = jnp.dot(pick_c, jnp.concatenate([mixed, x], axis=1), preferred_element_type=jnp.float32).astype(BF)
-    out = out.reshape(nrow, k, 2 * b)
+    out = jnp.dot(pick_c, mixed, preferred_element_type=jnp.float32).astype(BF).reshape(nrow, k, b)
+    side = jnp.dot(pick_c, x, preferred_element_type=jnp.float32).astype(BF).reshape(nrow, k, b)
     out, quad, mixed = lax.optimization_barrier((out, quad.astype(BF), mixed))
-    got = joined_exchange(out[..., :b], quad, out[..., b:])
+    got = joined_exchange(out, quad, side)
 
     held = gathered(mixed).reshape(nrow, rb, b)
     out = jnp.einsum("tsb,tbl->tsl", pick_r, held, preferred_element_type=jnp.float32).astype(BF)

time: 144 us -> 144 us (level)
  no operation moved by 1% of the time
where the time goes in v10:
time: 144 us
  waiting for transfers between devices  53.5 us (37%)
  starting transfers between devices  42.5 us (30%)
  blocking collectives  36 us (25%)
  matrix products  4.41 us (3%)
  other arithmetic  4.3 us (3%)
  local copies, waits for them, and re-layouts  1.99 us (1%)
    all_to_all x1, blocking collectives, exchange(): lax.all_to_all(x, 'row', 0, 0, tiled=True, axis_index_groups=[member_orde...  36 us
    all_to_all x2, waiting for transfers between devices, exchange(): lax.all_to_all(x, 'row', 0, 0, tiled=True, axis_index_groups=[member_orde...  21 us
    all_to_all x2, starting transfers between devices, exchange(): lax.all_to_all(x, 'row', 0, 0, tiled=True, axis_index_groups=[member_orde...  16.1 us
    ppermute x4, waiting for transfers between devices, gathered(): other = lax.ppermute(v, 'col', [(c, c ^ bit) for c in range(ncol)])  15.3 us
    ppermute x4, starting transfers between devices, gathered(): other = lax.ppermute(v, 'col', [(c, c ^ bit) for c in range(ncol)])  12.7 us
    all_to_all x1, waiting for transfers between devices, in_group(): lax.all_to_all(v, ('row', 'col'), 0, 0, tiled=True, axis_index_groups=[[g...  9.37 us
    ppermute x1, waiting for transfers between devices, turned(): return lax.ppermute(v, ('row', 'col'), perm)  7.74 us
    all_to_all x1, starting transfers between devices, in_group(): lax.all_to_all(v, ('row', 'col'), 0, 0, tiled=True, axis_index_groups=[[g...  7.18 us
  transfers between devices with their start and end apart: 8, of which 8 were waited for; matrix products, arithmetic and copies ran while one was open for 1% of the time, Pallas kernels for 0%

profile of v10, /device:TPU:38, one launch (start us, length us, event | category | flops | bytes accessed | tf_op | source)
XLA Modules:
  0.0 143.6 jit_solution(13178331897280141243)
XLA Ops:
  0.6 0.0 copy-start.3
  0.6 0.0 copy-start.2
  0.6 1.0 reduce.6
  1.7 6.6 %collective-permute-start = (bf16[128,128]{1,0:T(8,128)(2,1)S(1)}, bf16[128,128]{1,0:T(8,128)(2,1)S(1)}, u32[]{:S(2)}, u32[]{:S(2)}) collective-permute-start(bf16[128,128]{1,0:T(8,128)(2,1)S(1)} %bitcast.66), channel_id=1, source_target_pairs={{0,11},{1,47},{2,69},{3,107},{4,135},{5,169},{6,195},{7,231},{8,26... | collective-permute-start | bytes 98312 | tf_op jit(solution)/shard_map/ppermute | solution.py:66
  8.2 7.7 %collective-permute-done = bf16[128,128]{1,0:T(8,128)(2,1)S(1)} collective-permute-done((bf16[128,128]{1,0:T(8,128)(2,1)S(1)}, bf16[128,128]{1,0:T(8,128)(2,1)S(1)}, u32[]{:S(2)}, u32[]{:S(2)}) %collective-permute-start) | collective-permute-done | bytes 32800 | tf_op jit(solution)/shard_map/ppermute | solution.py:66
  16.0 0.9 broadcast_in_dim.9
  16.9 0.0 copy-start
  16.9 7.2 %all-to-all-start = ((bf16[32,64,128]{2,1,0:T(8,128)(2,1)}), bf16[32,64,128]{2,1,0:T(8,128)(2,1)S(1)}, u32[]{:S(2)}, u32[]{:S(2)}) async-start(bf16[32,64,128]{2,1,0:T(8,128)(2,1)} %bitcast.4), calls=%async_computation | async-start | bytes 1048576 | tf_op jit(solution)/shard_map/all_to_all | solution.py:69
  24.1 0.0 copy-done.3
  24.1 0.0 copy-done.2
  24.1 0.2 scatter.9
  24.3 9.4 %all-to-all-done = bf16[32,64,128]{2,1,0:T(8,128)(2,1)S(1)} async-done(((bf16[32,64,128]{2,1,0:T(8,128)(2,1)}), bf16[32,64,128]{2,1,0:T(8,128)(2,1)S(1)}, u32[]{:S(2)}, u32[]{:S(2)}) %all-to-all-start) | async-done | bytes 524320 | tf_op jit(solution)/shard_map/all_to_all | solution.py:69
  33.7 0.3 fusion.1
  34.0 0.0 copy-done
  34.0 0.4 convolution_convert_fusion.3
  34.3 0.0 copy-start.1
  34.3 0.1 copy.13
  34.5 0.2 pad_maximum_fusion.3
  34.7 36.0 %all_to_all.20 = bf16[32,9,4,128]{3,2,1,0:T(4,128)(2,1)S(1)} all-to-all(bf16[32,9,4,128]{3,2,1,0:T(4,128)(2,1)S(1)} %pad_maximum_fusion.3), channel_id=1, replica_groups={{0,16,32,48,256,272,288,304,64,80,96,112,320,336,352,368,128,144,160,17..., dimensions={0} | all-to-all | bytes 589824 | tf_op jit(solution)/shard_map/all_to_all | solution.py:35
  70.7 0.1 fusion.21
  70.8 0.1 eq.85
  70.9 0.1 eq.89
  71.0 0.3 convolution_convert_fusion
  71.3 0.0 copy-done.1
  71.3 0.5 fusion.13
  71.9 0.3 convolution_convert_fusion.2
  72.2 1.2 pad_maximum_fusion
  73.4 5.2 %all-to-all-start.2 = ((bf16[32,17,4,128]{3,2,1,0:T(4,128)(2,1)}), bf16[32,17,4,128]{3,2,1,0:T(4,128)(2,1)S(1)}, u32[]{:S(2)}, u32[]{:S(2)}) async-start(bf16[32,17,4,128]{3,2,1,0:T(4,128)(2,1)} %pad_maximum_fusion), calls=%async_computation.2 | async-start | bytes 1114112 | tf_op jit(solution)/shard_map/all_to_all | solution.py:35
  78.6 1.9 %collective-permute-start.1 = (bf16[1,128,128]{2,1,0:T(8,128)(2,1)S(1)}, bf16[1,128,128]{2,1,0:T(8,128)(2,1)S(1)}, u32[]{:S(2)}, u32[]{:S(2)}) collective-permute-start(bf16[1,128,128]{2,1,0:T(8,128)(2,1)S(1)} %bitcast.67), channel_id=1, source_target_pairs={{0,1},{1,0},{2,3},{3,2},{4,5},{5,4},{6,7},{7,6},{8,9},{9,8},{10,11... | collective-permute-start | bytes 98312 | tf_op jit(solution)/shard_map/ppermute | solution.py:74
  80.5 1.2 collective-permute-done.1
  81.7 4.3 %collective-permute-start.2 = (bf16[2,128,128]{2,1,0:T(8,128)(2,1)S(1)}, bf16[2,128,128]{2,1,0:T(8,128)(2,1)S(1)}, u32[]{:S(2)}, u32[]{:S(2)}) collective-permute-start(bf16[2,128,128]{2,1,0:T(8,128)(2,1)S(1)} %pad_maximum_fusion.7), channel_id=1, source_target_pairs={{0,8},{1,9},{2,10},{3,11},{4,12},{5,13},{6,14},{7,15},{8,0},{9,1},... | collective-permute-start | bytes 196616 | tf_op jit(solution)/shard_map/ppermute | solution.py:74
  86.0 3.4 %collective-permute-done.2 = bf16[2,128,128]{2,1,0:T(8,128)(2,1)S(1)} collective-permute-done((bf16[2,128,128]{2,1,0:T(8,128)(2,1)S(1)}, bf16[2,128,128]{2,1,0:T(8,128)(2,1)S(1)}, u32[]{:S(2)}, u32[]{:S(2)}) %collective-permute-start.2) | collective-permute-done | bytes 65568 | tf_op jit(solution)/shard_map/ppermute | solution.py:74
  89.4 3.5 %collective-permute-start.3 = (bf16[4,128,128]{2,1,0:T(8,128)(2,1)S(1)}, bf16[4,128,128]{2,1,0:T(8,128)(2,1)S(1)}, u32[]{:S(2)}, u32[]{:S(2)}) collective-permute-start(bf16[4,128,128]{2,1,0:T(8,128)(2,1)S(1)} %pad_maximum_fusion.6), channel_id=1, source_target_pairs={{0,2},{1,3},{2,0},{3,1},{4,6},{5,7},{6,4},{7,5},{8,10},{9,11},{10,... | collective-permute-start | bytes 393224 | tf_op jit(solution)/shard_map/ppermute | solution.py:74
  92.9 5.5 %collective-permute-done.3 = bf16[4,128,128]{2,1,0:T(8,128)(2,1)S(1)} collective-permute-done((bf16[4,128,128]{2,1,0:T(8,128)(2,1)S(1)}, bf16[4,128,128]{2,1,0:T(8,128)(2,1)S(1)}, u32[]{:S(2)}, u32[]{:S(2)}) %collective-permute-start.3) | collective-permute-done | bytes 131104 | tf_op jit(solution)/shard_map/ppermute | solution.py:74
  98.5 3.0 %collective-permute-start.4 = (bf16[8,128,128]{2,1,0:T(8,128)(2,1)S(1)}, bf16[8,128,128]{2,1,0:T(8,128)(2,1)S(1)}, u32[]{:S(2)}, u32[]{:S(2)}) collective-permute-start(bf16[8,128,128]{2,1,0:T(8,128)(2,1)S(1)} %pad_maximum_fusion.5), channel_id=1, source_target_pairs={{0,4},{1,5},{2,6},{3,7},{4,0},{5,1},{6,2},{7,3},{8,12},{9,13},{10,... | collective-permute-start | bytes 786440 | tf_op jit(solution)/shard_map/ppermute | solution.py:74
  101.5 5.3 %collective-permute-done.4 = bf16[8,128,128]{2,1,0:T(8,128)(2,1)S(1)} collective-permute-done((bf16[8,128,128]{2,1,0:T(8,128)(2,1)S(1)}, bf16[8,128,128]{2,1,0:T(8,128)(2,1)S(1)}, u32[]{:S(2)}, u32[]{:S(2)}) %collective-permute-start.4) | collective-permute-done | bytes 262176 | tf_op jit(solution)/shard_map/ppermute | solution.py:74
  106.9 0.3 convolution_convert_fusion.1
  107.2 2.4 %all-to-all-done.2 = bf16[32,17,4,128]{3,2,1,0:T(4,128)(2,1)S(1)} async-done(((bf16[32,17,4,128]{3,2,1,0:T(4,128)(2,1)}), bf16[32,17,4,128]{3,2,1,0:T(4,128)(2,1)S(1)}, u32[]{:S(2)}, u32[]{:S(2)}) %all-to-all-start.2) | async-done | bytes 557088 | tf_op jit(solution)/shard_map/all_to_all | solution.py:35
  109.6 0.9 pad_maximum_fusion.4
  110.5 10.9 %all-to-all-start.3 = ((bf16[32,9,4,128]{3,2,1,0:T(4,128)(2,1)}), bf16[32,9,4,128]{3,2,1,0:T(4,128)(2,1)S(1)}, u32[]{:S(2)}, u32[]{:S(2)}) async-start(bf16[32,9,4,128]{3,2,1,0:T(4,128)(2,1)} %pad_maximum_fusion.4), calls=%async_computation.3 | async-start | bytes 589824 | tf_op jit(solution)/shard_map/all_to_all | solution.py:35
  121.4 0.2 fusion.20
  121.6 0.1 copy.15
  121.7 0.1 copy.16
  121.8 18.7 %all-to-all-done.3 = bf16[32,9,4,128]{3,2,1,0:T(4,128)(2,1)S(1)} async-done(((bf16[32,9,4,128]{3,2,1,0:T(4,128)(2,1)}), bf16[32,9,4,128]{3,2,1,0:T(4,128)(2,1)S(1)}, u32[]{:S(2)}, u32[]{:S(2)}) %all-to-all-start.3) | async-done | bytes 294944 | tf_op jit(solution)/shard_map/all_to_all | solution.py:35
  140.5 0.1 slice.72
  140.7 0.6 multiply_subtract_fusion
  141.3 2.3 %fusion = bf16[1,1,32,128,128]{4,3,2,1,0:T(8,128)(2,1)} fusion(bf16[1,1,32,128,128]{4,3,2,1,0:T(8,128)(2,1)S(1)} %copy-done, bf16[32,32,128]{2,0,1:T(8,128)(2,1)S(1)} %bitcast.65, bf16[32,32,128]{2,0,1:T(8,128)(2,1)S(1)} %bitcast.64, bf16[64,32,128]{2,1,0:T(8,128)(2,1)S(1)} %pad_maximum_fusion.2), kind=kOutput, calls=%fused_computation.1 | convolution fusion | flops 72876032 | bytes 3145728 | tf_op jit(solution)/shard_map/nki,nkj->kij/dot_general | solution.py:115
  (18 shorter events, 0.4 us)
Async XLA Ops:
  0.6 23.5 %copy-start.3 = (s32[1,1,32]{2,1,0:T(1,128)S(1)}, s32[1,1,32]{2,1,0:T(1,128)}, u32[]{:S(2)}) copy-start(s32[1,1,32]{2,1,0:T(1,128)} %param.13) | copy-start | bytes 388
  0.6 23.5 %copy-start.2 = (s32[1,1,32]{2,1,0:T(1,128)S(1)}, s32[1,1,32]{2,1,0:T(1,128)}, u32[]{:S(2)}) copy-start(s32[1,1,32]{2,1,0:T(1,128)} %param.12) | copy-start | bytes 388
  1.7 14.3 %collective-permute-start = (bf16[128,128]{1,0:T(8,128)(2,1)S(1)}, bf16[128,128]{1,0:T(8,128)(2,1)S(1)}, u32[]{:S(2)}, u32[]{:S(2)}) collective-permute-start(bf16[128,128]{1,0:T(8,128)(2,1)S(1)} %bitcast.66), channel_id=1, source_target_pairs={{0,11},{1,47},{2,69},{3,107},{4,135},{5,169},{6,195},{7,231},{8,26... | collective-permute-start | bytes 98312 | tf_op jit(solution)/shard_map/ppermute | solution.py:66
  16.9 17.1 %copy-start = (bf16[1,1,32,128,128]{4,3,2,1,0:T(8,128)(2,1)S(1)}, bf16[1,1,32,128,128]{4,3,2,1,0:T(8,128)(2,1)}, u32[]{:S(2)}) copy-start(bf16[1,1,32,128,128]{4,3,2,1,0:T(8,128)(2,1)} %param.10) | copy-start | bytes 3145732
  16.9 16.8 %all-to-all-start = ((bf16[32,64,128]{2,1,0:T(8,128)(2,1)}), bf16[32,64,128]{2,1,0:T(8,128)(2,1)S(1)}, u32[]{:S(2)}, u32[]{:S(2)}) async-start(bf16[32,64,128]{2,1,0:T(8,128)(2,1)} %bitcast.4), calls=%async_computation | async-start | bytes 1048576 | tf_op jit(solution)/shard_map/all_to_all | solution.py:69
  34.3 37.0 %copy-start.1 = (f32[16384]{0:T(1024)S(1)}, f32[16384]{0:T(1024)}, u32[]{:S(2)}) copy-start(f32[16384]{0:T(1024)} %param.11) | copy-start | bytes 196612
  73.4 36.2 %all-to-all-start.2 = ((bf16[32,17,4,128]{3,2,1,0:T(4,128)(2,1)}), bf16[32,17,4,128]{3,2,1,0:T(4,128)(2,1)S(1)}, u32[]{:S(2)}, u32[]{:S(2)}) async-start(bf16[32,17,4,128]{3,2,1,0:T(4,128)(2,1)} %pad_maximum_fusion), calls=%async_computation.2 | async-start | bytes 1114112 | tf_op jit(solution)/shard_map/all_to_all | solution.py:35
  78.6 3.1 %collective-permute-start.1 = (bf16[1,128,128]{2,1,0:T(8,128)(2,1)S(1)}, bf16[1,128,128]{2,1,0:T(8,128)(2,1)S(1)}, u32[]{:S(2)}, u32[]{:S(2)}) collective-permute-start(bf16[1,128,128]{2,1,0:T(8,128)(2,1)S(1)} %bitcast.67), channel_id=1, source_target_pairs={{0,1},{1,0},{2,3},{3,2},{4,5},{5,4},{6,7},{7,6},{8,9},{9,8},{10,11... | collective-permute-start | bytes 98312 | tf_op jit(solution)/shard_map/ppermute | solution.py:74
  81.7 7.7 %collective-permute-start.2 = (bf16[2,128,128]{2,1,0:T(8,128)(2,1)S(1)}, bf16[2,128,128]{2,1,0:T(8,128)(2,1)S(1)}, u32[]{:S(2)}, u32[]{:S(2)}) collective-permute-start(bf16[2,128,128]{2,1,0:T(8,128)(2,1)S(1)} %pad_maximum_fusion.7), channel_id=1, source_target_pairs={{0,8},{1,9},{2,10},{3,11},{4,12},{5,13},{6,14},{7,15},{8,0},{9,1},... | collective-permute-start | bytes 196616 | tf_op jit(solution)/shard_map/ppermute | solution.py:74
  89.4 9.0 %collective-permute-start.3 = (bf16[4,128,128]{2,1,0:T(8,128)(2,1)S(1)}, bf16[4,128,128]{2,1,0:T(8,128)(2,1)S(1)}, u32[]{:S(2)}, u32[]{:S(2)}) collective-permute-start(bf16[4,128,128]{2,1,0:T(8,128)(2,1)S(1)} %pad_maximum_fusion.6), channel_id=1, source_target_pairs={{0,2},{1,3},{2,0},{3,1},{4,6},{5,7},{6,4},{7,5},{8,10},{9,11},{10,... | collective-permute-start | bytes 393224 | tf_op jit(solution)/shard_map/ppermute | solution.py:74
  98.5 8.3 %collective-permute-start.4 = (bf16[8,128,128]{2,1,0:T(8,128)(2,1)S(1)}, bf16[8,128,128]{2,1,0:T(8,128)(2,1)S(1)}, u32[]{:S(2)}, u32[]{:S(2)}) collective-permute-start(bf16[8,128,128]{2,1,0:T(8,128)(2,1)S(1)} %pad_maximum_fusion.5), channel_id=1, source_target_pairs={{0,4},{1,5},{2,6},{3,7},{4,0},{5,1},{6,2},{7,3},{8,12},{9,13},{10,... | collective-permute-start | bytes 786440 | tf_op jit(solution)/shard_map/ppermute | solution.py:74
  110.5 30.0 %all-to-all-start.3 = ((bf16[32,9,4,128]{3,2,1,0:T(4,128)(2,1)}), bf16[32,9,4,128]{3,2,1,0:T(4,128)(2,1)S(1)}, u32[]{:S(2)}, u32[]{:S(2)}) async-start(bf16[32,9,4,128]{3,2,1,0:T(4,128)(2,1)} %pad_maximum_fusion.4), calls=%async_computation.3 | async-start | bytes 589824 | tf_op jit(solution)/shard_map/all_to_all | solution.py:35
